TPU v7x, 256 devices: a whole 4x4x8 slice. The times are simulated.
256 devices in a mesh: dp: 32 (over z, x), vocab: 8 (over y, core).
Axes of the slice: x: 4, y: 4, z: 8, core: 2. Of those that a mesh axis runs over, the one named last changes fastest.
Arguments:
- hidden_states: bfloat16 [4096, 3584], P('dp'), may hold values from -40 to 40
- head_weight: bfloat16 [3584, 98304], P(None, ('dp', 'vocab')), as said below
- target_ids: int32 [4096], replicated, may hold values from 0 to 98303
- seq_lengths: int32 [256], P('dp'), may hold values from 1 to 16
- domain_labels: int32 [256], P('dp'), may hold values from 0 to 21
- domain_weights: float32 [22], replicated, may hold values from 0.5 to 4
Outputs:
- token_loss: float32 [4096], P('dp')
- new_weights: float32 [22], replicated
Inputs may be any that keep to these rules, and one draw needn't show every extreme that they name: `head_weight`: every entry lies within 6 / sqrt(3584) of zero.
All inputs are finite; a program needn't handle non-finite values.
Results may differ from a plain program's by a relative error of at most 0.0003.
Values may be sent and summed in bfloat16 or wider, within the bound.
No kernel may reach another device: no remote copies, remote signals or barrier semaphores. Data moves between devices by JAX's collectives and lax.ppermute only.
A program may use at most 128 MiB of HBM per device.

v0:
```python
import jax
import jax.numpy as jnp
from jax import lax
from jax.sharding import Mesh
from jax.sharding import PartitionSpec as P

SEQ_LEN = 16
DOMAINS = 22
DP = ("dp_0", "dp_1")
DP_VOCAB = ("dp_0", "dp_1", "vocab")


explore_share = 0.01
step_rate = 0.002


def whole_of(shard, axes, dim):
    if not axes:
        return shard
    nearer = lax.all_gather(shard, axes[-1], axis=dim, tiled=True)
    return whole_of(nearer, axes[:-1], dim)


def sent_to_all(shard, axis):
    length = lax.axis_size(axis)
    return lax.all_to_all(
        jnp.broadcast_to(shard[None], (length, *shard.shape)), axis, 0, 0, tiled=True
    )


def taken_together(shard, axis):
    everything = sent_to_all(shard, axis)
    return jnp.max(everything, axis=0)


def split_up(shard, dim, length):
    lengths = shard.shape
    parts = shard.reshape(*lengths[:dim], length, lengths[dim] // length, *lengths[dim + 1 :])
    return jnp.moveaxis(parts, dim, 0)


def sum_at_owner(shard, axis, dim):
    parts = split_up(shard, dim, lax.axis_size(axis))
    arrived = lax.all_to_all(parts, axis, split_axis=0, concat_axis=0, tiled=True)
    return arrived.sum(axis=0)


def gather_turned(arrays, axis, dims):
    turned = [jnp.moveaxis(a, dim, 0) for a, dim in zip(arrays, dims)]
    widths = [t[0].size for t in turned]
    both = jnp.concatenate([t.reshape(-1, w) for t, w in zip(turned, widths)], axis=1)
    whole = lax.all_gather(both, axis, axis=0, tiled=True)
    parts = jnp.split(whole, [sum(widths[:k]) for k in range(1, len(widths))], axis=1)
    return tuple(
        (
            jnp.moveaxis(b.reshape(-1, *t.shape[1:]), 0, dim)
            for b, t, dim in zip(parts, turned, dims)
        )
    )


def in_order(parts, dim):
    parts = jnp.moveaxis(parts, 0, dim)
    lengths = parts.shape
    return parts.reshape(*lengths[:dim], lengths[dim] * lengths[dim + 1], *lengths[dim + 2 :])


def gathered_copies(shard, axis, dim):
    return in_order(sent_to_all(shard, axis), dim)


def row_statistics(logits, targets, col_start):
    row_peak = jnp.max(logits, axis=1)
    mass_sum = jnp.sum(jnp.exp(logits - row_peak[:, None]), axis=1)
    columns = lax.broadcasted_iota(jnp.int32, logits.shape, 1) + col_start
    picked = jnp.sum(jnp.where(columns == targets[:, None], logits, 0.0), axis=1)
    return (row_peak, mass_sum, picked)


def combine_stats(earlier, later):
    joined = jnp.maximum(earlier[0], later[0])
    mass_sum = later[1] * jnp.exp(later[0] - joined)
    return (joined, mass_sum, later[2])


def body(hidden_states, head_weight, target_ids, seq_lengths, domain_labels, domain_weights):
    tok_dev = hidden_states.shape[0]
    col_count = head_weight.shape[1]
    vocab_count = lax.axis_size("vocab")
    dp_count = lax.axis_size(DP)
    dp_index = lax.axis_index(DP)
    vocab_index = lax.axis_index("vocab")
    share = tok_dev // vocab_count
    own_slice = lax.dynamic_slice_in_dim(hidden_states, vocab_index * share, share, 0)
    scored_rows = whole_of(own_slice, DP, 0)
    target_block = lax.dynamic_slice_in_dim(
        target_ids.reshape(dp_count, tok_dev), vocab_index * share, share, 1
    ).reshape(-1)
    group_start = dp_index * vocab_count * col_count
    scored_count = scored_rows.shape[0]
    start_stats = (
        jnp.full((scored_count,), -1e30, jnp.float32),
        jnp.zeros((scored_count,), jnp.float32),
        jnp.zeros((scored_count,), jnp.float32),
    )
    logits = jnp.dot(
        scored_rows,
        lax.all_gather(head_weight, "vocab", axis=1, tiled=True),
        preferred_element_type=jnp.float32,
    )
    fresh_vals = row_statistics(logits, target_block, group_start)
    block_stats = combine_stats(start_stats, fresh_vals)
    group_peak = taken_together(block_stats[0], DP)
    scaled = block_stats[1] * jnp.exp(block_stats[0] - group_peak)
    part_mass, part_pick = (sum_at_owner(scaled, DP, 0), sum_at_owner(block_stats[2], DP, 0))
    mine = (lax.dynamic_slice_in_dim(group_peak, dp_index * share, share), part_mass, part_pick)
    own_peak, own_mass, own_pick = gather_turned((mine[0], mine[1], mine[2]), "vocab", (0, 0, 0))
    seq_count = seq_lengths.shape[0]
    positions = jnp.arange(tok_dev) % SEQ_LEN
    valid = positions < jnp.repeat(seq_lengths, SEQ_LEN)
    token_loss = jnp.where(valid, jnp.log(own_mass) + own_peak - own_pick, 0.0)
    seq_loss = jnp.sum(token_loss.reshape(seq_count, SEQ_LEN), axis=1)
    seq_tokens = seq_lengths.astype(jnp.float32)
    owned_count = (DOMAINS + dp_count - 1) // dp_count
    padded_count = owned_count * dp_count
    domain_hot = (domain_labels[:, None] == jnp.arange(padded_count)[None, :]).astype(jnp.float32)
    by_owner = jnp.transpose(domain_hot.reshape(seq_count, dp_count, owned_count), (1, 0, 2))
    outgoing = jnp.concatenate(
        [by_owner * seq_loss[None, :, None], by_owner * seq_tokens[None, :, None]], axis=2
    )
    incoming = lax.all_to_all(outgoing, DP, split_axis=0, concat_axis=0, tiled=True)
    received = jnp.sum(incoming, axis=(0, 1))
    own_loss = received[:owned_count]
    own_count = received[owned_count:]
    first_slot = dp_index * owned_count
    padded_weights = jnp.concatenate(
        [domain_weights, jnp.zeros((padded_count - DOMAINS,), jnp.float32)]
    )
    own_weights = lax.dynamic_slice_in_dim(padded_weights, first_slot, owned_count)
    probability = (1.0 - DOMAINS * explore_share) * own_weights / jnp.sum(
        domain_weights
    ) + explore_share
    reward = own_loss / jnp.maximum(own_count, 1.0) / probability
    raised = own_weights * jnp.exp(step_rate * reward)
    every_raised = gathered_copies(raised, DP, 0)[:DOMAINS]
    new_weights = DOMAINS * every_raised / jnp.sum(every_raised)
    return (token_loss, new_weights)


def solution(mesh):
    torus = Mesh(mesh.devices.reshape(8, 4, mesh.shape["vocab"]), ("dp_0", "dp_1", "vocab"))
    in_specs = (P(DP, None), P(None, DP_VOCAB), P(), P(DP), P(DP), P())
    out_specs = (P(DP), P())
    return jax.shard_map(body, mesh=torus, in_specs=in_specs, out_specs=out_specs, check_vma=False)
```

profile of v0, /device:TPU:1, one launch (start us, length us, event | category | flops | bytes accessed | tf_op | source)
XLA Modules:
  0.0 304.7 jit_solution(8402878156980372884)
XLA Ops:
  7.2 1.1 copy-done
  8.4 12.5 %all_gather.12 = bf16[64,3584]{1,0:T(8,128)(2,1)} all-gather(bf16[16,3584]{1,0:T(8,128)(2,1)S(1)} %constant_dynamic-slice_fusion.1), channel_id=1, replica_groups=mesh['dp_0'=8,'dp_1'=4,'vocab'=8] {'dp_1'}, dimensions={0}, use_global_device_ids=true | all-gather | bytes 573440 | tf_op jit(solution)/shard_map/all_gather | solution.py:20
  21.0 0.7 all-gather.6.cloned.1.call-update
  21.7 0.8 constant_dynamic-slice_fusion
  22.6 53.4 %all-gather.4.cloned.1.call-done = bf16[512,3584]{1,0:T(8,128)(2,1)} async-done(((bf16[64,3584]{1,0:T(8,128)(2,1)}), bf16[512,3584]{1,0:T(8,128)(2,1)}) %all-gather.4.cloned.1.call-update) | async-done | bytes 3670032 | tf_op jit(solution)/shard_map/all_gather | solution.py:20
  75.9 110.2 %all-gather.6.cloned.1.call-done = bf16[3584,3072]{1,0:T(8,128)(2,1)} async-done(((bf16[3584,384]{1,0:T(8,128)(2,1)}), bf16[3584,3072]{1,0:T(8,128)(2,1)}) %all-gather.6.cloned.1.call-update) | async-done | bytes 22020112 | tf_op jit(solution)/shard_map/all_gather | solution.py:108
  186.1 16.3 %fusion.9 = (f32[512]{0:T(512)S(1)}, f32[512,3072]{1,0:T(8,128)S(1)}) fusion(bf16[512,3584]{1,0:T(8,128)(2,1)} %all-gather.4.cloned.1.call-done, bf16[3584,3072]{1,0:T(8,128)(2,1)} %all-gather.6.cloned.1.call-done), kind=kOutput, calls=%fused_computation.33 | convolution fusion | flops 11275862016 | bytes 31983616 | tf_op jit(solution)/shard_map/dot_general | solution.py:106
  202.4 1.9 exponential_reduce_fusion
  204.3 0.7 all_to_all.23
  205.0 9.5 %all-to-all-start.2 = ((f32[32,1,16]{2,1,0:T(1,128)}), f32[32,1,16]{2,1,0:T(1,128)S(1)}, u32[]{:S(2)}, u32[]{:S(2)}) async-start(f32[32,1,16]{2,1,0:T(1,128)} %bitcast.4), calls=%async_computation.2 | async-start | bytes 32768 | tf_op jit(solution)/shard_map/all_to_all | solution.py:44
  214.5 8.6 %all-to-all-done.2 = f32[32,1,16]{2,1,0:T(1,128)S(1)} async-done(((f32[32,1,16]{2,1,0:T(1,128)}), f32[32,1,16]{2,1,0:T(1,128)S(1)}, u32[]{:S(2)}, u32[]{:S(2)}) %all-to-all-start.2) | async-done | bytes 2080 | tf_op jit(solution)/shard_map/all_to_all | solution.py:44
  223.1 0.7 broadcast_in_dim.39
  223.8 3.9 %all-to-all-start = ((f32[32,1,512]{2,1,0:T(1,128)}), f32[32,1,512]{2,1,0:T(1,128)S(1)}, u32[]{:S(2)}, u32[]{:S(2)}) async-start(f32[32,1,512]{2,1,0:T(1,128)} %broadcast_in_dim.39), calls=%async_computation | async-start | bytes 131072 | tf_op jit(solution)/shard_map/all_to_all | solution.py:26
  227.9 8.7 %all-to-all-done = f32[32,1,512]{2,1,0:T(1,128)S(1)} async-done(((f32[32,1,512]{2,1,0:T(1,128)}), f32[32,1,512]{2,1,0:T(1,128)S(1)}, u32[]{:S(2)}, u32[]{:S(2)}) %all-to-all-start) | async-done | bytes 65568 | tf_op jit(solution)/shard_map/all_to_all | solution.py:26
  236.7 0.6 fusion.2
  237.3 3.9 %all-to-all-start.1 = ((f32[32,1,16]{2,1,0:T(1,128)}), f32[32,1,16]{2,1,0:T(1,128)S(1)}, u32[]{:S(2)}, u32[]{:S(2)}) async-start(f32[32,1,16]{2,1,0:T(1,128)} %bitcast.1), calls=%async_computation.1 | async-start | bytes 32768 | tf_op jit(solution)/shard_map/all_to_all | solution.py:44
  241.2 8.5 %all-to-all-done.1 = f32[32,1,16]{2,1,0:T(1,128)S(1)} async-done(((f32[32,1,16]{2,1,0:T(1,128)}), f32[32,1,16]{2,1,0:T(1,128)S(1)}, u32[]{:S(2)}, u32[]{:S(2)}) %all-to-all-start.1) | async-done | bytes 2080 | tf_op jit(solution)/shard_map/all_to_all | solution.py:44
  249.8 15.1 %all-gather = f32[8,16,3]{1,2,0:T(4,128)S(1)} all-gather(f32[1,16,3]{1,2,0:T(4,128)S(1)} %maximum_bitcast_fusion), channel_id=1, replica_groups=mesh['dp_0'=8,'dp_1'=4,'vocab'=8] {'vocab'}, dimensions={0}, use_global_device_ids=true | all-gather | bytes 1728 | tf_op jit(solution)/shard_map/all_gather | solution.py:52
  265.0 0.5 broadcast.138
  265.5 0.7 fusion.7
  266.5 0.7 copy.25
  267.2 3.9 %all-to-all-start.3 = ((f32[32,8,2]{1,2,0:T(2,128)}), f32[32,8,2]{1,2,0:T(2,128)S(1)}, u32[]{:S(2)}, u32[]{:S(2)}) async-start(f32[32,8,2]{1,2,0:T(2,128)} %copy.25), calls=%async_computation.3 | async-start | bytes 65536 | tf_op jit(solution)/shard_map/all_to_all | solution.py:131
  271.1 0.6 reduce_sum.81
  271.9 0.6 fusion.10
  273.8 6.1 %all-to-all-done.3 = f32[32,8,2]{1,2,0:T(2,128)S(1)} async-done(((f32[32,8,2]{1,2,0:T(2,128)}), f32[32,8,2]{1,2,0:T(2,128)S(1)}, u32[]{:S(2)}, u32[]{:S(2)}) %all-to-all-start.3) | async-done | bytes 2080 | tf_op jit(solution)/shard_map/all_to_all | solution.py:131
  280.0 0.6 fusion.8
  282.6 0.6 broadcast_in_dim.45
  283.2 3.8 %all-to-all-start.4 = ((f32[32,1,1]{2,1,0:T(1,128)}), f32[32,1,1]{2,1,0:T(1,128)S(1)}, u32[]{:S(2)}, u32[]{:S(2)}) async-start(f32[32,1,1]{2,1,0:T(1,128)} %broadcast_in_dim.45), calls=%async_computation.4 | async-start | bytes 32768 | tf_op jit(solution)/shard_map/all_to_all | solution.py:26
  287.1 0.5 compare_select_fusion
  287.6 8.1 %all-to-all-done.4 = f32[32,1,1]{2,1,0:T(1,128)S(1)} async-done(((f32[32,1,1]{2,1,0:T(1,128)}), f32[32,1,1]{2,1,0:T(1,128)S(1)}, u32[]{:S(2)}, u32[]{:S(2)}) %all-to-all-start.4) | async-done | bytes 160 | tf_op jit(solution)/shard_map/all_to_all | solution.py:26
  295.7 0.7 slice_reduce_fusion
  296.4 1.4 fusion.4
  (32 shorter events, 1.5 us)
Async XLA Ops:
  7.2 1.2 copy-start
  7.2 68.8 %all-gather.4.cloned.1.call-start = ((), (), s32[]{:S(2)}) async-start(), calls=%async_computation.5 | async-start | bytes 4128768 | tf_op jit(solution)/shard_map/all_gather | solution.py:20
  20.9 165.2 %all-gather.6.cloned.1.call-start = ((), (), s32[]{:S(2)}) async-start(), calls=%async_computation.6 | async-start | bytes 24772608 | tf_op jit(solution)/shard_map/all_gather | solution.py:108
  202.4 25.3 %copy-start.1 = (s32[8]{0:T(128)S(1)}, s32[8]{0:T(128)}, u32[]{:S(2)}) copy-start(s32[8]{0:T(128)} %param.9) | copy-start | bytes 100
  202.4 64.0 %copy-start.2 = (s32[8]{0:T(128)S(1)}, s32[8]{0:T(128)}, u32[]{:S(2)}) copy-start(s32[8]{0:T(128)} %param.10) | copy-start | bytes 100
  202.4 68.7 %copy-start.3 = (f32[22]{0:T(128)S(1)}, f32[22]{0:T(128)}, u32[]{:S(2)}) copy-start(f32[22]{0:T(128)} %param.11) | copy-start | bytes 268
  205.0 18.1 %all-to-all-start.2 = ((f32[32,1,16]{2,1,0:T(1,128)}), f32[32,1,16]{2,1,0:T(1,128)S(1)}, u32[]{:S(2)}, u32[]{:S(2)}) async-start(f32[32,1,16]{2,1,0:T(1,128)} %bitcast.4), calls=%async_computation.2 | async-start | bytes 32768 | tf_op jit(solution)/shard_map/all_to_all | solution.py:44
  223.8 12.8 %all-to-all-start = ((f32[32,1,512]{2,1,0:T(1,128)}), f32[32,1,512]{2,1,0:T(1,128)S(1)}, u32[]{:S(2)}, u32[]{:S(2)}) async-start(f32[32,1,512]{2,1,0:T(1,128)} %broadcast_in_dim.39), calls=%async_computation | async-start | bytes 131072 | tf_op jit(solution)/shard_map/all_to_all | solution.py:26
  237.3 12.4 %all-to-all-start.1 = ((f32[32,1,16]{2,1,0:T(1,128)}), f32[32,1,16]{2,1,0:T(1,128)S(1)}, u32[]{:S(2)}, u32[]{:S(2)}) async-start(f32[32,1,16]{2,1,0:T(1,128)} %bitcast.1), calls=%async_computation.1 | async-start | bytes 32768 | tf_op jit(solution)/shard_map/all_to_all | solution.py:44
  267.2 12.6 %all-to-all-start.3 = ((f32[32,8,2]{1,2,0:T(2,128)}), f32[32,8,2]{1,2,0:T(2,128)S(1)}, u32[]{:S(2)}, u32[]{:S(2)}) async-start(f32[32,8,2]{1,2,0:T(2,128)} %copy.25), calls=%async_computation.3 | async-start | bytes 65536 | tf_op jit(solution)/shard_map/all_to_all | solution.py:131
  283.2 12.4 %all-to-all-start.4 = ((f32[32,1,1]{2,1,0:T(1,128)}), f32[32,1,1]{2,1,0:T(1,128)S(1)}, u32[]{:S(2)}, u32[]{:S(2)}) async-start(f32[32,1,1]{2,1,0:T(1,128)} %broadcast_in_dim.45), calls=%async_computation.4 | async-start | bytes 32768 | tf_op jit(solution)/shard_map/all_to_all | solution.py:26
Sparse Core Ops, SparseCore 0:
  21.1 54.8 all-gather.3
  77.8 108.2 all-gather.5
where the time goes:
time: 305 us
  waiting for transfers between devices  204 us (67%)
  blocking collectives  27.6 us (9%)
  starting transfers between devices  25 us (8%)
  between operations  17.5 us (6%)
  matrix products  16.3 us (5%)
  other arithmetic  7.7 us (3%)
  local copies, waits for them, and re-layouts  6.4 us (2%)
    all_gather x1, waiting for transfers between devices, body(): lax.all_gather(head_weight, 'vocab', axis=1, tiled=True)  110 us
    all_gather x1, waiting for transfers between devices, whole_of(): nearer = lax.all_gather(shard, axes[-1], axis=dim, tiled=True)  53.4 us
    all_to_all x2, waiting for transfers between devices, sum_at_owner(): lax.all_to_all(parts, axis, split_axis=0, concat_axis=0, tiled=True)  17.1 us
    all_to_all x2, waiting for transfers between devices, sent_to_all(): lax.all_to_all(jnp.broadcast_to(shard[None], (length, *shard.shape)), axi...  16.7 us
    dot_general x1, matrix products, body(): jnp.dot(scored_rows, lax.all_gather(head_weight, 'vocab', axis=1, tiled=T...  16.3 us
    all_gather x1, blocking collectives, gather_turned(): whole = lax.all_gather(both, axis, axis=0, tiled=True)  15.1 us
    all_to_all x2, starting transfers between devices, sum_at_owner(): lax.all_to_all(parts, axis, split_axis=0, concat_axis=0, tiled=True)  13.3 us
    all_gather x1, blocking collectives, whole_of(): nearer = lax.all_gather(shard, axes[-1], axis=dim, tiled=True)  12.5 us
  transfers between devices with their start and end apart: 7, of which 7 were waited for; matrix products, arithmetic and copies ran while one was open for 1% of the time, Pallas kernels for 0%

commit v1 on v0

v1 whole, which is shorter than its diff:
```python
import functools
import jax
import jax.numpy as jnp
from jax import lax
from jax.experimental import pallas as pl
from jax.experimental.pallas import tpu as pltpu
from jax.sharding import Mesh
from jax.sharding import PartitionSpec as P

SEQ_LEN = 16
DOMAINS = 22
explore_share = 0.01
step_rate = 0.002

ALL = ("z", "x", "yh", "yl", "c")
DP = ("z", "x")
VOCAB_AXES = ("yh", "yl", "c")
SUB = 16


def shift(a, axis, by):
    n = lax.axis_size(axis)
    return lax.ppermute(a, axis, [(i, (i + by) % n) for i in range(n)])


def lane_parts(a):
    return [a[:, i : i + 128] for i in range(0, a.shape[1], 128)]


def stats_kernel(nb, np_, rows, starts, targets, *refs):
    blocks = refs[:nb]
    cols = refs[nb : nb + 2 * np_]
    out = refs[nb + 2 * np_]
    h_vm, w_vm, t_vm, m_vm, s_vm, p_vm, h_sem, w_sem = refs[nb + 2 * np_ + 1 :]
    height = blocks[0].shape[0]
    width = cols[0].shape[1]
    h_copies = [
        pltpu.make_async_copy(b, h_vm.at[pl.ds(i * height, height)], h_sem.at[i])
        for i, b in enumerate(blocks)
    ]
    w_copies = [
        pltpu.make_async_copy(w, w_vm.at[k // 2, :, pl.ds((k % 2) * width, width)], w_sem.at[k])
        for k, w in enumerate(cols)
    ]
    for copy in h_copies + w_copies:
        copy.start()
    total = nb * height
    spread = jnp.broadcast_to(targets[...].astype(jnp.float32), (128, total))
    t_vm[...] = spread.T.astype(jnp.int32)
    for copy in h_copies:
        copy.wait()
    for j in range(np_):
        w_copies[2 * j].wait()
        w_copies[2 * j + 1].wait()
        first, second = starts[2 * j], starts[2 * j + 1]

        @pl.loop(0, total // rows)
        def _(r):
            here = pl.ds(pl.multiple_of(r * rows, rows), rows)
            logits = jnp.dot(h_vm[here], w_vm[j], preferred_element_type=jnp.float32)
            parts = lane_parts(logits)
            peak = functools.reduce(jnp.maximum, parts)
            if j:
                before = m_vm[here]
                peak = jnp.maximum(peak, before)
                mass = s_vm[here] * jnp.exp(before - peak)
                pick = p_vm[here]
            else:
                mass = jnp.zeros_like(peak)
                pick = jnp.zeros_like(peak)
            away = t_vm[here] - lax.broadcasted_iota(jnp.int32, peak.shape, 1)
            for i, part in enumerate(parts):
                at = i * 128
                column = first + at if at < width else second + (at - width)
                mass = mass + jnp.exp(part - peak)
                pick = pick + jnp.where(away == column, part, 0.0)
            m_vm[here] = peak
            s_vm[here] = mass
            p_vm[here] = pick

    lane_peak = m_vm[...].T
    peak = jnp.max(lane_peak, axis=0, keepdims=True)
    mass = jnp.sum(s_vm[...].T * jnp.exp(lane_peak - peak), axis=0, keepdims=True)
    pick = jnp.sum(p_vm[...].T, axis=0, keepdims=True)
    out[0:1, :] = peak + jnp.log(mass)
    out[1:2, :] = pick


def tile_stats(blocks, targets, cols, starts):
    nb, np_ = len(blocks), len(cols) // 2
    height, depth = blocks[0].shape
    width = cols[0].shape[1]
    total = nb * height
    rows = 128
    any_spec = pl.BlockSpec(memory_space=pl.ANY)
    return pl.pallas_call(
        functools.partial(stats_kernel, nb, np_, rows),
        out_shape=jax.ShapeDtypeStruct((2, total), jnp.float32),
        in_specs=[
            pl.BlockSpec(memory_space=pltpu.SMEM),
            pl.BlockSpec(memory_space=pltpu.VMEM),
        ]
        + [any_spec] * (nb + 2 * np_),
        out_specs=pl.BlockSpec(memory_space=pltpu.VMEM),
        scratch_shapes=[
            pltpu.VMEM((total, depth), jnp.bfloat16),
            pltpu.VMEM((np_, depth, 2 * width), jnp.bfloat16),
            pltpu.VMEM((total, 128), jnp.int32),
            pltpu.VMEM((total, 128), jnp.float32),
            pltpu.VMEM((total, 128), jnp.float32),
            pltpu.VMEM((total, 128), jnp.float32),
            pltpu.SemaphoreType.DMA((nb,)),
            pltpu.SemaphoreType.DMA((2 * np_,)),
        ],
        compiler_params=pltpu.CompilerParams(vmem_limit_bytes=40 * 2**20),
        cost_estimate=pl.CostEstimate(
            flops=2 * total * depth * 2 * np_ * width,
            bytes_accessed=2 * depth * (total + 2 * np_ * width),
            transcendentals=total * 2 * np_ * width,
        ),
    )(starts, targets.reshape(1, total), *blocks, *cols)


def rolled(a, axis, by):
    n = a.shape[axis]
    twice = jnp.concatenate([a, a], axis=axis)
    return lax.dynamic_slice_in_dim(twice, by, n, axis)


def merged(lse, axis):
    top = jnp.max(lse, axis=axis, keepdims=True)
    return jnp.squeeze(top, axis) + jnp.log(jnp.sum(jnp.exp(lse - top), axis=axis))


def body(hidden_states, head_weight, target_ids, seq_lengths, domain_labels, domain_weights):
    z, x = lax.axis_index("z"), lax.axis_index("x")
    yh, yl, c = (lax.axis_index(a) for a in VOCAB_AXES)
    nz, nx = lax.axis_size("z"), lax.axis_size("x")
    dp_count = nz * nx
    dp_index = z * nx + x
    y = yh * 2 + yl
    quarter = yl * 2 + c
    share = hidden_states.shape[0] // 4
    width = head_weight.shape[1]

    own = lax.dynamic_slice_in_dim(hidden_states, quarter * share, share, 0)
    a, b = own[:SUB], own[SUB:]

    moves = [
        (k * 2 + core, ((k + (1 if core == 0 else -1)) % 4) * 2 + core)
        for k in range(4)
        for core in range(2)
    ]
    col_in = lax.ppermute(head_weight, VOCAB_AXES, moves)
    col_mate = shift(head_weight, "c", 1)

    a_m, a_p, a_o = shift(a, "x", 1), shift(a, "x", -1), shift(a, "x", 2)
    a1 = jnp.concatenate([a, a_m, a_p, a_o], axis=0)
    zm, zp = [a1], [a1]
    bm, bp = [b], [b]
    for _ in range(3):
        bm.append(shift(bm[-1], "z", 1))
        bp.append(shift(bp[-1], "z", -1))
    b4 = shift(bp[3], "z", -1)
    half_1 = jnp.concatenate([b, bm[1], bp[1], bm[2]], axis=0)
    half_2 = jnp.concatenate([bp[2], bm[3], bp[3], b4], axis=0)
    for _ in range(3):
        zm.append(shift(zm[-1], "z", 1))
        zp.append(shift(zp[-1], "z", -1))
    z4 = jnp.concatenate(
        [shift(zm[3][: 2 * SUB], "z", 1), shift(zp[3][2 * SUB :], "z", -1)], axis=0
    )
    h1m, h1p = shift(half_1, "x", 1), shift(half_1, "x", -1)
    h2m, h2p = shift(half_2, "x", 1), shift(half_2, "x", -1)
    h1o, h2o = shift(h1m, "x", 1), shift(h2p, "x", -1)
    col_in_mate = shift(col_in, "c", 1)

    dx_order = (0, nx - 1, 1, 2)
    z_blocks = [(a1, 0)]
    for k in range(1, 4):
        z_blocks += [(zm[k], nz - k), (zp[k], k)]
    z_blocks.append((z4, 4))
    half_dz = ((0, nz - 1, 1, nz - 2), (2, nz - 3, 3, 4))
    x_blocks = [
        (block, half_dz[h], dx)
        for h, four in enumerate(((half_1, h1m, h1p, h1o), (half_2, h2m, h2p, h2o)))
        for block, dx in zip(four, dx_order)
    ]
    order = []
    for block, dz in z_blocks:
        order.append((block, [(dz, dx, 0) for dx in dx_order]))
    for block, dzs, dx in x_blocks:
        order.append((block, [(dz, dx, 1) for dz in dzs]))
    groups = [(0, 1, 2, 8, 9, 10, 12, 3), (4, 13, 14, 11, 5, 6, 15, 7)]

    targets = target_ids.reshape(nz, nx, 4, 2, SUB)
    targets = lax.dynamic_index_in_dim(targets, quarter, 2, keepdims=False)
    targets = rolled(rolled(targets, 0, z), 1, x)

    def start_of(y_at, core):
        return (dp_index * 8 + (y_at % 4) * 2 + core) * width

    def start_in(core):
        return jnp.where(core == 0, start_of(y + 3, 0), start_of(y + 1, 1))

    starts = jnp.stack([start_of(y, c), start_of(y, 1 - c), start_in(c), start_in(1 - c)])
    cols = [head_weight, col_mate, col_in, col_in_mate]

    found = {}
    for group in groups:
        subs = [s for g in group for s in order[g][1]]
        wanted = jnp.concatenate([targets[s] for s in subs])
        stats = tile_stats([order[g][0] for g in group], wanted, cols, starts.astype(jnp.int32))
        for i, s in enumerate(subs):
            found[s] = stats[:, i * SUB : (i + 1) * SUB]
    every = jnp.stack(
        [
            jnp.concatenate([found[dz, dx, 0], found[dz, dx, 1]], axis=1)
            for dz in range(nz)
            for dx in range(nx)
        ]
    )
    every = every.reshape(nz, nx, -1)
    every = rolled(rolled(every, 0, (nz - z) % nz), 1, (nx - x) % nx).reshape(dp_count, -1)
    mine = lax.all_to_all(every, DP, 0, 0, tiled=True)
    lse = merged(mine[:, :share], 0)
    pick = jnp.sum(mine[:, share:], axis=0)
    note = jnp.concatenate(
        [lse, pick, seq_lengths.astype(jnp.float32), domain_labels.astype(jnp.float32)]
    )
    note = jnp.concatenate([note, jnp.zeros((128 - note.shape[0],), jnp.float32)])
    sent = jnp.broadcast_to(note[None], (lax.axis_size(ALL), 128))
    notes = lax.all_to_all(sent, ALL, 0, 0, tiled=True).reshape(dp_count, 2, 4, 128)
    raw = merged(notes[..., :share], 1) - jnp.sum(notes[..., share : 2 * share], axis=1)
    seqs = seq_lengths.shape[0]
    lengths = notes[:, 0, 0, 2 * share : 2 * share + seqs]
    labels = notes[:, 0, 0, 2 * share + seqs : 2 * share + 2 * seqs]
    raw = raw.reshape(dp_count, seqs, SEQ_LEN)
    valid = jnp.arange(SEQ_LEN, dtype=jnp.float32) < lengths[..., None]
    token_loss = jnp.where(valid, raw, 0.0)
    seq_loss = jnp.sum(token_loss, axis=2)
    hot = (labels[..., None] == jnp.arange(DOMAINS, dtype=jnp.float32)).astype(jnp.float32)
    domain_loss = jnp.sum(hot * seq_loss[..., None], axis=(0, 1))
    domain_count = jnp.sum(hot * lengths[..., None], axis=(0, 1))
    probability = (1.0 - DOMAINS * explore_share) * domain_weights / jnp.sum(
        domain_weights
    ) + explore_share
    reward = domain_loss / jnp.maximum(domain_count, 1.0) / probability
    raised = domain_weights * jnp.exp(step_rate * reward)
    new_weights = DOMAINS * raised / jnp.sum(raised)
    mine_loss = lax.dynamic_index_in_dim(token_loss, dp_index, 0, keepdims=False).reshape(-1)
    return (mine_loss, new_weights)


def solution(mesh):
    torus = Mesh(mesh.devices.reshape(8, 4, 2, 2, 2), ALL)
    in_specs = (P(DP, None), P(None, ALL), P(), P(DP), P(DP), P())
    out_specs = (P(DP), P())
    return jax.shard_map(body, mesh=torus, in_specs=in_specs, out_specs=out_specs, check_vma=False)
```

time: 305 us -> 175 us (0.57)
  waiting for transfers between devices: 204 us -> 67.2 us
  starting transfers between devices: 25 us -> 63.8 us
  blocking collectives: 27.6 us -> 0 us
  Pallas kernels: 0 us -> 25 us
  between operations: 17.5 us -> 1.05 us
  matrix products: 16.3 us -> 0 us
    all_gather x2 -> x0, waiting for transfers between devices: 164 us -> none  [the longest x1 110 us: body(): lax.all_gather(head_weight, 'vocab', axis=1, tiled=True)]
    ppermute x0 -> x27, waiting for transfers between devices: none -> 46.1 us  [the longest x26 46.1 us: shift(): return lax.ppermute(a, axis, [(i, (i + by) % n) for i in range(n)])]
    ppermute x0 -> x27, starting transfers between devices: none -> 44.7 us  [the longest x26 41.1 us: shift(): return lax.ppermute(a, axis, [(i, (i + by) % n) for i in range(n)])]
    all_gather x2 -> x0, blocking collectives: 27.6 us -> none  [the longest x1 15.1 us: gather_turned(): whole = lax.all_gather(both, axis, axis=0, tiled=True)]
    pallas_call x0 -> x2, Pallas kernels: none -> 25 us  [tile_stats(): pl.pallas_call(functools.partial(stats_kernel, nb, np_, rows), out_shape=...]
    all_to_all x5 -> x2, waiting for transfers between devices: 39.9 us -> 21.1 us  [the longest x1 12.5 us: body(): lax.all_to_all(sent, ALL, 0, 0, tiled=True).reshape(dp_count, 2, 4, 128)]
    dot_general x1 -> x0, matrix products: 16.3 us -> none  [body(): jnp.dot(scored_rows, lax.all_gather(head_weight, 'vocab', axis=1, tiled=T...]
    all_to_all x5 -> x2, starting transfers between devices: 24.9 us -> 19.1 us  [the longest x1 13 us: body(): lax.all_to_all(sent, ALL, 0, 0, tiled=True).reshape(dp_count, 2, 4, 128)]
  transfers between devices with their start and end apart: 7 -> 29, of which waited for: 7 -> 10; matrix products, arithmetic and copies ran while one was open for 1% -> 5% of each run, Pallas kernels for 0% -> 7%
where the time goes in v1:
time: 175 us
  waiting for transfers between devices  67.2 us (38%)
  starting transfers between devices  63.8 us (36%)
  Pallas kernels  25 us (14%)
  other arithmetic  9.11 us (5%)
  local copies, waits for them, and re-layouts  8.92 us (5%)
    ppermute x26, waiting for transfers between devices, shift(): return lax.ppermute(a, axis, [(i, (i + by) % n) for i in range(n)])  46.1 us
    ppermute x26, starting transfers between devices, shift(): return lax.ppermute(a, axis, [(i, (i + by) % n) for i in range(n)])  41.1 us
    pallas_call x2, Pallas kernels, tile_stats(): pl.pallas_call(functools.partial(stats_kernel, nb, np_, rows), out_shape=...  25 us
    all_to_all x1, starting transfers between devices, body(): lax.all_to_all(sent, ALL, 0, 0, tiled=True).reshape(dp_count, 2, 4, 128)  13 us
    all_to_all x1, waiting for transfers between devices, body(): lax.all_to_all(sent, ALL, 0, 0, tiled=True).reshape(dp_count, 2, 4, 128)  12.5 us
    all_to_all x1, waiting for transfers between devices, body(): mine = lax.all_to_all(every, DP, 0, 0, tiled=True)  8.55 us
    all_to_all x1, starting transfers between devices, body(): mine = lax.all_to_all(every, DP, 0, 0, tiled=True)  6.05 us
    ppermute x1, starting transfers between devices, body(): col_in = lax.ppermute(head_weight, VOCAB_AXES, moves)  3.64 us
  transfers between devices with their start and end apart: 29, of which 10 were waited for; matrix products, arithmetic and copies ran while one was open for 5% of the time, Pallas kernels for 7%

profile of v1, /device:TPU:1, one launch (start us, length us, event | category | flops | bytes accessed | tf_op | source)
XLA Modules:
  0.0 175.0 jit_solution(12526110053623987905)
XLA Ops:
  0.6 3.6 %collective-permute-start.16 = (bf16[3584,384]{1,0:T(8,128)(2,1)}, bf16[3584,384]{1,0:T(8,128)(2,1)}, u32[]{:S(2)}, u32[]{:S(2)}) collective-permute-start(bf16[3584,384]{1,0:T(8,128)(2,1)} %refs_8_.3), channel_id=1, source_target_pairs={{0,2},{1,7},{2,4},{3,1},{4,6},{5,3},{6,0},{7,5},{8,10},{9,15},{10,... | collective-permute-start | bytes 8257544 | tf_op jit(solution)/shard_map/ppermute | solution.py:154
  5.3 2.8 %collective-permute-start.2 = (bf16[16,3584]{1,0:T(8,128)(2,1)S(1)}, bf16[16,3584]{1,0:T(8,128)(2,1)S(1)}, u32[]{:S(2)}, u32[]{:S(2)}) collective-permute-start(bf16[16,3584]{1,0:T(8,128)(2,1)S(1)} %get-tuple-element.13), channel_id=1, source_target_pairs={{0,16},{8,24},{16,0},{24,8},{1,17},{9,25},{17,1},{25,9},{2,18},{10... | collective-permute-start | bytes 344072 | tf_op jit(solution)/shard_map/ppermute | solution.py:23
  9.6 1.6 collective-permute-start.5
  13.6 4.0 %collective-permute-start.6 = (bf16[16,3584]{1,0:T(8,128)(2,1)S(1)}, bf16[16,3584]{1,0:T(8,128)(2,1)}, u32[]{:S(2)}, u32[]{:S(2)}) collective-permute-start(bf16[16,3584]{1,0:T(8,128)(2,1)S(1)} %get-tuple-element.12), channel_id=1, source_target_pairs={{0,224},{32,0},{64,32},{96,64},{128,96},{160,128},{192,160},{224,1... | collective-permute-start | bytes 344072 | tf_op jit(solution)/shard_map/ppermute | solution.py:23
  19.4 2.7 %collective-permute-start.4 = (bf16[64,3584]{1,0:T(8,128)(2,1)S(1)}, bf16[64,3584]{1,0:T(8,128)(2,1)}, u32[]{:S(2)}, u32[]{:S(2)}) collective-permute-start(bf16[64,3584]{1,0:T(8,128)(2,1)S(1)} %pad_maximum_fusion.refs_0_), channel_id=1, source_target_pairs={{0,224},{32,0},{64,32},{96,64},{128,96},{160,128},{192,160},{224,1... | collective-permute-start | bytes 1376264 | tf_op jit(solution)/shard_map/ppermute | solution.py:23
  22.2 1.3 collective-permute-start.15
  23.5 11.1 %collective-permute-done.7 = bf16[16,3584]{1,0:T(8,128)(2,1)S(1)} collective-permute-done((bf16[16,3584]{1,0:T(8,128)(2,1)}, bf16[16,3584]{1,0:T(8,128)(2,1)S(1)}, u32[]{:S(2)}, u32[]{:S(2)}) %collective-permute-start.7) | collective-permute-done | bytes 114720 | tf_op jit(solution)/shard_map/ppermute | solution.py:23
  34.6 1.5 collective-permute-start.10
  36.0 2.5 %collective-permute-start.17 = (bf16[3584,384]{1,0:T(8,128)(2,1)}, bf16[3584,384]{1,0:T(8,128)(2,1)}, u32[]{:S(2)}, u32[]{:S(2)}) collective-permute-start(bf16[3584,384]{1,0:T(8,128)(2,1)} %collective-permute-done.16.refs_10_), channel_id=1, source_target_pairs={{0,1},{1,0},{2,3},{3,2},{4,5},{5,4},{6,7},{7,6},{8,9},{9,8},{10,11... | collective-permute-start | bytes 8257544 | tf_op jit(solution)/shard_map/ppermute | solution.py:23
  40.4 1.5 collective-permute-start.14
  41.9 2.5 %collective-permute-start.18 = (bf16[64,3584]{1,0:T(8,128)(2,1)}, bf16[64,3584]{1,0:T(8,128)(2,1)S(1)}, u32[]{:S(2)}, u32[]{:S(2)}) collective-permute-start(bf16[64,3584]{1,0:T(8,128)(2,1)} %collective-permute-done.4.refs_2_), channel_id=1, source_target_pairs={{0,224},{32,0},{64,32},{96,64},{128,96},{160,128},{192,160},{224,1... | collective-permute-start | bytes 1376264 | tf_op jit(solution)/shard_map/ppermute | solution.py:23
  45.4 2.3 %collective-permute-done.11 = bf16[16,3584]{1,0:T(8,128)(2,1)S(1)} collective-permute-done((bf16[16,3584]{1,0:T(8,128)(2,1)S(1)}, bf16[16,3584]{1,0:T(8,128)(2,1)S(1)}, u32[]{:S(2)}, u32[]{:S(2)}) %collective-permute-start.11) | collective-permute-done | bytes 114720 | tf_op jit(solution)/shard_map/ppermute | solution.py:23
  47.7 1.3 collective-permute-start.12
  50.0 7.2 %collective-permute-done.12 = bf16[16,3584]{1,0:T(8,128)(2,1)S(1)} collective-permute-done((bf16[16,3584]{1,0:T(8,128)(2,1)}, bf16[16,3584]{1,0:T(8,128)(2,1)S(1)}, u32[]{:S(2)}, u32[]{:S(2)}) %collective-permute-start.12) | collective-permute-done | bytes 114720 | tf_op jit(solution)/shard_map/ppermute | solution.py:23
  57.1 3.3 %collective-permute-start.13 = (bf16[16,3584]{1,0:T(8,128)(2,1)S(1)}, bf16[16,3584]{1,0:T(8,128)(2,1)S(1)}, u32[]{:S(2)}, u32[]{:S(2)}) collective-permute-start(bf16[16,3584]{1,0:T(8,128)(2,1)S(1)} %collective-permute-done.12), channel_id=1, source_target_pairs={{0,224},{32,0},{64,32},{96,64},{128,96},{160,128},{192,160},{224,1... | collective-permute-start | bytes 344072 | tf_op jit(solution)/shard_map/ppermute | solution.py:23
  60.5 2.7 %collective-permute-start.23 = (bf16[64,3584]{1,0:T(8,128)(2,1)S(1)}, bf16[64,3584]{1,0:T(8,128)(2,1)S(1)}, u32[]{:S(2)}, u32[]{:S(2)}) collective-permute-start(bf16[64,3584]{1,0:T(8,128)(2,1)S(1)} %collective-permute-done.18.refs_0_), channel_id=1, source_target_pairs={{0,224},{32,0},{64,32},{96,64},{128,96},{160,128},{192,160},{224,1... | collective-permute-start | bytes 1376264 | tf_op jit(solution)/shard_map/ppermute | solution.py:23
  63.2 8.4 %collective-permute-done.23.refs_5_ = bf16[64,3584]{1,0:T(8,128)(2,1)S(1)} collective-permute-done((bf16[64,3584]{1,0:T(8,128)(2,1)S(1)}, bf16[64,3584]{1,0:T(8,128)(2,1)S(1)}, u32[]{:S(2)}, u32[]{:S(2)}) %collective-permute-start.23) | collective-permute-done | bytes 458784 | tf_op jit(solution)/shard_map/ppermute | solution.py:23
  71.6 1.2 collective-permute-start.8
  72.8 3.5 %collective-permute-start.26 = (bf16[32,3584]{1,0:T(8,128)(2,1)S(1)}, bf16[32,3584]{1,0:T(8,128)(2,1)S(1)}, u32[]{:S(2)}, u32[]{:S(2)}) collective-permute-start(bf16[32,3584]{1,0:T(8,128)(2,1)S(1)} %slice.622), channel_id=1, source_target_pairs={{0,224},{32,0},{64,32},{96,64},{128,96},{160,128},{192,160},{224,1... | collective-permute-start | bytes 688136 | tf_op jit(solution)/shard_map/ppermute | solution.py:23
  76.5 2.8 %collective-permute-done.26 = bf16[32,3584]{1,0:T(8,128)(2,1)S(1)} collective-permute-done((bf16[32,3584]{1,0:T(8,128)(2,1)S(1)}, bf16[32,3584]{1,0:T(8,128)(2,1)S(1)}, u32[]{:S(2)}, u32[]{:S(2)}) %collective-permute-start.26) | collective-permute-done | bytes 229408 | tf_op jit(solution)/shard_map/ppermute | solution.py:23
  79.3 1.5 collective-permute-start.9
  80.8 2.1 %collective-permute-done.25 = bf16[32,3584]{1,0:T(8,128)(2,1)S(1)} collective-permute-done((bf16[32,3584]{1,0:T(8,128)(2,1)S(1)}, bf16[32,3584]{1,0:T(8,128)(2,1)S(1)}, u32[]{:S(2)}, u32[]{:S(2)}) %collective-permute-start.25) | collective-permute-done | bytes 229408 | tf_op jit(solution)/shard_map/ppermute | solution.py:23
  84.4 3.5 %collective-permute-done.9.refs_5_ = bf16[64,3584]{1,0:T(8,128)(2,1)S(1)} collective-permute-done((bf16[64,3584]{1,0:T(8,128)(2,1)S(1)}, bf16[64,3584]{1,0:T(8,128)(2,1)S(1)}, u32[]{:S(2)}, u32[]{:S(2)}) %collective-permute-start.9) | collective-permute-done | bytes 458784 | tf_op jit(solution)/shard_map/ppermute | solution.py:23
  89.1 8.6 %collective-permute-done.20.refs_2_ = bf16[64,3584]{1,0:T(8,128)(2,1)S(1)} collective-permute-done((bf16[64,3584]{1,0:T(8,128)(2,1)S(1)}, bf16[64,3584]{1,0:T(8,128)(2,1)S(1)}, u32[]{:S(2)}, u32[]{:S(2)}) %collective-permute-start.20) | collective-permute-done | bytes 458784 | tf_op jit(solution)/shard_map/ppermute | solution.py:23
  97.7 2.7 %collective-permute-start.24 = (bf16[64,3584]{1,0:T(8,128)(2,1)S(1)}, bf16[64,3584]{1,0:T(8,128)(2,1)S(1)}, u32[]{:S(2)}, u32[]{:S(2)}) collective-permute-start(bf16[64,3584]{1,0:T(8,128)(2,1)S(1)} %collective-permute-done.20.refs_2_), channel_id=1, source_target_pairs={{0,24},{8,0},{16,8},{24,16},{1,25},{9,1},{17,9},{25,17},{2,26},{10... | collective-permute-start | bytes 1376264 | tf_op jit(solution)/shard_map/ppermute | solution.py:23
  100.4 12.2 %shard_map.77 = f32[2,512]{1,0:T(2,128)S(1)} custom-call(s32[4]{0:T(128)S(1)} %pad_add_fusion.starts, s32[1,512]{1,0:T(1,128)S(1)} %bitcast.275, bf16[64,3584]{1,0:T(8,128)(2,1)S(1)} %pad_maximum_fusion.refs_0_, bf16[64,3584]{1,0:T(8,128)(2,1)} %collective-permute-done.3.refs_1_, bf16[64,3584]{1,0:T(8,128)(2,1)} %collective-permute-done.4.refs_2_, ...), custom_call_target="tpu_custom_call" | custom-call | flops 5637144576 | bytes 14680064 | tf_op jit(solution)/shard_map/pallas_call | solution.py:96
  112.9 12.7 %shard_map.78 = f32[2,512]{1,0:T(2,128)S(1)} custom-call(s32[4]{0:T(128)S(1)} %pad_add_fusion.starts, s32[1,512]{1,0:T(1,128)S(1)} %bitcast.274, bf16[64,3584]{1,0:T(8,128)(2,1)S(1)} %collective-permute-done.18.refs_0_, bf16[64,3584]{1,0:T(8,128)(2,1)S(1)} %collective-permute-done.19.refs_1_, bf16[64,3584]{1,0:T(8,128)(2,1)S(1)} %collective-permute-done.20.refs_2_, ...), custom_call_target="tpu_custom_call" | custom-call | flops 5637144576 | bytes 14680064 | tf_op jit(solution)/shard_map/pallas_call | solution.py:96
  129.1 6.1 %all-to-all-start = ((f32[32,1,64]{2,1,0:T(1,128)}), f32[32,1,64]{2,1,0:T(1,128)S(1)}, u32[]{:S(2)}, u32[]{:S(2)}) async-start(f32[32,1,64]{2,1,0:T(1,128)} %bitcast.103), calls=%async_computation | async-start | bytes 32768 | tf_op jit(solution)/shard_map/all_to_all | solution.py:225
  135.2 8.6 %all-to-all-done = f32[32,1,64]{2,1,0:T(1,128)S(1)} async-done(((f32[32,1,64]{2,1,0:T(1,128)}), f32[32,1,64]{2,1,0:T(1,128)S(1)}, u32[]{:S(2)}, u32[]{:S(2)}) %all-to-all-start) | async-done | bytes 8224 | tf_op jit(solution)/shard_map/all_to_all | solution.py:225
  144.7 13.0 %all-to-all-start.1 = ((f32[256,1,128]{2,1,0:T(1,128)}), f32[256,1,128]{2,1,0:T(1,128)S(1)}, u32[]{:S(2)}, u32[]{:S(2)}) async-start(f32[256,1,128]{2,1,0:T(1,128)} %broadcast_in_dim.8), calls=%async_computation.1 | async-start | bytes 262144 | tf_op jit(solution)/shard_map/all_to_all | solution.py:233
  158.4 12.5 %all-to-all-done.1 = f32[256,1,128]{2,1,0:T(1,128)S(1)} async-done(((f32[256,1,128]{2,1,0:T(1,128)}), f32[256,1,128]{2,1,0:T(1,128)S(1)}, u32[]{:S(2)}, u32[]{:S(2)}) %all-to-all-start.1) | async-done | bytes 131104 | tf_op jit(solution)/shard_map/all_to_all | solution.py:233
  172.5 1.3 fusion.5
  (120 shorter events, 21.3 us)
Async XLA Ops:
  0.6 35.4 %collective-permute-start.16 = (bf16[3584,384]{1,0:T(8,128)(2,1)}, bf16[3584,384]{1,0:T(8,128)(2,1)}, u32[]{:S(2)}, u32[]{:S(2)}) collective-permute-start(bf16[3584,384]{1,0:T(8,128)(2,1)} %refs_8_.3), channel_id=1, source_target_pairs={{0,2},{1,7},{2,4},{3,1},{4,6},{5,3},{6,0},{7,5},{8,10},{9,15},{10,... | collective-permute-start | bytes 8257544 | tf_op jit(solution)/shard_map/ppermute | solution.py:154
  5.2 95.2 %copy-start = (bf16[3584,384]{1,0:T(8,128)(2,1)S(1)}, bf16[3584,384]{1,0:T(8,128)(2,1)}, u32[]{:S(2)}) copy-start(bf16[3584,384]{1,0:T(8,128)(2,1)} %refs_8_.3) | copy-start | bytes 8257540
  5.3 8.4 %collective-permute-start.2 = (bf16[16,3584]{1,0:T(8,128)(2,1)S(1)}, bf16[16,3584]{1,0:T(8,128)(2,1)S(1)}, u32[]{:S(2)}, u32[]{:S(2)}) collective-permute-start(bf16[16,3584]{1,0:T(8,128)(2,1)S(1)} %get-tuple-element.13), channel_id=1, source_target_pairs={{0,16},{8,24},{16,0},{24,8},{1,17},{9,25},{17,1},{25,9},{2,18},{10... | collective-permute-start | bytes 344072 | tf_op jit(solution)/shard_map/ppermute | solution.py:23
  8.1 9.6 %collective-permute-start.1 = (bf16[16,3584]{1,0:T(8,128)(2,1)S(1)}, bf16[16,3584]{1,0:T(8,128)(2,1)S(1)}, u32[]{:S(2)}, u32[]{:S(2)}) collective-permute-start(bf16[16,3584]{1,0:T(8,128)(2,1)S(1)} %get-tuple-element.13), channel_id=1, source_target_pairs={{0,24},{8,0},{16,8},{24,16},{1,25},{9,1},{17,9},{25,17},{2,26},{10... | collective-permute-start | bytes 344072 | tf_op jit(solution)/shard_map/ppermute | solution.py:23
  8.9 9.4 %collective-permute-start = (bf16[16,3584]{1,0:T(8,128)(2,1)S(1)}, bf16[16,3584]{1,0:T(8,128)(2,1)}, u32[]{:S(2)}, u32[]{:S(2)}) collective-permute-start(bf16[16,3584]{1,0:T(8,128)(2,1)S(1)} %get-tuple-element.13), channel_id=1, source_target_pairs={{0,8},{8,16},{16,24},{24,0},{1,9},{9,17},{17,25},{25,1},{2,10},{10... | collective-permute-start | bytes 344072 | tf_op jit(solution)/shard_map/ppermute | solution.py:23
  9.6 12.5 %collective-permute-start.5 = (bf16[16,3584]{1,0:T(8,128)(2,1)S(1)}, bf16[16,3584]{1,0:T(8,128)(2,1)}, u32[]{:S(2)}, u32[]{:S(2)}) collective-permute-start(bf16[16,3584]{1,0:T(8,128)(2,1)S(1)} %get-tuple-element.12), channel_id=1, source_target_pairs={{0,32},{32,64},{64,96},{96,128},{128,160},{160,192},{192,224},{224... | collective-permute-start | bytes 344072 | tf_op jit(solution)/shard_map/ppermute | solution.py:23
  13.6 8.5 %collective-permute-start.6 = (bf16[16,3584]{1,0:T(8,128)(2,1)S(1)}, bf16[16,3584]{1,0:T(8,128)(2,1)}, u32[]{:S(2)}, u32[]{:S(2)}) collective-permute-start(bf16[16,3584]{1,0:T(8,128)(2,1)S(1)} %get-tuple-element.12), channel_id=1, source_target_pairs={{0,224},{32,0},{64,32},{96,64},{128,96},{160,128},{192,160},{224,1... | collective-permute-start | bytes 344072 | tf_op jit(solution)/shard_map/ppermute | solution.py:23
  19.3 21.1 %collective-permute-start.3 = (bf16[64,3584]{1,0:T(8,128)(2,1)S(1)}, bf16[64,3584]{1,0:T(8,128)(2,1)}, u32[]{:S(2)}, u32[]{:S(2)}) collective-permute-start(bf16[64,3584]{1,0:T(8,128)(2,1)S(1)} %pad_maximum_fusion.refs_0_), channel_id=1, source_target_pairs={{0,32},{32,64},{64,96},{96,128},{128,160},{160,192},{192,224},{224... | collective-permute-start | bytes 1376264 | tf_op jit(solution)/shard_map/ppermute | solution.py:23
  19.4 22.5 %collective-permute-start.4 = (bf16[64,3584]{1,0:T(8,128)(2,1)S(1)}, bf16[64,3584]{1,0:T(8,128)(2,1)}, u32[]{:S(2)}, u32[]{:S(2)}) collective-permute-start(bf16[64,3584]{1,0:T(8,128)(2,1)S(1)} %pad_maximum_fusion.refs_0_), channel_id=1, source_target_pairs={{0,224},{32,0},{64,32},{96,64},{128,96},{160,128},{192,160},{224,1... | collective-permute-start | bytes 1376264 | tf_op jit(solution)/shard_map/ppermute | solution.py:23
  22.1 12.5 %collective-permute-start.7 = (bf16[16,3584]{1,0:T(8,128)(2,1)}, bf16[16,3584]{1,0:T(8,128)(2,1)S(1)}, u32[]{:S(2)}, u32[]{:S(2)}) collective-permute-start(bf16[16,3584]{1,0:T(8,128)(2,1)} %collective-permute-done.5), channel_id=1, source_target_pairs={{0,32},{32,64},{64,96},{96,128},{128,160},{160,192},{192,224},{224... | collective-permute-start | bytes 344072 | tf_op jit(solution)/shard_map/ppermute | solution.py:23
  22.2 78.2 %collective-permute-start.15 = (bf16[3584,384]{1,0:T(8,128)(2,1)}, bf16[3584,384]{1,0:T(8,128)(2,1)}, u32[]{:S(2)}, u32[]{:S(2)}) collective-permute-start(bf16[3584,384]{1,0:T(8,128)(2,1)} %refs_8_.3), channel_id=1, source_target_pairs={{0,1},{1,0},{2,3},{3,2},{4,5},{5,4},{6,7},{7,6},{8,9},{9,8},{10,11... | collective-permute-start | bytes 8257544 | tf_op jit(solution)/shard_map/ppermute | solution.py:23
  34.6 5.7 %collective-permute-start.10 = (bf16[16,3584]{1,0:T(8,128)(2,1)}, bf16[16,3584]{1,0:T(8,128)(2,1)}, u32[]{:S(2)}, u32[]{:S(2)}) collective-permute-start(bf16[16,3584]{1,0:T(8,128)(2,1)} %collective-permute-done.6), channel_id=1, source_target_pairs={{0,224},{32,0},{64,32},{96,64},{128,96},{160,128},{192,160},{224,1... | collective-permute-start | bytes 344072 | tf_op jit(solution)/shard_map/ppermute | solution.py:23
  36.0 64.4 %collective-permute-start.17 = (bf16[3584,384]{1,0:T(8,128)(2,1)}, bf16[3584,384]{1,0:T(8,128)(2,1)}, u32[]{:S(2)}, u32[]{:S(2)}) collective-permute-start(bf16[3584,384]{1,0:T(8,128)(2,1)} %collective-permute-done.16.refs_10_), channel_id=1, source_target_pairs={{0,1},{1,0},{2,3},{3,2},{4,5},{5,4},{6,7},{7,6},{8,9},{9,8},{10,11... | collective-permute-start | bytes 8257544 | tf_op jit(solution)/shard_map/ppermute | solution.py:23
  40.3 7.4 %collective-permute-start.11 = (bf16[16,3584]{1,0:T(8,128)(2,1)S(1)}, bf16[16,3584]{1,0:T(8,128)(2,1)S(1)}, u32[]{:S(2)}, u32[]{:S(2)}) collective-permute-start(bf16[16,3584]{1,0:T(8,128)(2,1)S(1)} %collective-permute-done.7), channel_id=1, source_target_pairs={{0,32},{32,64},{64,96},{96,128},{128,160},{160,192},{192,224},{224... | collective-permute-start | bytes 344072 | tf_op jit(solution)/shard_map/ppermute | solution.py:23
  40.4 20.0 %collective-permute-start.14 = (bf16[64,3584]{1,0:T(8,128)(2,1)}, bf16[64,3584]{1,0:T(8,128)(2,1)S(1)}, u32[]{:S(2)}, u32[]{:S(2)}) collective-permute-start(bf16[64,3584]{1,0:T(8,128)(2,1)} %collective-permute-done.3.refs_1_), channel_id=1, source_target_pairs={{0,32},{32,64},{64,96},{96,128},{128,160},{160,192},{192,224},{224... | collective-permute-start | bytes 1376264 | tf_op jit(solution)/shard_map/ppermute | solution.py:23
  41.9 18.5 %collective-permute-start.18 = (bf16[64,3584]{1,0:T(8,128)(2,1)}, bf16[64,3584]{1,0:T(8,128)(2,1)S(1)}, u32[]{:S(2)}, u32[]{:S(2)}) collective-permute-start(bf16[64,3584]{1,0:T(8,128)(2,1)} %collective-permute-done.4.refs_2_), channel_id=1, source_target_pairs={{0,224},{32,0},{64,32},{96,64},{128,96},{160,128},{192,160},{224,1... | collective-permute-start | bytes 1376264 | tf_op jit(solution)/shard_map/ppermute | solution.py:23
  47.7 9.4 %collective-permute-start.12 = (bf16[16,3584]{1,0:T(8,128)(2,1)}, bf16[16,3584]{1,0:T(8,128)(2,1)S(1)}, u32[]{:S(2)}, u32[]{:S(2)}) collective-permute-start(bf16[16,3584]{1,0:T(8,128)(2,1)} %collective-permute-done.10), channel_id=1, source_target_pairs={{0,224},{32,0},{64,32},{96,64},{128,96},{160,128},{192,160},{224,1... | collective-permute-start | bytes 344072 | tf_op jit(solution)/shard_map/ppermute | solution.py:23
  57.1 19.2 %collective-permute-start.13 = (bf16[16,3584]{1,0:T(8,128)(2,1)S(1)}, bf16[16,3584]{1,0:T(8,128)(2,1)S(1)}, u32[]{:S(2)}, u32[]{:S(2)}) collective-permute-start(bf16[16,3584]{1,0:T(8,128)(2,1)S(1)} %collective-permute-done.12), channel_id=1, source_target_pairs={{0,224},{32,0},{64,32},{96,64},{128,96},{160,128},{192,160},{224,1... | collective-permute-start | bytes 344072 | tf_op jit(solution)/shard_map/ppermute | solution.py:23
  60.4 12.4 %collective-permute-start.22 = (bf16[64,3584]{1,0:T(8,128)(2,1)S(1)}, bf16[64,3584]{1,0:T(8,128)(2,1)S(1)}, u32[]{:S(2)}, u32[]{:S(2)}) collective-permute-start(bf16[64,3584]{1,0:T(8,128)(2,1)S(1)} %collective-permute-done.14.refs_7_), channel_id=1, source_target_pairs={{0,32},{32,64},{64,96},{96,128},{128,160},{160,192},{192,224},{224... | collective-permute-start | bytes 1376264 | tf_op jit(solution)/shard_map/ppermute | solution.py:23
  60.5 11.1 %collective-permute-start.23 = (bf16[64,3584]{1,0:T(8,128)(2,1)S(1)}, bf16[64,3584]{1,0:T(8,128)(2,1)S(1)}, u32[]{:S(2)}, u32[]{:S(2)}) collective-permute-start(bf16[64,3584]{1,0:T(8,128)(2,1)S(1)} %collective-permute-done.18.refs_0_), channel_id=1, source_target_pairs={{0,224},{32,0},{64,32},{96,64},{128,96},{160,128},{192,160},{224,1... | collective-permute-start | bytes 1376264 | tf_op jit(solution)/shard_map/ppermute | solution.py:23
  71.6 12.4 %collective-permute-start.8 = (bf16[64,3584]{1,0:T(8,128)(2,1)S(1)}, bf16[64,3584]{1,0:T(8,128)(2,1)S(1)}, u32[]{:S(2)}, u32[]{:S(2)}) collective-permute-start(bf16[64,3584]{1,0:T(8,128)(2,1)S(1)} %pad_maximum_fusion.1.refs_3_), channel_id=1, source_target_pairs={{0,8},{8,16},{16,24},{24,0},{1,9},{9,17},{17,25},{25,1},{2,10},{10... | collective-permute-start | bytes 1376264 | tf_op jit(solution)/shard_map/ppermute | solution.py:23
  72.8 6.5 %collective-permute-start.26 = (bf16[32,3584]{1,0:T(8,128)(2,1)S(1)}, bf16[32,3584]{1,0:T(8,128)(2,1)S(1)}, u32[]{:S(2)}, u32[]{:S(2)}) collective-permute-start(bf16[32,3584]{1,0:T(8,128)(2,1)S(1)} %slice.622), channel_id=1, source_target_pairs={{0,224},{32,0},{64,32},{96,64},{128,96},{160,128},{192,160},{224,1... | collective-permute-start | bytes 688136 | tf_op jit(solution)/shard_map/ppermute | solution.py:23
  76.3 6.5 %collective-permute-start.25 = (bf16[32,3584]{1,0:T(8,128)(2,1)S(1)}, bf16[32,3584]{1,0:T(8,128)(2,1)S(1)}, u32[]{:S(2)}, u32[]{:S(2)}) collective-permute-start(bf16[32,3584]{1,0:T(8,128)(2,1)S(1)} %slice.621), channel_id=1, source_target_pairs={{0,32},{32,64},{64,96},{96,128},{128,160},{160,192},{192,224},{224... | collective-permute-start | bytes 688136 | tf_op jit(solution)/shard_map/ppermute | solution.py:23
  79.3 8.6 %collective-permute-start.9 = (bf16[64,3584]{1,0:T(8,128)(2,1)S(1)}, bf16[64,3584]{1,0:T(8,128)(2,1)S(1)}, u32[]{:S(2)}, u32[]{:S(2)}) collective-permute-start(bf16[64,3584]{1,0:T(8,128)(2,1)S(1)} %pad_maximum_fusion.1.refs_3_), channel_id=1, source_target_pairs={{0,24},{8,0},{16,8},{24,16},{1,25},{9,1},{17,9},{25,17},{2,26},{10... | collective-permute-start | bytes 1376264 | tf_op jit(solution)/shard_map/ppermute | solution.py:23
  82.8 14.9 %collective-permute-start.20 = (bf16[64,3584]{1,0:T(8,128)(2,1)S(1)}, bf16[64,3584]{1,0:T(8,128)(2,1)S(1)}, u32[]{:S(2)}, u32[]{:S(2)}) collective-permute-start(bf16[64,3584]{1,0:T(8,128)(2,1)S(1)} %constant_dynamic-update-slice_fusion.refs_6_), channel_id=1, source_target_pairs={{0,24},{8,0},{16,8},{24,16},{1,25},{9,1},{17,9},{25,17},{2,26},{10... | collective-permute-start | bytes 1376264 | tf_op jit(solution)/shard_map/ppermute | solution.py:23
  84.0 28.8 %collective-permute-start.19 = (bf16[64,3584]{1,0:T(8,128)(2,1)S(1)}, bf16[64,3584]{1,0:T(8,128)(2,1)S(1)}, u32[]{:S(2)}, u32[]{:S(2)}) collective-permute-start(bf16[64,3584]{1,0:T(8,128)(2,1)S(1)} %constant_dynamic-update-slice_fusion.refs_6_), channel_id=1, source_target_pairs={{0,8},{8,16},{16,24},{24,0},{1,9},{9,17},{17,25},{25,1},{2,10},{10... | collective-permute-start | bytes 1376264 | tf_op jit(solution)/shard_map/ppermute | solution.py:23
  87.9 24.9 %collective-permute-start.21 = (bf16[64,3584]{1,0:T(8,128)(2,1)S(1)}, bf16[64,3584]{1,0:T(8,128)(2,1)S(1)}, u32[]{:S(2)}, u32[]{:S(2)}) collective-permute-start(bf16[64,3584]{1,0:T(8,128)(2,1)S(1)} %collective-permute-done.8.refs_4_), channel_id=1, source_target_pairs={{0,8},{8,16},{16,24},{24,0},{1,9},{9,17},{17,25},{25,1},{2,10},{10... | collective-permute-start | bytes 1376264 | tf_op jit(solution)/shard_map/ppermute | solution.py:23
  97.7 15.1 %collective-permute-start.24 = (bf16[64,3584]{1,0:T(8,128)(2,1)S(1)}, bf16[64,3584]{1,0:T(8,128)(2,1)S(1)}, u32[]{:S(2)}, u32[]{:S(2)}) collective-permute-start(bf16[64,3584]{1,0:T(8,128)(2,1)S(1)} %collective-permute-done.20.refs_2_), channel_id=1, source_target_pairs={{0,24},{8,0},{16,8},{24,16},{1,25},{9,1},{17,9},{25,17},{2,26},{10... | collective-permute-start | bytes 1376264 | tf_op jit(solution)/shard_map/ppermute | solution.py:23
  112.8 22.4 %copy-start.4 = (s32[8]{0:T(128)S(1)}, s32[8]{0:T(128)}, u32[]{:S(2)}) copy-start(s32[8]{0:T(128)} %param.10) | copy-start | bytes 100
  112.9 44.9 %copy-start.2 = (f32[22]{0:T(128)S(1)}, f32[22]{0:T(128)}, u32[]{:S(2)}) copy-start(f32[22]{0:T(128)} %param.11) | copy-start | bytes 268
  129.1 14.7 %all-to-all-start = ((f32[32,1,64]{2,1,0:T(1,128)}), f32[32,1,64]{2,1,0:T(1,128)S(1)}, u32[]{:S(2)}, u32[]{:S(2)}) async-start(f32[32,1,64]{2,1,0:T(1,128)} %bitcast.103), calls=%async_computation | async-start | bytes 32768 | tf_op jit(solution)/shard_map/all_to_all | solution.py:225
  144.7 26.2 %all-to-all-start.1 = ((f32[256,1,128]{2,1,0:T(1,128)}), f32[256,1,128]{2,1,0:T(1,128)S(1)}, u32[]{:S(2)}, u32[]{:S(2)}) async-start(f32[256,1,128]{2,1,0:T(1,128)} %broadcast_in_dim.8), calls=%async_computation.1 | async-start | bytes 262144 | tf_op jit(solution)/shard_map/all_to_all | solution.py:233
  (2 other events, 23.0 us)

commit v2 on v0

v2 whole, which is shorter than its diff:
```python
import functools
import jax
import jax.numpy as jnp
from jax import lax
from jax.experimental import pallas as pl
from jax.experimental.pallas import tpu as pltpu
from jax.sharding import Mesh
from jax.sharding import PartitionSpec as P

SEQ_LEN = 16
DOMAINS = 22
explore_share = 0.01
step_rate = 0.002

ALL = ("z", "x", "yh", "yl", "c")
DP = ("z", "x")
VOCAB_AXES = ("yh", "yl", "c")
SUB = 16
VMEM_LIMIT = 60 * 2**20


def shift(a, axis, by):
    n = lax.axis_size(axis)
    return lax.ppermute(a, axis, [(i, (i + by) % n) for i in range(n)])


def together(*arrays):
    return lax.optimization_barrier(arrays)


def onward(a, axis):
    n = lax.axis_size(axis)
    moves = [
        (i * 2 + core, ((i + (1 if core == 0 else -1)) % n) * 2 + core)
        for i in range(n)
        for core in range(2)
    ]
    return lax.ppermute(a, (axis, "c"), moves)


def mirrored(a, axis):
    return jnp.roll(jnp.flip(a, axis), 1, axis)


def lane_parts(a):
    return [a[:, i : i + 128] for i in range(0, a.shape[1], 128)]


def stats_kernel(pieces, chunks, has_prev, others, starts, targets, *refs):
    n_arrays = 1 + max(p[0] for p in pieces)
    refs = list(refs)
    arrays = [refs.pop(0) for _ in range(n_arrays)]
    cols = [[refs.pop(0) for _ in range(n)] for n in chunks]
    prev = refs.pop(0) if has_prev else None
    earlier = [refs.pop(0) for _ in others]
    out, h_vm, w_vm, t_vm, m_vm, s_vm, p_vm, h_sem, w_sem = refs
    width = cols[0][0].shape[1]
    total = sum(p[2] for p in pieces)
    padded = m_vm.shape[0]
    h_copies, at = [], 0
    for i, (k, first, n, _) in enumerate(pieces):
        h_copies.append(
            pltpu.make_async_copy(
                arrays[k].at[pl.ds(first, n)], h_vm.at[pl.ds(at, n)], h_sem.at[i]
            )
        )
        at += n
    w_copies, used = [], 0
    for k, chunk_refs in enumerate(cols):
        copies, depth = [], 0
        for w in chunk_refs:
            to = w_vm.at[pl.ds(depth, w.shape[0]), pl.ds(k * width, width)]
            copies.append(pltpu.make_async_copy(w, to, w_sem.at[used]))
            depth += w.shape[0]
            used += 1
        w_copies.append(copies)
    for copy in h_copies + sum(w_copies, []):
        copy.start()
    spread = jnp.broadcast_to(targets[...].astype(jnp.float32), (128, padded))
    t_vm[...] = spread.T.astype(jnp.int32)
    if padded > total:
        rest = pl.ds(total, padded - total)
        for ref in (m_vm, s_vm, p_vm):
            ref[rest] = jnp.zeros((padded - total, 128), jnp.float32)
    for copy in h_copies:
        copy.wait()
    here = pl.ds(0, total)
    for k in range(len(cols)):
        for copy in w_copies[k]:
            copy.wait()
        logits = jnp.dot(
            h_vm[...], w_vm[:, k * width : (k + 1) * width], preferred_element_type=jnp.float32
        )
        parts = lane_parts(logits)
        peak = functools.reduce(jnp.maximum, parts)
        if k:
            before = m_vm[here]
            peak = jnp.maximum(peak, before)
            mass = s_vm[here] * jnp.exp(before - peak)
            pick = p_vm[here]
        else:
            mass = jnp.zeros_like(peak)
            pick = jnp.zeros_like(peak)
        away = t_vm[here] - lax.broadcasted_iota(jnp.int32, peak.shape, 1)
        for i, part in enumerate(parts):
            column = starts[k] + i * 128
            mass = mass + jnp.exp(part - peak)
            pick = pick + jnp.where(away == column, part, 0.0)
        m_vm[here] = peak
        s_vm[here] = mass
        p_vm[here] = pick

    lane_peak = m_vm[...].T
    peak = jnp.max(lane_peak, axis=0, keepdims=True)
    mass = jnp.sum(s_vm[...].T * jnp.exp(lane_peak - peak), axis=0, keepdims=True)
    pick = jnp.sum(p_vm[...].T, axis=0, keepdims=True)
    if has_prev:
        joined = jnp.maximum(peak, prev[0:1, :])
        mass = mass * jnp.exp(peak - joined) + jnp.exp(prev[0:1, :] - joined)
        pick = pick + prev[1:2, :]
        peak = joined
    lse = peak + jnp.log(mass)
    if not others:
        out[0:1, :] = lse
        out[1:2, :] = pick
        return
    z, x, sign = (starts[len(cols) + i] for i in range(3))
    out[:, : 4 * SUB] = jnp.full((out.shape[0], 4 * SUB), -1e30, jnp.float32)
    out[:, 4 * SUB :] = jnp.zeros((out.shape[0], 4 * SUB), jnp.float32)
    found = [([s for p in pieces for s in p[3]], lse, pick)]
    found += [(subs, ref[0:1, :], ref[1:2, :]) for subs, ref in zip(others, earlier)]
    for subs, all_lse, all_pick in found:
        for i, (mz, mx, part, half) in enumerate(subs):
            row = lax.rem(z + mz * sign + 8, 8) * 4 + lax.rem(x + mx * sign + 4, 4)
            lanes = slice(i * SUB, (i + 1) * SUB)
            to = (part * 2 + half) * SUB
            out[pl.ds(row, 1), to : to + SUB] = all_lse[:, lanes]
            out[pl.ds(row, 1), 4 * SUB + to : 5 * SUB + to] = all_pick[:, lanes]


def wanted_of(targets, subs):
    picked = jnp.concatenate([targets[mz % 8, mx % 4, part, half] for mz, mx, part, half in subs])
    return jnp.pad(picked, (0, -picked.shape[0] % 128)).reshape(1, -1)


def tile_stats(pieces, wanted, cols, scalars, prev=None, others=()):
    arrays, listed = [], []
    for array, first, n, subs in pieces:
        for k, known in enumerate(arrays):
            if known is array:
                break
        else:
            k = len(arrays)
            arrays.append(array)
        listed.append((k, first, n, tuple(subs)))
    flat = sum(cols, [])
    depth, width = sum(w.shape[0] for w in cols[0]), flat[0].shape[1]
    n_cols = len(cols) * width
    total = sum(p[2] for p in listed)
    padded = -(-total // 128) * 128
    in_vmem = pl.BlockSpec(memory_space=pltpu.VMEM)
    any_spec = pl.BlockSpec(memory_space=pl.ANY)
    operands = [scalars, wanted, *arrays, *flat]
    in_specs = [pl.BlockSpec(memory_space=pltpu.SMEM), in_vmem]
    in_specs += [any_spec] * (len(arrays) + len(flat))
    if prev is not None:
        operands.append(prev)
        in_specs.append(in_vmem)
    for _, stats in others:
        operands.append(stats)
        in_specs.append(in_vmem)
    shape = (32, 8 * SUB) if others else (2, padded)
    subs = [s for p in listed for s in p[3]]
    stats = pl.pallas_call(
        functools.partial(
            stats_kernel, tuple(listed), tuple(len(w) for w in cols), prev is not None, tuple(o[0] for o in others)
        ),
        out_shape=jax.ShapeDtypeStruct(shape, jnp.float32),
        in_specs=in_specs,
        out_specs=in_vmem,
        scratch_shapes=[
            pltpu.VMEM((total, depth), jnp.bfloat16),
            pltpu.VMEM((depth, n_cols), jnp.bfloat16),
            pltpu.VMEM((padded, 128), jnp.int32),
            pltpu.VMEM((padded, 128), jnp.float32),
            pltpu.VMEM((padded, 128), jnp.float32),
            pltpu.VMEM((padded, 128), jnp.float32),
            pltpu.SemaphoreType.DMA((len(listed),)),
            pltpu.SemaphoreType.DMA((len(flat),)),
        ],
        compiler_params=pltpu.CompilerParams(vmem_limit_bytes=VMEM_LIMIT),
        cost_estimate=pl.CostEstimate(
            flops=2 * total * depth * n_cols,
            bytes_accessed=2 * depth * (total + n_cols),
            transcendentals=total * n_cols,
        ),
    )(*operands)
    return tuple(subs), stats


def finish_kernel(place, notes, weights, loss_out, weights_out, loss_vm, sum_vm, count_vm):
    n = notes[...]
    twin = pltpu.roll(n, 4, 1)
    top = jnp.maximum(n, twin)
    lse = top + jnp.log(jnp.exp(n - top) + jnp.exp(twin - top))
    raw = lse - pltpu.roll(n + twin, 96, 2)
    core_row = lax.broadcasted_iota(jnp.int32, (1, 8, 128), 1)
    lane = lax.broadcasted_iota(jnp.int32, (1, 8, 128), 2)
    seq = (core_row // 2) * 4 + (lane // SEQ_LEN) * 2 + core_row % 2
    position = lane % SEQ_LEN
    live = jnp.logical_and(core_row < 4, lane < 2 * SEQ_LEN)
    length = jnp.zeros_like(n)
    label = jnp.full(n.shape, -1.0, jnp.float32)
    for k in range(8):
        here = jnp.logical_and(seq == k, live)
        length = jnp.where(here, n[:, 0:1, 64 + k : 65 + k], length)
        label = jnp.where(here, n[:, 0:1, 72 + k : 73 + k], label)
    loss = jnp.where(position.astype(jnp.float32) < length, raw, 0.0)
    count = jnp.where(position == 0, length, 0.0)
    loss_vm[...] = loss
    sum_vm[...] = jnp.zeros_like(sum_vm)
    count_vm[...] = jnp.zeros_like(count_vm)
    for d in range(DOMAINS):
        inside = label == float(d)
        sum_d = jnp.sum(jnp.where(inside, loss, 0.0), axis=0)
        count_d = jnp.sum(jnp.where(inside, count, 0.0), axis=0)
        sum_vm[d : d + 1, :] = jnp.sum(sum_d, axis=0, keepdims=True)
        count_vm[d : d + 1, :] = jnp.sum(count_d, axis=0, keepdims=True)
    domain_loss = jnp.sum(sum_vm[...], axis=1, keepdims=True)
    domain_count = jnp.sum(count_vm[...], axis=1, keepdims=True)
    w = weights[...]
    probability = (1.0 - DOMAINS * explore_share) * w / jnp.sum(w, axis=0, keepdims=True)
    probability = probability + explore_share
    reward = domain_loss / jnp.maximum(domain_count, 1.0) / probability
    raised = w * jnp.exp(step_rate * reward)
    weights_out[...] = DOMAINS * raised / jnp.sum(raised, axis=0, keepdims=True)
    mine = loss_vm[place[0]]
    for row in range(4):
        for part in range(2):
            to = ((row // 2) * 4 + part * 2 + row % 2) * SEQ_LEN
            loss_out[:, to : to + SEQ_LEN] = mine[
                row : row + 1, part * SEQ_LEN : (part + 1) * SEQ_LEN
            ]


def rolled(a, axis, by):
    n = a.shape[axis]
    twice = jnp.concatenate([a, a], axis=axis)
    return lax.dynamic_slice_in_dim(twice, by, n, axis)


def merged(lse, axis):
    top = jnp.max(lse, axis=axis, keepdims=True)
    return jnp.squeeze(top, axis) + jnp.log(jnp.sum(jnp.exp(lse - top), axis=axis))


def body(hidden_states, head_weight, target_ids, seq_lengths, domain_labels, domain_weights):
    z, x = lax.axis_index("z"), lax.axis_index("x")
    yh, yl, c = (lax.axis_index(a) for a in VOCAB_AXES)
    nz, nx = lax.axis_size("z"), lax.axis_size("x")
    dp_count = nz * nx
    dp_index = z * nx + x
    y = yh * 2 + yl
    width = head_weight.shape[1]
    sign = 1 - 2 * c

    targets = target_ids.reshape(nz, nx, 2, 2, 2, SUB)
    targets = lax.dynamic_index_in_dim(targets, yl, 2, keepdims=False)
    targets = rolled(rolled(targets, 0, z), 1, x)
    other = jnp.flip(mirrored(mirrored(targets, 0), 1), 3)
    targets = jnp.where(c == 0, targets, other)

    def start_of(y_at, core):
        return (dp_index * 8 + (y_at % 4) * 2 + core) * width

    def start_in(core):
        return jnp.where(core == 0, start_of(y + 3, 0), start_of(y + 1, 1))

    own_starts = [start_of(y, c), start_of(y, 1 - c)]
    in_starts = [start_in(c), start_in(1 - c)]

    def scalars(*values):
        return jnp.stack(values).astype(jnp.int32)

    def rows_of(part, half):
        first = (yl * 4 + part * 2 + half) * SUB
        return lax.dynamic_slice_in_dim(hidden_states, first, SUB, 0)

    moves = [
        (k * 2 + core, ((k + (1 if core == 0 else -1)) % 4) * 2 + core)
        for k in range(4)
        for core in range(2)
    ]
    def moved(subs, dz, dx):
        return [(mz + dz, mx + dx, part, half) for mz, mx, part, half in subs]

    def mates(subs):
        return [(-mz, -mx, part, 1 - half) for mz, mx, part, half in subs]

    subs_a = [(0, 0, 0, 0), (0, -1, 0, 0), (0, -1, 0, 1), (0, -2, 0, 0)]
    subs_b1 = [(0, 0, 1, 0), (-1, 0, 1, 0), (-1, 0, 1, 1), (-2, 0, 1, 0), (-2, 0, 1, 1)]
    subs_b2 = [(-3, 0, 1, 0), (-3, 0, 1, 1), (-4, 0, 1, 0)]

    mine_1 = [
        subs_a,
        subs_b1,
        moved(subs_a, -1, 0),
        moved(mates(subs_a), -1, 0),
        moved(subs_b1, 0, -1),
        moved(mates(subs_b1), 0, -1),
        subs_b2[:2],
    ]
    mine_3 = [
        moved(subs_a, -2, 0),
        moved(mates(subs_a), -2, 0),
        moved(subs_b1, 0, -2),
        subs_b2[2:],
    ]
    mine_4 = [
        moved(subs_a, -3, 0),
        moved(mates(subs_a), -3, 0),
        moved(subs_b2, 0, -1),
        moved(mates(subs_b2), 0, -1),
        moved(subs_a, -4, 0),
        moved(subs_b2, 0, -2),
    ]
    subs_1, subs_3, subs_4 = (sum(m, []) for m in (mine_1, mine_3, mine_4))

    def pieces_of(arrays, subs):
        return [(a, 0, a.shape[0], s) for a, s in zip(arrays, subs)]

    col_in = lax.ppermute(head_weight, VOCAB_AXES, moves)
    own_a = jnp.concatenate([rows_of(0, c), rows_of(0, 1 - c)], axis=0)
    own_b = jnp.concatenate([rows_of(1, c), rows_of(1, 1 - c)], axis=0)
    xa1, zb1 = onward(own_a, "x"), onward(own_b, "z")
    xa1, zb1 = together(xa1, zb1)
    xa2, zb2 = onward(xa1[:SUB], "x"), onward(zb1, "z")
    xa2, zb2, late_w = together(xa2, zb2, head_weight)
    mine_a = jnp.concatenate([own_a[:SUB], xa1, xa2], axis=0)
    mine_b1 = jnp.concatenate([own_b[:SUB], zb1, zb2], axis=0)
    xb1, za1 = onward(mine_b1, "x"), onward(mine_a, "z")
    mate_b1, mate_a = shift(mine_b1, "c", 1), shift(mine_a, "c", 1)
    wanted = [wanted_of(targets, subs) for subs in (subs_1, subs_3, subs_4)]
    xb1_mate, za1_mate, zb3 = onward(mate_b1, "x"), onward(mate_a, "z"), onward(zb2, "z")
    col_mate = shift(late_w, "c", 1)
    xb1, za1, xb1_mate, za1_mate, zb3, col_mate, col_in, *wanted = together(
        xb1, za1, xb1_mate, za1_mate, zb3, col_mate, col_in, *wanted
    )
    za2, za2_mate = onward(za1, "z"), onward(za1_mate, "z")
    xb2, zb4 = onward(xb1, "x"), onward(zb3[:SUB], "z")

    pieces = pieces_of([mine_a, mine_b1, za1, za1_mate, xb1, xb1_mate, zb3], mine_1)
    near_cols = [[head_weight], [col_mate]]
    _, stats_1 = tile_stats(pieces, wanted[0], near_cols, scalars(*own_starts))
    za2, za2_mate, xb2, zb4, stats_1 = together(za2, za2_mate, xb2, zb4, stats_1)
    za3, za3_mate = onward(za2, "z"), onward(za2_mate, "z")
    mine_b2 = jnp.concatenate([zb3, zb4], axis=0)
    mate_b2 = shift(mine_b2, "c", 1)
    xb3, xb3_mate = onward(mine_b2, "x"), onward(mate_b2, "x")
    col_in_mate = shift(col_in, "c", 1)
    far_cols = [[col_in], [col_in_mate]]
    done_1 = tile_stats(pieces, wanted[0], far_cols, scalars(*in_starts), prev=stats_1)
    stats_2 = done_1[1]
    za3, za3_mate, xb3, xb3_mate, stats_2 = together(za3, za3_mate, xb3, xb3_mate, stats_2)
    za4, xb4 = onward(za3, "z"), onward(xb3, "x")
    cols = near_cols + far_cols
    pieces = pieces_of([za2, za2_mate, xb2, zb4], mine_3)
    done_2 = tile_stats(pieces, wanted[1], cols, scalars(*own_starts, *in_starts))
    stats_3 = done_2[1]
    za4, xb4, stats_3 = together(za4, xb4, stats_3)
    pieces = pieces_of([za3, za3_mate, xb3, xb3_mate, za4, xb4], mine_4)
    _, every = tile_stats(
        pieces,
        wanted[2],
        cols,
        scalars(*own_starts, *in_starts, z, x, sign),
        others=[(done_1[0], stats_2), (done_2[0], stats_3)],
    )
    share = 4 * SUB
    mine = lax.all_to_all(every, DP, 0, 0, tiled=True)
    found = jnp.concatenate([merged(mine[:, :share], 0), jnp.sum(mine[:, share:], axis=0)])
    halves = found.reshape(2, 2, 2, SUB)
    rest = jnp.flip(shift(found, "c", 1).reshape(2, 2, 2, SUB), 2)
    lse = merged(jnp.stack([halves[0, :, 0], rest[0, :, 0]]), 0).reshape(-1)
    pick = (halves[1, :, 0] + rest[1, :, 0]).reshape(-1)
    note = jnp.concatenate(
        [lse, pick, seq_lengths.astype(jnp.float32), domain_labels.astype(jnp.float32)]
    )
    note = jnp.pad(note, (0, 128 - note.shape[0]))
    sent = jnp.broadcast_to(note[None], (lax.axis_size(ALL), 128))
    notes = lax.all_to_all(sent, ALL, 0, 0, tiled=True)
    weights = jnp.pad(domain_weights, (0, 32 - DOMAINS)).reshape(32, 1)
    token_loss, new_weights = pl.pallas_call(
        finish_kernel,
        out_shape=(
            jax.ShapeDtypeStruct((1, 128), jnp.float32),
            jax.ShapeDtypeStruct((32, 1), jnp.float32),
        ),
        in_specs=[
            pl.BlockSpec(memory_space=pltpu.SMEM),
            pl.BlockSpec(memory_space=pltpu.VMEM),
            pl.BlockSpec(memory_space=pltpu.VMEM),
        ],
        out_specs=(
            pl.BlockSpec(memory_space=pltpu.VMEM),
            pl.BlockSpec(memory_space=pltpu.VMEM),
        ),
        scratch_shapes=[
            pltpu.VMEM((dp_count, 8, 128), jnp.float32),
            pltpu.VMEM((32, 128), jnp.float32),
            pltpu.VMEM((32, 128), jnp.float32),
        ],
    )(dp_index.reshape(1), notes.reshape(dp_count, 8, 128), weights)
    return (token_loss.reshape(-1), new_weights[:DOMAINS, 0])


def solution(mesh):
    torus = Mesh(mesh.devices.reshape(8, 4, 2, 2, 2), ALL)
    in_specs = (P(DP, None), P(None, ALL), P(), P(DP), P(DP), P())
    out_specs = (P(DP), P())
    return jax.shard_map(body, mesh=torus, in_specs=in_specs, out_specs=out_specs, check_vma=False)
```

time: 305 us -> 158 us (0.52)
  waiting for transfers between devices: 204 us -> 30.3 us
  Pallas kernels: 0 us -> 40.4 us
  starting transfers between devices: 25 us -> 51.1 us
  between operations: 17.5 us -> 1.03 us
  matrix products: 16.3 us -> 0 us
  blocking collectives: 27.6 us -> 15 us
  local copies, waits for them, and re-layouts: 6.4 us -> 13.5 us
    all_gather x2 -> x0, waiting for transfers between devices: 164 us -> none  [the longest x1 110 us: body(): lax.all_gather(head_weight, 'vocab', axis=1, tiled=True)]
    ppermute x0 -> x26, starting transfers between devices: none -> 45 us  [the longest x19 37.7 us: onward(): return lax.ppermute(a, (axis, 'c'), moves)]
    pallas_call x0 -> x5, Pallas kernels: none -> 40.4 us  [the longest x4 37.4 us: tile_stats(): pl.pallas_call(functools.partial(stats_kernel, tuple(listed), tuple((len(...]
    all_gather x2 -> x0, blocking collectives: 27.6 us -> none  [the longest x1 15.1 us: gather_turned(): whole = lax.all_gather(both, axis, axis=0, tiled=True)]
    all_to_all x5 -> x1, waiting for transfers between devices: 39.9 us -> 12.3 us  [body(): notes = lax.all_to_all(sent, ALL, 0, 0, tiled=True)]
    all_to_all x5 -> x1, starting transfers between devices: 24.9 us -> 6.14 us  [body(): notes = lax.all_to_all(sent, ALL, 0, 0, tiled=True)]
    ppermute x0 -> x26, waiting for transfers between devices: none -> 18.1 us  [the longest x19 15.9 us: onward(): return lax.ppermute(a, (axis, 'c'), moves)]
    dot_general x1 -> x0, matrix products: 16.3 us -> none  [body(): jnp.dot(scored_rows, lax.all_gather(head_weight, 'vocab', axis=1, tiled=T...]
  transfers between devices with their start and end apart: 7 -> 27, of which waited for: 7 -> 10; matrix products, arithmetic and copies ran while one was open for 1% -> 7% of each run, Pallas kernels for 0% -> 16%
where the time goes in v2:
time: 158 us; the launch traced here: 157 us
  starting transfers between devices  51.1 us (32%)
  Pallas kernels  40.4 us (26%)
  waiting for transfers between devices  30.3 us (19%)
  blocking collectives  15 us (9%)
  local copies, waits for them, and re-layouts  13.5 us (9%)
  other arithmetic  5.98 us (4%)
    ppermute x19, starting transfers between devices, onward(): return lax.ppermute(a, (axis, 'c'), moves)  37.7 us
    pallas_call x4, Pallas kernels, tile_stats(): pl.pallas_call(functools.partial(stats_kernel, tuple(listed), tuple((len(...  37.4 us
    ppermute x19, waiting for transfers between devices, onward(): return lax.ppermute(a, (axis, 'c'), moves)  15.9 us
    all_to_all x1, blocking collectives, body(): mine = lax.all_to_all(every, DP, 0, 0, tiled=True)  15 us
    all_to_all x1, waiting for transfers between devices, body(): notes = lax.all_to_all(sent, ALL, 0, 0, tiled=True)  12.3 us
    all_to_all x1, starting transfers between devices, body(): notes = lax.all_to_all(sent, ALL, 0, 0, tiled=True)  6.14 us
    unnamed x31, local copies, waits for them, and re-layouts  4.91 us
    ppermute x6, starting transfers between devices, shift(): return lax.ppermute(a, axis, [(i, (i + by) % n) for i in range(n)])  4.56 us
  transfers between devices with their start and end apart: 27, of which 10 were waited for; matrix products, arithmetic and copies ran while one was open for 7% of the time, Pallas kernels for 16%

profile of v2, /device:TPU:1, one launch (start us, length us, event | category | flops | bytes accessed | tf_op | source)
XLA Modules:
  0.0 157.4 jit_solution(13405129214147168829)
XLA Ops:
  1.8 6.5 %collective-permute-start.1 = (bf16[32,3584]{1,0:T(8,128)(2,1)S(1)}, bf16[32,3584]{1,0:T(8,128)(2,1)S(1)}, u32[]{:S(2)}, u32[]{:S(2)}) collective-permute-start(bf16[32,3584]{1,0:T(8,128)(2,1)S(1)} %pad_maximum_fusion.3), channel_id=1, source_target_pairs={{0,32},{1,225},{32,64},{33,1},{64,96},{65,33},{96,128},{97,65},{12... | collective-permute-start | bytes 688136 | tf_op jit(solution)/shard_map/ppermute | solution.py:38
  8.3 2.6 %collective-permute-start = (bf16[32,3584]{1,0:T(8,128)(2,1)S(1)}, bf16[32,3584]{1,0:T(8,128)(2,1)S(1)}, u32[]{:S(2)}, u32[]{:S(2)}) collective-permute-start(bf16[32,3584]{1,0:T(8,128)(2,1)S(1)} %pad_maximum_fusion.2), channel_id=1, source_target_pairs={{0,8},{1,25},{8,16},{9,1},{16,24},{17,9},{24,0},{25,17},{2,10},{3,... | collective-permute-start | bytes 688136 | tf_op jit(solution)/shard_map/ppermute | solution.py:38
  11.2 2.6 %collective-permute-done = bf16[32,3584]{1,0:T(8,128)(2,1)S(1)} collective-permute-done((bf16[32,3584]{1,0:T(8,128)(2,1)S(1)}, bf16[32,3584]{1,0:T(8,128)(2,1)S(1)}, u32[]{:S(2)}, u32[]{:S(2)}) %collective-permute-start) | collective-permute-done | bytes 229408 | tf_op jit(solution)/shard_map/ppermute | solution.py:38
  14.7 3.1 %collective-permute-start.2 = (bf16[16,3584]{1,0:T(8,128)(2,1)S(1)}, bf16[16,3584]{1,0:T(8,128)(2,1)S(1)}, u32[]{:S(2)}, u32[]{:S(2)}) collective-permute-start(bf16[16,3584]{1,0:T(8,128)(2,1)S(1)} %slice.247), channel_id=1, source_target_pairs={{0,8},{1,25},{8,16},{9,1},{16,24},{17,9},{24,0},{25,17},{2,10},{3,... | collective-permute-start | bytes 344072 | tf_op jit(solution)/shard_map/ppermute | solution.py:38
  17.7 2.7 %collective-permute-start.12 = (bf16[3584,384]{1,0:T(8,128)(2,1)}, bf16[3584,384]{1,0:T(8,128)(2,1)S(1)}, u32[]{:S(2)}, u32[]{:S(2)}) collective-permute-start(bf16[3584,384]{1,0:T(8,128)(2,1)} %refs_6_.1), channel_id=1, source_target_pairs={{0,2},{1,7},{2,4},{3,1},{4,6},{5,3},{6,0},{7,5},{8,10},{9,15},{10,... | collective-permute-start | bytes 8257544 | tf_op jit(solution)/shard_map/ppermute | solution.py:332
  22.5 1.8 %collective-permute-start.10 = (bf16[32,3584]{1,0:T(8,128)(2,1)}, bf16[32,3584]{1,0:T(8,128)(2,1)S(1)}, u32[]{:S(2)}, u32[]{:S(2)}) collective-permute-start(bf16[32,3584]{1,0:T(8,128)(2,1)} %copy-done.6), channel_id=1, source_target_pairs={{0,32},{1,225},{32,64},{33,1},{64,96},{65,33},{96,128},{97,65},{12... | collective-permute-start | bytes 688136 | tf_op jit(solution)/shard_map/ppermute | solution.py:38
  24.4 2.0 %pad_maximum_fusion.refs_1_ = bf16[80,3584]{1,0:T(8,128)(2,1)} fusion(bf16[32,3584]{1,0:T(8,128)(2,1)} %copy-done.6, bf16[32,3584]{1,0:T(8,128)(2,1)} %copy-done.5, bf16[16,3584]{1,0:T(8,128)(2,1)S(1)} %get-tuple-element.66), kind=kLoop, calls=%fused_computation | loop fusion | flops 1720320 | bytes 1146880 | tf_op jit(solution)/shard_map/concatenate | solution.py:340
  28.2 2.8 %collective-permute-start.5 = (bf16[64,3584]{1,0:T(8,128)(2,1)}, bf16[64,3584]{1,0:T(8,128)(2,1)}, u32[]{:S(2)}, u32[]{:S(2)}) collective-permute-start(bf16[64,3584]{1,0:T(8,128)(2,1)} %pad_maximum_fusion.1.refs_0_), channel_id=1, source_target_pairs={{0,32},{1,225},{32,64},{33,1},{64,96},{65,33},{96,128},{97,65},{12... | collective-permute-start | bytes 1376264 | tf_op jit(solution)/shard_map/ppermute | solution.py:38
  31.3 1.2 collective-permute-start.4
  32.5 5.0 %collective-permute-done.5.refs_2_ = bf16[64,3584]{1,0:T(8,128)(2,1)} collective-permute-done((bf16[64,3584]{1,0:T(8,128)(2,1)}, bf16[64,3584]{1,0:T(8,128)(2,1)}, u32[]{:S(2)}, u32[]{:S(2)}) %collective-permute-start.5) | collective-permute-done | bytes 458784 | tf_op jit(solution)/shard_map/ppermute | solution.py:38
  37.5 2.6 %collective-permute-start.9 = (bf16[64,3584]{1,0:T(8,128)(2,1)}, bf16[64,3584]{1,0:T(8,128)(2,1)}, u32[]{:S(2)}, u32[]{:S(2)}) collective-permute-start(bf16[64,3584]{1,0:T(8,128)(2,1)} %collective-permute-done.8), channel_id=1, source_target_pairs={{0,32},{1,225},{32,64},{33,1},{64,96},{65,33},{96,128},{97,65},{12... | collective-permute-start | bytes 1376264 | tf_op jit(solution)/shard_map/ppermute | solution.py:38
  43.3 2.6 %collective-permute-done.9.refs_3_ = bf16[64,3584]{1,0:T(8,128)(2,1)} collective-permute-done((bf16[64,3584]{1,0:T(8,128)(2,1)}, bf16[64,3584]{1,0:T(8,128)(2,1)}, u32[]{:S(2)}, u32[]{:S(2)}) %collective-permute-start.9) | collective-permute-done | bytes 458784 | tf_op jit(solution)/shard_map/ppermute | solution.py:38
  45.8 3.4 %collective-permute-done.7.refs_5_ = bf16[80,3584]{1,0:T(8,128)(2,1)} collective-permute-done((bf16[80,3584]{1,0:T(8,128)(2,1)}, bf16[80,3584]{1,0:T(8,128)(2,1)}, u32[]{:S(2)}, u32[]{:S(2)}) %collective-permute-start.7) | collective-permute-done | bytes 573472 | tf_op jit(solution)/shard_map/ppermute | solution.py:38
  49.3 1.5 collective-permute-done.12.refs_7_.refs_6_.refs_8_
  52.4 1.2 collective-permute-start.15
  53.6 3.0 %collective-permute-start.13 = (bf16[64,3584]{1,0:T(8,128)(2,1)}, bf16[64,3584]{1,0:T(8,128)(2,1)}, u32[]{:S(2)}, u32[]{:S(2)}) collective-permute-start(bf16[64,3584]{1,0:T(8,128)(2,1)} %collective-permute-done.5.refs_2_), channel_id=1, source_target_pairs={{0,32},{1,225},{32,64},{33,1},{64,96},{65,33},{96,128},{97,65},{12... | collective-permute-start | bytes 1376264 | tf_op jit(solution)/shard_map/ppermute | solution.py:38
  57.3 1.4 collective-permute-start.16
  58.7 8.2 %shard_map.77.refs_9_ = f32[2,512]{1,0:T(2,128)} custom-call(s32[2]{0:T(128)} %pad_add_fusion.3.starts, s32[1,512]{1,0:T(1,128)} %bitcast.159, bf16[64,3584]{1,0:T(8,128)(2,1)} %pad_maximum_fusion.1.refs_0_, bf16[80,3584]{1,0:T(8,128)(2,1)} %pad_maximum_fusion.refs_1_, bf16[64,3584]{1,0:T(8,128)(2,1)} %collective-permute-done.5.refs_2_, ...), custom_call_target="tpu_custom_call" | custom-call | flops 2554331136 | bytes 8830976 | tf_op jit(solution)/shard_map/pallas_call | solution.py:174
  66.9 1.4 collective-permute-done.16.refs_3_
  70.0 2.8 %collective-permute-start.17 = (bf16[64,3584]{1,0:T(8,128)(2,1)}, bf16[64,3584]{1,0:T(8,128)(2,1)}, u32[]{:S(2)}, u32[]{:S(2)}) collective-permute-start(bf16[64,3584]{1,0:T(8,128)(2,1)} %collective-permute-done.13.refs_0_), channel_id=1, source_target_pairs={{0,32},{1,225},{32,64},{33,1},{64,96},{65,33},{96,128},{97,65},{12... | collective-permute-start | bytes 1376264 | tf_op jit(solution)/shard_map/ppermute | solution.py:38
  72.8 1.9 %collective-permute-start.19 = (bf16[48,3584]{1,0:T(8,128)(2,1)}, bf16[48,3584]{1,0:T(8,128)(2,1)}, u32[]{:S(2)}, u32[]{:S(2)}) collective-permute-start(bf16[48,3584]{1,0:T(8,128)(2,1)} %constant_dynamic-update-slice_fusion), channel_id=1, source_target_pairs={{0,8},{1,25},{8,16},{9,1},{16,24},{17,9},{24,0},{25,17},{2,10},{3,... | collective-permute-start | bytes 1032200 | tf_op jit(solution)/shard_map/ppermute | solution.py:38
  75.4 8.2 %shard_map.78.refs_10_ = f32[2,512]{1,0:T(2,128)} custom-call(s32[2]{0:T(128)} %pad_add_fusion.4.starts, s32[1,512]{1,0:T(1,128)} %bitcast.160, bf16[64,3584]{1,0:T(8,128)(2,1)} %pad_maximum_fusion.1.refs_0_, bf16[80,3584]{1,0:T(8,128)(2,1)} %pad_maximum_fusion.refs_1_, bf16[64,3584]{1,0:T(8,128)(2,1)} %collective-permute-done.5.refs_2_, ...), custom_call_target="tpu_custom_call" | custom-call | flops 2554331136 | bytes 8830976 | tf_op jit(solution)/shard_map/pallas_call | solution.py:174
  83.6 2.9 %collective-permute-start.23 = (bf16[64,3584]{1,0:T(8,128)(2,1)}, bf16[64,3584]{1,0:T(8,128)(2,1)S(1)}, u32[]{:S(2)}, u32[]{:S(2)}) collective-permute-start(bf16[64,3584]{1,0:T(8,128)(2,1)} %collective-permute-done.17.refs_0_), channel_id=1, source_target_pairs={{0,32},{1,225},{32,64},{33,1},{64,96},{65,33},{96,128},{97,65},{12... | collective-permute-start | bytes 1376264 | tf_op jit(solution)/shard_map/ppermute | solution.py:38
  86.5 1.9 %collective-permute-start.24 = (bf16[48,3584]{1,0:T(8,128)(2,1)}, bf16[48,3584]{1,0:T(8,128)(2,1)S(1)}, u32[]{:S(2)}, u32[]{:S(2)}) collective-permute-start(bf16[48,3584]{1,0:T(8,128)(2,1)} %collective-permute-done.19.refs_2_), channel_id=1, source_target_pairs={{0,8},{1,25},{8,16},{9,1},{16,24},{17,9},{24,0},{25,17},{2,10},{3,... | collective-permute-start | bytes 1032200 | tf_op jit(solution)/shard_map/ppermute | solution.py:38
  89.6 9.4 %shard_map.79.refs_11_ = f32[2,256]{1,0:T(2,128)} custom-call(s32[4]{0:T(128)} %pad_add_fusion.5.starts, s32[1,256]{1,0:T(1,128)} %bitcast.155, bf16[64,3584]{1,0:T(8,128)(2,1)} %collective-permute-done.13.refs_0_, bf16[64,3584]{1,0:T(8,128)(2,1)} %collective-permute-done.14.refs_1_, bf16[80,3584]{1,0:T(8,128)(2,1)} %copy-done.1, ...), custom_call_target="tpu_custom_call" | custom-call | flops 2466250752 | bytes 12615680 | tf_op jit(solution)/shard_map/pallas_call | solution.py:174
  100.7 11.6 %shard_map.80 = f32[32,128]{1,0:T(8,128)} custom-call(s32[7]{0:T(128)} %stack.51.starts, s32[1,384]{1,0:T(1,128)} %reshape.92.targets, bf16[64,3584]{1,0:T(8,128)(2,1)} %collective-permute-done.17.refs_0_, bf16[64,3584]{1,0:T(8,128)(2,1)} %collective-permute-done.18.refs_1_, bf16[48,3584]{1,0:T(8,128)(2,1)} %collective-permute-done.19.refs_2_, ...), custom_call_target="tpu_custom_call" | custom-call | flops 3699376128 | bytes 13418496 | tf_op jit(solution)/shard_map/pallas_call | solution.py:174
  112.3 15.0 %all_to_all.18 = f32[32,1,128]{2,1,0:T(1,128)S(1)} all-to-all(f32[32,1,128]{2,1,0:T(1,128)} %bitcast.154), channel_id=1, replica_groups=mesh['z'=8,'x'=4,'yh'=2,'yl'=2,'c'=2] {'z','x'}, dimensions={0} | all-to-all | bytes 32768 | tf_op jit(solution)/shard_map/all_to_all | solution.py:380
  127.5 2.6 %collective-permute-start.25 = (f32[128]{0:T(128)S(1)}, f32[128]{0:T(128)S(1)}, u32[]{:S(2)}, u32[]{:S(2)}) collective-permute-start(f32[128]{0:T(128)S(1)} %pad_maximum_fusion.4), channel_id=1, source_target_pairs={{0,1},{1,0},{2,3},{3,2},{4,5},{5,4},{6,7},{7,6},{8,9},{9,8},{10,11... | collective-permute-start | bytes 1544 | tf_op jit(solution)/shard_map/ppermute | solution.py:24
  133.3 6.1 %all-to-all-start.1 = ((f32[256,1,128]{2,1,0:T(1,128)}), f32[256,1,128]{2,1,0:T(1,128)S(1)}, u32[]{:S(2)}, u32[]{:S(2)}) async-start(f32[256,1,128]{2,1,0:T(1,128)} %broadcast_in_dim.2), calls=%async_computation.1 | async-start | bytes 262144 | tf_op jit(solution)/shard_map/all_to_all | solution.py:391
  140.2 12.3 %all-to-all-done.1 = f32[256,1,128]{2,1,0:T(1,128)S(1)} async-done(((f32[256,1,128]{2,1,0:T(1,128)}), f32[256,1,128]{2,1,0:T(1,128)S(1)}, u32[]{:S(2)}, u32[]{:S(2)}) %all-to-all-start.1) | async-done | bytes 131104 | tf_op jit(solution)/shard_map/all_to_all | solution.py:391
  153.1 2.9 %shard_map.81 = (f32[1,128]{1,0:T(1,128)}, f32[32,1]{1,0:T(8,128)}) custom-call(s32[1]{0:T(128)} %bitcast.place, f32[32,8,128]{2,1,0:T(8,128)} %bitcast.151, f32[32,1]{1,0:T(8,128)} %copy.11.weights), custom_call_target="tpu_custom_call" | custom-call | tf_op jit(solution)/shard_map/pallas_call | solution.py:393
  156.0 1.3 slice_reduce_fusion.2
  (117 shorter events, 21.8 us)
Async XLA Ops:
  0.6 21.3 %copy-start.9 = (s32[4096]{0:T(1024)S(1)}, s32[4096]{0:T(1024)}, u32[]{:S(2)}) copy-start(s32[4096]{0:T(1024)} %param.8) | copy-start | bytes 49156
  1.8 9.4 %collective-permute-start.1 = (bf16[32,3584]{1,0:T(8,128)(2,1)S(1)}, bf16[32,3584]{1,0:T(8,128)(2,1)S(1)}, u32[]{:S(2)}, u32[]{:S(2)}) collective-permute-start(bf16[32,3584]{1,0:T(8,128)(2,1)S(1)} %pad_maximum_fusion.3), channel_id=1, source_target_pairs={{0,32},{1,225},{32,64},{33,1},{64,96},{65,33},{96,128},{97,65},{12... | collective-permute-start | bytes 688136 | tf_op jit(solution)/shard_map/ppermute | solution.py:38
  8.3 5.5 %collective-permute-start = (bf16[32,3584]{1,0:T(8,128)(2,1)S(1)}, bf16[32,3584]{1,0:T(8,128)(2,1)S(1)}, u32[]{:S(2)}, u32[]{:S(2)}) collective-permute-start(bf16[32,3584]{1,0:T(8,128)(2,1)S(1)} %pad_maximum_fusion.2), channel_id=1, source_target_pairs={{0,8},{1,25},{8,16},{9,1},{16,24},{17,9},{24,0},{25,17},{2,10},{3,... | collective-permute-start | bytes 688136 | tf_op jit(solution)/shard_map/ppermute | solution.py:38
  13.8 6.7 %collective-permute-start.3 = (bf16[32,3584]{1,0:T(8,128)(2,1)S(1)}, bf16[32,3584]{1,0:T(8,128)(2,1)S(1)}, u32[]{:S(2)}, u32[]{:S(2)}) collective-permute-start(bf16[32,3584]{1,0:T(8,128)(2,1)S(1)} %collective-permute-done.1), channel_id=1, source_target_pairs={{0,32},{1,225},{32,64},{33,1},{64,96},{65,33},{96,128},{97,65},{12... | collective-permute-start | bytes 688136 | tf_op jit(solution)/shard_map/ppermute | solution.py:38
  14.7 5.8 %collective-permute-start.2 = (bf16[16,3584]{1,0:T(8,128)(2,1)S(1)}, bf16[16,3584]{1,0:T(8,128)(2,1)S(1)}, u32[]{:S(2)}, u32[]{:S(2)}) collective-permute-start(bf16[16,3584]{1,0:T(8,128)(2,1)S(1)} %slice.247), channel_id=1, source_target_pairs={{0,8},{1,25},{8,16},{9,1},{16,24},{17,9},{24,0},{25,17},{2,10},{3,... | collective-permute-start | bytes 344072 | tf_op jit(solution)/shard_map/ppermute | solution.py:38
  17.7 33.1 %collective-permute-start.12 = (bf16[3584,384]{1,0:T(8,128)(2,1)}, bf16[3584,384]{1,0:T(8,128)(2,1)S(1)}, u32[]{:S(2)}, u32[]{:S(2)}) collective-permute-start(bf16[3584,384]{1,0:T(8,128)(2,1)} %refs_6_.1), channel_id=1, source_target_pairs={{0,2},{1,7},{2,4},{3,1},{4,6},{5,3},{6,0},{7,5},{8,10},{9,15},{10,... | collective-permute-start | bytes 8257544 | tf_op jit(solution)/shard_map/ppermute | solution.py:332
  21.8 29.0 %collective-permute-start.11 = (bf16[3584,384]{1,0:T(8,128)(2,1)}, bf16[3584,384]{1,0:T(8,128)(2,1)}, u32[]{:S(2)}, u32[]{:S(2)}) collective-permute-start(bf16[3584,384]{1,0:T(8,128)(2,1)} %refs_6_.1), channel_id=1, source_target_pairs={{0,1},{1,0},{2,3},{3,2},{4,5},{5,4},{6,7},{7,6},{8,9},{9,8},{10,11... | collective-permute-start | bytes 8257544 | tf_op jit(solution)/shard_map/ppermute | solution.py:24
  22.5 5.6 %collective-permute-start.10 = (bf16[32,3584]{1,0:T(8,128)(2,1)}, bf16[32,3584]{1,0:T(8,128)(2,1)S(1)}, u32[]{:S(2)}, u32[]{:S(2)}) collective-permute-start(bf16[32,3584]{1,0:T(8,128)(2,1)} %copy-done.6), channel_id=1, source_target_pairs={{0,32},{1,225},{32,64},{33,1},{64,96},{65,33},{96,128},{97,65},{12... | collective-permute-start | bytes 688136 | tf_op jit(solution)/shard_map/ppermute | solution.py:38
  26.3 13.8 %collective-permute-start.6 = (bf16[80,3584]{1,0:T(8,128)(2,1)}, bf16[80,3584]{1,0:T(8,128)(2,1)}, u32[]{:S(2)}, u32[]{:S(2)}) collective-permute-start(bf16[80,3584]{1,0:T(8,128)(2,1)} %pad_maximum_fusion.refs_1_), channel_id=1, source_target_pairs={{0,1},{1,0},{2,3},{3,2},{4,5},{5,4},{6,7},{7,6},{8,9},{9,8},{10,11... | collective-permute-start | bytes 1720328 | tf_op jit(solution)/shard_map/ppermute | solution.py:24
  27.3 4.0 %collective-permute-start.8 = (bf16[64,3584]{1,0:T(8,128)(2,1)}, bf16[64,3584]{1,0:T(8,128)(2,1)}, u32[]{:S(2)}, u32[]{:S(2)}) collective-permute-start(bf16[64,3584]{1,0:T(8,128)(2,1)} %pad_maximum_fusion.1.refs_0_), channel_id=1, source_target_pairs={{0,1},{1,0},{2,3},{3,2},{4,5},{5,4},{6,7},{7,6},{8,9},{9,8},{10,11... | collective-permute-start | bytes 1376264 | tf_op jit(solution)/shard_map/ppermute | solution.py:24
  28.2 30.5 %copy-start.3 = (bf16[32,3584]{1,0:T(8,128)(2,1)}, bf16[32,3584]{1,0:T(8,128)(2,1)S(1)}, u32[]{:S(2)}) copy-start(bf16[32,3584]{1,0:T(8,128)(2,1)S(1)} %collective-permute-done.10.refs_6_) | copy-start | bytes 688132
  28.2 9.3 %collective-permute-start.5 = (bf16[64,3584]{1,0:T(8,128)(2,1)}, bf16[64,3584]{1,0:T(8,128)(2,1)}, u32[]{:S(2)}, u32[]{:S(2)}) collective-permute-start(bf16[64,3584]{1,0:T(8,128)(2,1)} %pad_maximum_fusion.1.refs_0_), channel_id=1, source_target_pairs={{0,32},{1,225},{32,64},{33,1},{64,96},{65,33},{96,128},{97,65},{12... | collective-permute-start | bytes 1376264 | tf_op jit(solution)/shard_map/ppermute | solution.py:38
  31.3 12.0 %collective-permute-start.4 = (bf16[80,3584]{1,0:T(8,128)(2,1)}, bf16[80,3584]{1,0:T(8,128)(2,1)}, u32[]{:S(2)}, u32[]{:S(2)}) collective-permute-start(bf16[80,3584]{1,0:T(8,128)(2,1)} %pad_maximum_fusion.refs_1_), channel_id=1, source_target_pairs={{0,8},{1,25},{8,16},{9,1},{16,24},{17,9},{24,0},{25,17},{2,10},{3,... | collective-permute-start | bytes 1720328 | tf_op jit(solution)/shard_map/ppermute | solution.py:38
  37.5 8.4 %collective-permute-start.9 = (bf16[64,3584]{1,0:T(8,128)(2,1)}, bf16[64,3584]{1,0:T(8,128)(2,1)}, u32[]{:S(2)}, u32[]{:S(2)}) collective-permute-start(bf16[64,3584]{1,0:T(8,128)(2,1)} %collective-permute-done.8), channel_id=1, source_target_pairs={{0,32},{1,225},{32,64},{33,1},{64,96},{65,33},{96,128},{97,65},{12... | collective-permute-start | bytes 1376264 | tf_op jit(solution)/shard_map/ppermute | solution.py:38
  40.1 9.2 %collective-permute-start.7 = (bf16[80,3584]{1,0:T(8,128)(2,1)}, bf16[80,3584]{1,0:T(8,128)(2,1)}, u32[]{:S(2)}, u32[]{:S(2)}) collective-permute-start(bf16[80,3584]{1,0:T(8,128)(2,1)} %collective-permute-done.6), channel_id=1, source_target_pairs={{0,8},{1,25},{8,16},{9,1},{16,24},{17,9},{24,0},{25,17},{2,10},{3,... | collective-permute-start | bytes 1720328 | tf_op jit(solution)/shard_map/ppermute | solution.py:38
  50.8 24.6 %collective-permute-start.22 = (bf16[3584,384]{1,0:T(8,128)(2,1)S(1)}, bf16[3584,384]{1,0:T(8,128)(2,1)}, u32[]{:S(2)}, u32[]{:S(2)}) collective-permute-start(bf16[3584,384]{1,0:T(8,128)(2,1)S(1)} %collective-permute-done.12.refs_7_.refs_6_.refs_8_), channel_id=1, source_target_pairs={{0,1},{1,0},{2,3},{3,2},{4,5},{5,4},{6,7},{7,6},{8,9},{9,8},{10,11... | collective-permute-start | bytes 8257544 | tf_op jit(solution)/shard_map/ppermute | solution.py:24
  52.4 15.9 %collective-permute-start.15 = (bf16[80,3584]{1,0:T(8,128)(2,1)}, bf16[80,3584]{1,0:T(8,128)(2,1)S(1)}, u32[]{:S(2)}, u32[]{:S(2)}) collective-permute-start(bf16[80,3584]{1,0:T(8,128)(2,1)} %collective-permute-done.4.refs_4_), channel_id=1, source_target_pairs={{0,8},{1,25},{8,16},{9,1},{16,24},{17,9},{24,0},{25,17},{2,10},{3,... | collective-permute-start | bytes 1720328 | tf_op jit(solution)/shard_map/ppermute | solution.py:38
  53.6 14.7 %collective-permute-start.13 = (bf16[64,3584]{1,0:T(8,128)(2,1)}, bf16[64,3584]{1,0:T(8,128)(2,1)}, u32[]{:S(2)}, u32[]{:S(2)}) collective-permute-start(bf16[64,3584]{1,0:T(8,128)(2,1)} %collective-permute-done.5.refs_2_), channel_id=1, source_target_pairs={{0,32},{1,225},{32,64},{33,1},{64,96},{65,33},{96,128},{97,65},{12... | collective-permute-start | bytes 1376264 | tf_op jit(solution)/shard_map/ppermute | solution.py:38
  56.5 11.8 %collective-permute-start.14 = (bf16[64,3584]{1,0:T(8,128)(2,1)}, bf16[64,3584]{1,0:T(8,128)(2,1)}, u32[]{:S(2)}, u32[]{:S(2)}) collective-permute-start(bf16[64,3584]{1,0:T(8,128)(2,1)} %collective-permute-done.9.refs_3_), channel_id=1, source_target_pairs={{0,32},{1,225},{32,64},{33,1},{64,96},{65,33},{96,128},{97,65},{12... | collective-permute-start | bytes 1376264 | tf_op jit(solution)/shard_map/ppermute | solution.py:38
  57.3 11.0 %collective-permute-start.16 = (bf16[16,3584]{1,0:T(8,128)(2,1)S(1)}, bf16[16,3584]{1,0:T(8,128)(2,1)S(1)}, u32[]{:S(2)}, u32[]{:S(2)}) collective-permute-start(bf16[16,3584]{1,0:T(8,128)(2,1)S(1)} %slice.318), channel_id=1, source_target_pairs={{0,32},{1,225},{32,64},{33,1},{64,96},{65,33},{96,128},{97,65},{12... | collective-permute-start | bytes 344072 | tf_op jit(solution)/shard_map/ppermute | solution.py:38
  69.6 5.1 %collective-permute-start.20 = (bf16[48,3584]{1,0:T(8,128)(2,1)}, bf16[48,3584]{1,0:T(8,128)(2,1)}, u32[]{:S(2)}, u32[]{:S(2)}) collective-permute-start(bf16[48,3584]{1,0:T(8,128)(2,1)} %constant_dynamic-update-slice_fusion), channel_id=1, source_target_pairs={{0,1},{1,0},{2,3},{3,2},{4,5},{5,4},{6,7},{7,6},{8,9},{9,8},{10,11... | collective-permute-start | bytes 1032200 | tf_op jit(solution)/shard_map/ppermute | solution.py:24
  70.0 13.7 %collective-permute-start.17 = (bf16[64,3584]{1,0:T(8,128)(2,1)}, bf16[64,3584]{1,0:T(8,128)(2,1)}, u32[]{:S(2)}, u32[]{:S(2)}) collective-permute-start(bf16[64,3584]{1,0:T(8,128)(2,1)} %collective-permute-done.13.refs_0_), channel_id=1, source_target_pairs={{0,32},{1,225},{32,64},{33,1},{64,96},{65,33},{96,128},{97,65},{12... | collective-permute-start | bytes 1376264 | tf_op jit(solution)/shard_map/ppermute | solution.py:38
  72.8 10.9 %collective-permute-start.18 = (bf16[64,3584]{1,0:T(8,128)(2,1)}, bf16[64,3584]{1,0:T(8,128)(2,1)}, u32[]{:S(2)}, u32[]{:S(2)}) collective-permute-start(bf16[64,3584]{1,0:T(8,128)(2,1)} %collective-permute-done.14.refs_1_), channel_id=1, source_target_pairs={{0,32},{1,225},{32,64},{33,1},{64,96},{65,33},{96,128},{97,65},{12... | collective-permute-start | bytes 1376264 | tf_op jit(solution)/shard_map/ppermute | solution.py:38
  72.8 10.8 %collective-permute-start.19 = (bf16[48,3584]{1,0:T(8,128)(2,1)}, bf16[48,3584]{1,0:T(8,128)(2,1)}, u32[]{:S(2)}, u32[]{:S(2)}) collective-permute-start(bf16[48,3584]{1,0:T(8,128)(2,1)} %constant_dynamic-update-slice_fusion), channel_id=1, source_target_pairs={{0,8},{1,25},{8,16},{9,1},{16,24},{17,9},{24,0},{25,17},{2,10},{3,... | collective-permute-start | bytes 1032200 | tf_op jit(solution)/shard_map/ppermute | solution.py:38
  74.7 8.9 %collective-permute-start.21 = (bf16[48,3584]{1,0:T(8,128)(2,1)}, bf16[48,3584]{1,0:T(8,128)(2,1)}, u32[]{:S(2)}, u32[]{:S(2)}) collective-permute-start(bf16[48,3584]{1,0:T(8,128)(2,1)} %collective-permute-done.20), channel_id=1, source_target_pairs={{0,8},{1,25},{8,16},{9,1},{16,24},{17,9},{24,0},{25,17},{2,10},{3,... | collective-permute-start | bytes 1032200 | tf_op jit(solution)/shard_map/ppermute | solution.py:38
  83.6 15.5 %collective-permute-start.23 = (bf16[64,3584]{1,0:T(8,128)(2,1)}, bf16[64,3584]{1,0:T(8,128)(2,1)S(1)}, u32[]{:S(2)}, u32[]{:S(2)}) collective-permute-start(bf16[64,3584]{1,0:T(8,128)(2,1)} %collective-permute-done.17.refs_0_), channel_id=1, source_target_pairs={{0,32},{1,225},{32,64},{33,1},{64,96},{65,33},{96,128},{97,65},{12... | collective-permute-start | bytes 1376264 | tf_op jit(solution)/shard_map/ppermute | solution.py:38
  86.5 12.5 %collective-permute-start.24 = (bf16[48,3584]{1,0:T(8,128)(2,1)}, bf16[48,3584]{1,0:T(8,128)(2,1)S(1)}, u32[]{:S(2)}, u32[]{:S(2)}) collective-permute-start(bf16[48,3584]{1,0:T(8,128)(2,1)} %collective-permute-done.19.refs_2_), channel_id=1, source_target_pairs={{0,8},{1,25},{8,16},{9,1},{16,24},{17,9},{24,0},{25,17},{2,10},{3,... | collective-permute-start | bytes 1032200 | tf_op jit(solution)/shard_map/ppermute | solution.py:38
  99.0 31.1 %copy-start.12 = (s32[8]{0:T(128)S(1)}, s32[8]{0:T(128)}, u32[]{:S(2)}) copy-start(s32[8]{0:T(128)} %param.9) | copy-start | bytes 100
  99.1 31.1 %copy-start.13 = (s32[8]{0:T(128)S(1)}, s32[8]{0:T(128)}, u32[]{:S(2)}) copy-start(s32[8]{0:T(128)} %param.10) | copy-start | bytes 100
  99.1 40.4 %copy-start.14 = (f32[22]{0:T(128)S(1)}, f32[22]{0:T(128)}, u32[]{:S(2)}) copy-start(f32[22]{0:T(128)} %param.11) | copy-start | bytes 268
  127.5 3.4 %collective-permute-start.25 = (f32[128]{0:T(128)S(1)}, f32[128]{0:T(128)S(1)}, u32[]{:S(2)}, u32[]{:S(2)}) collective-permute-start(f32[128]{0:T(128)S(1)} %pad_maximum_fusion.4), channel_id=1, source_target_pairs={{0,1},{1,0},{2,3},{3,2},{4,5},{5,4},{6,7},{7,6},{8,9},{9,8},{10,11... | collective-permute-start | bytes 1544 | tf_op jit(solution)/shard_map/ppermute | solution.py:24
  133.3 19.1 %all-to-all-start.1 = ((f32[256,1,128]{2,1,0:T(1,128)}), f32[256,1,128]{2,1,0:T(1,128)S(1)}, u32[]{:S(2)}, u32[]{:S(2)}) async-start(f32[256,1,128]{2,1,0:T(1,128)} %broadcast_in_dim.2), calls=%async_computation.1 | async-start | bytes 262144 | tf_op jit(solution)/shard_map/all_to_all | solution.py:391
  (10 other events, 49.6 us)

commit v3 on v2

--- a/solution.py
+++ b/solution.py
@@ -16,7 +16,6 @@
 DP = ("z", "x")
 VOCAB_AXES = ("yh", "yl", "c")
 SUB = 16
-VMEM_LIMIT = 60 * 2**20
 
 
 def shift(a, axis, by):
@@ -188,7 +187,7 @@
             pltpu.SemaphoreType.DMA((len(listed),)),
             pltpu.SemaphoreType.DMA((len(flat),)),
         ],
-        compiler_params=pltpu.CompilerParams(vmem_limit_bytes=VMEM_LIMIT),
+        compiler_params=pltpu.CompilerParams(vmem_limit_bytes=60 * 2**20),
         cost_estimate=pl.CostEstimate(
             flops=2 * total * depth * n_cols,
             bytes_accessed=2 * depth * (total + n_cols),
@@ -226,14 +225,15 @@
         count_d = jnp.sum(jnp.where(inside, count, 0.0), axis=0)
         sum_vm[d : d + 1, :] = jnp.sum(sum_d, axis=0, keepdims=True)
         count_vm[d : d + 1, :] = jnp.sum(count_d, axis=0, keepdims=True)
-    domain_loss = jnp.sum(sum_vm[...], axis=1, keepdims=True)
-    domain_count = jnp.sum(count_vm[...], axis=1, keepdims=True)
+    domain_loss = jnp.sum(sum_vm[...].T, axis=0, keepdims=True)
+    domain_count = jnp.sum(count_vm[...].T, axis=0, keepdims=True)
     w = weights[...]
-    probability = (1.0 - DOMAINS * explore_share) * w / jnp.sum(w, axis=0, keepdims=True)
+    probability = (1.0 - DOMAINS * explore_share) * w / jnp.sum(w, axis=1, keepdims=True)
     probability = probability + explore_share
     reward = domain_loss / jnp.maximum(domain_count, 1.0) / probability
     raised = w * jnp.exp(step_rate * reward)
-    weights_out[...] = DOMAINS * raised / jnp.sum(raised, axis=0, keepdims=True)
+    scaled = DOMAINS * raised / jnp.sum(raised, axis=1, keepdims=True)
+    weights_out[...] = scaled[:, :DOMAINS]
     mine = loss_vm[place[0]]
     for row in range(4):
         for part in range(2):
@@ -304,19 +304,15 @@
     mine_1 = [
         subs_a,
         subs_b1,
-        moved(subs_a, -1, 0),
+        moved(subs_a, -1, 0) + subs_b2[:2],
         moved(mates(subs_a), -1, 0),
         moved(subs_b1, 0, -1),
         moved(mates(subs_b1), 0, -1),
-        subs_b2[:2],
     ]
-    mine_3 = [
-        moved(subs_a, -2, 0),
+    mine_4 = [
+        moved(subs_a, -2, 0) + subs_b2[2:],
         moved(mates(subs_a), -2, 0),
         moved(subs_b1, 0, -2),
-        subs_b2[2:],
-    ]
-    mine_4 = [
         moved(subs_a, -3, 0),
         moved(mates(subs_a), -3, 0),
         moved(subs_b2, 0, -1),
@@ -324,57 +320,56 @@
         moved(subs_a, -4, 0),
         moved(subs_b2, 0, -2),
     ]
-    subs_1, subs_3, subs_4 = (sum(m, []) for m in (mine_1, mine_3, mine_4))
+    subs_1, subs_4 = sum(mine_1, []), sum(mine_4, [])
 
     def pieces_of(arrays, subs):
-        return [(a, 0, a.shape[0], s) for a, s in zip(arrays, subs)]
+        return [(a, 0, len(s) * SUB, s) for a, s in zip(arrays, subs)]
 
     col_in = lax.ppermute(head_weight, VOCAB_AXES, moves)
     own_a = jnp.concatenate([rows_of(0, c), rows_of(0, 1 - c)], axis=0)
     own_b = jnp.concatenate([rows_of(1, c), rows_of(1, 1 - c)], axis=0)
     xa1, zb1 = onward(own_a, "x"), onward(own_b, "z")
-    xa1, zb1 = together(xa1, zb1)
+    col_mate = shift(head_weight, "c", 1)
+    xa1, zb1, col_mate = together(xa1, zb1, col_mate)
     xa2, zb2 = onward(xa1[:SUB], "x"), onward(zb1, "z")
-    xa2, zb2, late_w = together(xa2, zb2, head_weight)
+    xa2, zb2 = together(xa2, zb2)
     mine_a = jnp.concatenate([own_a[:SUB], xa1, xa2], axis=0)
     mine_b1 = jnp.concatenate([own_b[:SUB], zb1, zb2], axis=0)
-    xb1, za1 = onward(mine_b1, "x"), onward(mine_a, "z")
+    riding = jnp.concatenate([own_a[:SUB], xa1, xa2, zb2], axis=0)
+    xb1, za1 = onward(mine_b1, "x"), onward(riding, "z")
     mate_b1, mate_a = shift(mine_b1, "c", 1), shift(mine_a, "c", 1)
-    wanted = [wanted_of(targets, subs) for subs in (subs_1, subs_3, subs_4)]
-    xb1_mate, za1_mate, zb3 = onward(mate_b1, "x"), onward(mate_a, "z"), onward(zb2, "z")
-    col_mate = shift(late_w, "c", 1)
-    xb1, za1, xb1_mate, za1_mate, zb3, col_mate, col_in, *wanted = together(
-        xb1, za1, xb1_mate, za1_mate, zb3, col_mate, col_in, *wanted
+    wanted = [wanted_of(targets, subs) for subs in (subs_1, subs_4)]
+    xb1_mate, za1_mate = onward(mate_b1, "x"), onward(mate_a, "z")
+    xb1, za1, xb1_mate, za1_mate, col_in, *wanted = together(
+        xb1, za1, xb1_mate, za1_mate, col_in, *wanted
     )
     za2, za2_mate = onward(za1, "z"), onward(za1_mate, "z")
-    xb2, zb4 = onward(xb1, "x"), onward(zb3[:SUB], "z")
-
-    pieces = pieces_of([mine_a, mine_b1, za1, za1_mate, xb1, xb1_mate, zb3], mine_1)
+    xb2 = onward(xb1, "x")
+
+    pieces = pieces_of([mine_a, mine_b1, za1, za1_mate, xb1, xb1_mate], mine_1)
     near_cols = [[head_weight], [col_mate]]
     _, stats_1 = tile_stats(pieces, wanted[0], near_cols, scalars(*own_starts))
-    za2, za2_mate, xb2, zb4, stats_1 = together(za2, za2_mate, xb2, zb4, stats_1)
-    za3, za3_mate = onward(za2, "z"), onward(za2_mate, "z")
-    mine_b2 = jnp.concatenate([zb3, zb4], axis=0)
+    za2, za2_mate, xb2, stats_1 = together(za2, za2_mate, xb2, stats_1)
+    za3, za3_mate = onward(za2[: 4 * SUB], "z"), onward(za2_mate, "z")
+    mine_b2 = jnp.concatenate([za1[4 * SUB :], za2[4 * SUB : 5 * SUB]], axis=0)
     mate_b2 = shift(mine_b2, "c", 1)
     xb3, xb3_mate = onward(mine_b2, "x"), onward(mate_b2, "x")
     col_in_mate = shift(col_in, "c", 1)
     far_cols = [[col_in], [col_in_mate]]
     done_1 = tile_stats(pieces, wanted[0], far_cols, scalars(*in_starts), prev=stats_1)
     stats_2 = done_1[1]
-    za3, za3_mate, xb3, xb3_mate, stats_2 = together(za3, za3_mate, xb3, xb3_mate, stats_2)
+    za3, xb3, stats_2 = together(za3, xb3, stats_2)
     za4, xb4 = onward(za3, "z"), onward(xb3, "x")
     cols = near_cols + far_cols
-    pieces = pieces_of([za2, za2_mate, xb2, zb4], mine_3)
-    done_2 = tile_stats(pieces, wanted[1], cols, scalars(*own_starts, *in_starts))
-    stats_3 = done_2[1]
-    za4, xb4, stats_3 = together(za4, xb4, stats_3)
-    pieces = pieces_of([za3, za3_mate, xb3, xb3_mate, za4, xb4], mine_4)
+    pieces = pieces_of(
+        [za2, za2_mate, xb2, za3, za3_mate, xb3, xb3_mate, za4, xb4], mine_4
+    )
     _, every = tile_stats(
         pieces,
-        wanted[2],
+        wanted[1],
         cols,
         scalars(*own_starts, *in_starts, z, x, sign),
-        others=[(done_1[0], stats_2), (done_2[0], stats_3)],
+        others=[(done_1[0], stats_2)],
     )
     share = 4 * SUB
     mine = lax.all_to_all(every, DP, 0, 0, tiled=True)
@@ -389,12 +384,12 @@
     note = jnp.pad(note, (0, 128 - note.shape[0]))
     sent = jnp.broadcast_to(note[None], (lax.axis_size(ALL), 128))
     notes = lax.all_to_all(sent, ALL, 0, 0, tiled=True)
-    weights = jnp.pad(domain_weights, (0, 32 - DOMAINS)).reshape(32, 1)
+    weights = jnp.pad(domain_weights, (0, 128 - DOMAINS)).reshape(1, 128)
     token_loss, new_weights = pl.pallas_call(
         finish_kernel,
         out_shape=(
             jax.ShapeDtypeStruct((1, 128), jnp.float32),
-            jax.ShapeDtypeStruct((32, 1), jnp.float32),
+            jax.ShapeDtypeStruct((1, DOMAINS), jnp.float32),
         ),
         in_specs=[
             pl.BlockSpec(memory_space=pltpu.SMEM),
@@ -407,11 +402,11 @@
         ),
         scratch_shapes=[
             pltpu.VMEM((dp_count, 8, 128), jnp.float32),
-            pltpu.VMEM((32, 128), jnp.float32),
-            pltpu.VMEM((32, 128), jnp.float32),
+            pltpu.VMEM((128, 128), jnp.float32),
+            pltpu.VMEM((128, 128), jnp.float32),
         ],
     )(dp_index.reshape(1), notes.reshape(dp_count, 8, 128), weights)
-    return (token_loss.reshape(-1), new_weights[:DOMAINS, 0])
+    return (token_loss.reshape(-1), new_weights.reshape(-1))
 
 
 def solution(mesh):

time: 158 us -> 144 us (0.911)
  starting transfers between devices: 51.1 us -> 43.3 us
  waiting for transfers between devices: 30.3 us -> 37.2 us
  Pallas kernels: 40.4 us -> 34.9 us
  local copies, waits for them, and re-layouts: 13.5 us -> 8.09 us
  other arithmetic: 5.98 us -> 2.71 us
  blocking collectives: 15 us -> 16.8 us
    ppermute x19 -> x17, starting transfers between devices: 37.7 us -> 30.4 us  [onward(): return lax.ppermute(a, (axis, 'c'), moves)]
    pallas_call x4 -> x3, Pallas kernels: 37.4 us -> 31.9 us  [tile_stats(): pl.pallas_call(functools.partial(stats_kernel, tuple(listed), tuple((len(...]
    ppermute x1, waiting for transfers between devices: 1.51 us -> 4.97 us  [body(): col_in = lax.ppermute(head_weight, VOCAB_AXES, moves)]
    ppermute x19 -> x17, waiting for transfers between devices: 15.9 us -> 19.1 us  [onward(): return lax.ppermute(a, (axis, 'c'), moves)]
    unnamed x31 -> x32, local copies, waits for them, and re-layouts: 4.91 us -> 2.2 us
    ppermute x6, starting transfers between devices: 4.56 us -> 6.62 us  [shift(): return lax.ppermute(a, axis, [(i, (i + by) % n) for i in range(n)])]
    concatenate x1, other arithmetic: 1.96 us -> 0.05 us  [body(): mine_b1 = jnp.concatenate([own_b[:SUB], zb1, zb2], axis=0)]
    all_to_all x1, blocking collectives: 15 us -> 16.8 us  [body(): mine = lax.all_to_all(every, DP, 0, 0, tiled=True)]
  transfers between devices with their start and end apart: 27 -> 25, of which waited for: 10 -> 10; matrix products, arithmetic and copies ran while one was open for 7% -> 4% of each run, Pallas kernels for 16% -> 11%
where the time goes in v3:
time: 144 us
  starting transfers between devices  43.3 us (30%)
  waiting for transfers between devices  37.2 us (26%)
  Pallas kernels  34.9 us (24%)
  blocking collectives  16.8 us (12%)
  local copies, waits for them, and re-layouts  8.09 us (6%)
  other arithmetic  2.71 us (2%)
    pallas_call x3, Pallas kernels, tile_stats(): pl.pallas_call(functools.partial(stats_kernel, tuple(listed), tuple((len(...  31.9 us
    ppermute x17, starting transfers between devices, onward(): return lax.ppermute(a, (axis, 'c'), moves)  30.4 us
    ppermute x17, waiting for transfers between devices, onward(): return lax.ppermute(a, (axis, 'c'), moves)  19.1 us
    all_to_all x1, blocking collectives, body(): mine = lax.all_to_all(every, DP, 0, 0, tiled=True)  16.8 us
    all_to_all x1, waiting for transfers between devices, body(): notes = lax.all_to_all(sent, ALL, 0, 0, tiled=True)  12.5 us
    ppermute x6, starting transfers between devices, shift(): return lax.ppermute(a, axis, [(i, (i + by) % n) for i in range(n)])  6.62 us
    all_to_all x1, starting transfers between devices, body(): notes = lax.all_to_all(sent, ALL, 0, 0, tiled=True)  5.25 us
    ppermute x1, waiting for transfers between devices, body(): col_in = lax.ppermute(head_weight, VOCAB_AXES, moves)  4.97 us
  transfers between devices with their start and end apart: 25, of which 10 were waited for; matrix products, arithmetic and copies ran while one was open for 4% of the time, Pallas kernels for 11%

profile of v3, /device:TPU:1, one launch (start us, length us, event | category | flops | bytes accessed | tf_op | source)
XLA Modules:
  0.0 144.1 jit_solution(7162350379944912312)
XLA Ops:
  0.6 3.3 %collective-permute-start.2 = (bf16[3584,384]{1,0:T(8,128)(2,1)}, bf16[3584,384]{1,0:T(8,128)(2,1)}, u32[]{:S(2)}, u32[]{:S(2)}) collective-permute-start(bf16[3584,384]{1,0:T(8,128)(2,1)} %refs_9_.1), channel_id=1, source_target_pairs={{0,1},{1,0},{2,3},{3,2},{4,5},{5,4},{6,7},{7,6},{8,9},{9,8},{10,11... | collective-permute-start | bytes 8257544 | tf_op jit(solution)/shard_map/ppermute | solution.py:23
  4.0 1.0 collective-permute-start.11
  5.0 1.1 constant_dynamic-slice_fusion.3
  6.1 5.7 %collective-permute-start.1 = (bf16[32,3584]{1,0:T(8,128)(2,1)S(1)}, bf16[32,3584]{1,0:T(8,128)(2,1)S(1)}, u32[]{:S(2)}, u32[]{:S(2)}) collective-permute-start(bf16[32,3584]{1,0:T(8,128)(2,1)S(1)} %pad_maximum_fusion.5), channel_id=1, source_target_pairs={{0,32},{1,225},{32,64},{33,1},{64,96},{65,33},{96,128},{97,65},{12... | collective-permute-start | bytes 688136 | tf_op jit(solution)/shard_map/ppermute | solution.py:37
  11.8 2.6 %collective-permute-start = (bf16[32,3584]{1,0:T(8,128)(2,1)S(1)}, bf16[32,3584]{1,0:T(8,128)(2,1)S(1)}, u32[]{:S(2)}, u32[]{:S(2)}) collective-permute-start(bf16[32,3584]{1,0:T(8,128)(2,1)S(1)} %pad_maximum_fusion.4), channel_id=1, source_target_pairs={{0,8},{1,25},{8,16},{9,1},{16,24},{17,9},{24,0},{25,17},{2,10},{3,... | collective-permute-start | bytes 688136 | tf_op jit(solution)/shard_map/ppermute | solution.py:37
  14.9 2.4 %collective-permute-done = bf16[32,3584]{1,0:T(8,128)(2,1)S(1)} collective-permute-done((bf16[32,3584]{1,0:T(8,128)(2,1)S(1)}, bf16[32,3584]{1,0:T(8,128)(2,1)S(1)}, u32[]{:S(2)}, u32[]{:S(2)}) %collective-permute-start) | collective-permute-done | bytes 229408 | tf_op jit(solution)/shard_map/ppermute | solution.py:37
  17.3 0.9 collective-permute-start.4
  18.4 3.4 %collective-permute-start.3 = (bf16[16,3584]{1,0:T(8,128)(2,1)S(1)}, bf16[16,3584]{1,0:T(8,128)(2,1)S(1)}, u32[]{:S(2)}, u32[]{:S(2)}) collective-permute-start(bf16[16,3584]{1,0:T(8,128)(2,1)S(1)} %slice.250), channel_id=1, source_target_pairs={{0,8},{1,25},{8,16},{9,1},{16,24},{17,9},{24,0},{25,17},{2,10},{3,... | collective-permute-start | bytes 344072 | tf_op jit(solution)/shard_map/ppermute | solution.py:37
  21.9 1.7 %collective-permute-done.3 = bf16[16,3584]{1,0:T(8,128)(2,1)S(1)} collective-permute-done((bf16[16,3584]{1,0:T(8,128)(2,1)S(1)}, bf16[16,3584]{1,0:T(8,128)(2,1)S(1)}, u32[]{:S(2)}, u32[]{:S(2)}) %collective-permute-start.3) | collective-permute-done | bytes 114720 | tf_op jit(solution)/shard_map/ppermute | solution.py:37
  24.5 1.2 collective-permute-start.6
  25.6 3.4 %collective-permute-start.5 = (bf16[80,3584]{1,0:T(8,128)(2,1)S(1)}, bf16[80,3584]{1,0:T(8,128)(2,1)S(1)}, u32[]{:S(2)}, u32[]{:S(2)}) collective-permute-start(bf16[80,3584]{1,0:T(8,128)(2,1)S(1)} %pad_maximum_fusion.1.refs_1_), channel_id=1, source_target_pairs={{0,8},{1,25},{8,16},{9,1},{16,24},{17,9},{24,0},{25,17},{2,10},{3,... | collective-permute-start | bytes 1720328 | tf_op jit(solution)/shard_map/ppermute | solution.py:37
  31.5 5.0 %collective-permute-done.11.refs_6_.refs_11_ = bf16[3584,384]{1,0:T(8,128)(2,1)} collective-permute-done((bf16[3584,384]{1,0:T(8,128)(2,1)}, bf16[3584,384]{1,0:T(8,128)(2,1)}, u32[]{:S(2)}, u32[]{:S(2)}) %collective-permute-start.11) | collective-permute-done | bytes 2752544 | tf_op jit(solution)/shard_map/ppermute | solution.py:328
  36.5 3.1 %collective-permute-done.10.refs_3_ = bf16[64,3584]{1,0:T(8,128)(2,1)} collective-permute-done((bf16[64,3584]{1,0:T(8,128)(2,1)}, bf16[64,3584]{1,0:T(8,128)(2,1)}, u32[]{:S(2)}, u32[]{:S(2)}) %collective-permute-start.10) | collective-permute-done | bytes 458784 | tf_op jit(solution)/shard_map/ppermute | solution.py:37
  39.6 2.3 %collective-permute-done.8.refs_5_ = bf16[80,3584]{1,0:T(8,128)(2,1)} collective-permute-done((bf16[80,3584]{1,0:T(8,128)(2,1)}, bf16[80,3584]{1,0:T(8,128)(2,1)}, u32[]{:S(2)}, u32[]{:S(2)}) %collective-permute-start.8) | collective-permute-done | bytes 573472 | tf_op jit(solution)/shard_map/ppermute | solution.py:37
  41.9 1.4 collective-permute-start.17
  43.3 1.9 %collective-permute-start.12 = (bf16[96,3584]{1,0:T(8,128)(2,1)S(1)}, bf16[96,3584]{1,0:T(8,128)(2,1)S(1)}, u32[]{:S(2)}, u32[]{:S(2)}) collective-permute-start(bf16[96,3584]{1,0:T(8,128)(2,1)S(1)} %collective-permute-done.6.refs_2_), channel_id=1, source_target_pairs={{0,32},{1,225},{32,64},{33,1},{64,96},{65,33},{96,128},{97,65},{12... | collective-permute-start | bytes 2064392 | tf_op jit(solution)/shard_map/ppermute | solution.py:37
  45.3 1.7 %collective-permute-start.14 = (bf16[80,3584]{1,0:T(8,128)(2,1)S(1)}, bf16[80,3584]{1,0:T(8,128)(2,1)}, u32[]{:S(2)}, u32[]{:S(2)}) collective-permute-start(bf16[80,3584]{1,0:T(8,128)(2,1)S(1)} %collective-permute-done.5.refs_4_), channel_id=1, source_target_pairs={{0,8},{1,25},{8,16},{9,1},{16,24},{17,9},{24,0},{25,17},{2,10},{3,... | collective-permute-start | bytes 1720328 | tf_op jit(solution)/shard_map/ppermute | solution.py:37
  47.7 8.1 %shard_map.77.refs_8_ = f32[2,512]{1,0:T(2,128)} custom-call(s32[2]{0:T(128)} %pad_add_fusion.3.starts, s32[1,512]{1,0:T(1,128)} %bitcast.158, bf16[64,3584]{1,0:T(8,128)(2,1)} %copy-done.3, bf16[80,3584]{1,0:T(8,128)(2,1)} %copy-done, bf16[96,3584]{1,0:T(8,128)(2,1)} %copy-done.4, bf16[64,3584]{1,0:T(8,128)(2,1)} %collective-permute-done.10.refs_3_, ...), custom_call_target="tpu_custom_call" | custom-call | flops 2554331136 | bytes 8830976 | tf_op jit(solution)/shard_map/pallas_call | solution.py:173
  55.9 3.3 %collective-permute-done.13.refs_1_ = bf16[64,3584]{1,0:T(8,128)(2,1)} collective-permute-done((bf16[64,3584]{1,0:T(8,128)(2,1)}, bf16[64,3584]{1,0:T(8,128)(2,1)}, u32[]{:S(2)}, u32[]{:S(2)}) %collective-permute-start.13) | collective-permute-done | bytes 458784 | tf_op jit(solution)/shard_map/ppermute | solution.py:37
  59.2 2.2 %collective-permute-start.15 = (bf16[64,3584]{1,0:T(8,128)(2,1)S(1)}, bf16[64,3584]{1,0:T(8,128)(2,1)S(1)}, u32[]{:S(2)}, u32[]{:S(2)}) collective-permute-start(bf16[64,3584]{1,0:T(8,128)(2,1)S(1)} %slice.321), channel_id=1, source_target_pairs={{0,32},{1,225},{32,64},{33,1},{64,96},{65,33},{96,128},{97,65},{12... | collective-permute-start | bytes 1376264 | tf_op jit(solution)/shard_map/ppermute | solution.py:37
  61.5 1.8 %collective-permute-start.16 = (bf16[48,3584]{1,0:T(8,128)(2,1)S(1)}, bf16[48,3584]{1,0:T(8,128)(2,1)S(1)}, u32[]{:S(2)}, u32[]{:S(2)}) collective-permute-start(bf16[48,3584]{1,0:T(8,128)(2,1)S(1)} %pad_maximum_fusion.3), channel_id=1, source_target_pairs={{0,8},{1,25},{8,16},{9,1},{16,24},{17,9},{24,0},{25,17},{2,10},{3,... | collective-permute-start | bytes 1032200 | tf_op jit(solution)/shard_map/ppermute | solution.py:37
  64.3 8.1 %shard_map.78.refs_13_ = f32[2,512]{1,0:T(2,128)} custom-call(s32[2]{0:T(128)} %pad_add_fusion.4.starts, s32[1,512]{1,0:T(1,128)} %bitcast.159, bf16[64,3584]{1,0:T(8,128)(2,1)} %copy-done.3, bf16[80,3584]{1,0:T(8,128)(2,1)} %copy-done, bf16[96,3584]{1,0:T(8,128)(2,1)} %copy-done.4, bf16[64,3584]{1,0:T(8,128)(2,1)} %collective-permute-done.10.refs_3_, ...), custom_call_target="tpu_custom_call" | custom-call | flops 2554331136 | bytes 8830976 | tf_op jit(solution)/shard_map/pallas_call | solution.py:173
  72.6 3.0 %collective-permute-start.20 = (bf16[48,3584]{1,0:T(8,128)(2,1)S(1)}, bf16[48,3584]{1,0:T(8,128)(2,1)S(1)}, u32[]{:S(2)}, u32[]{:S(2)}) collective-permute-start(bf16[48,3584]{1,0:T(8,128)(2,1)S(1)} %collective-permute-done.19), channel_id=1, source_target_pairs={{0,8},{1,25},{8,16},{9,1},{16,24},{17,9},{24,0},{25,17},{2,10},{3,... | collective-permute-start | bytes 1032200 | tf_op jit(solution)/shard_map/ppermute | solution.py:37
  75.6 1.0 collective-permute-start.22
  77.2 2.6 %collective-permute-done.20.refs_6_ = bf16[48,3584]{1,0:T(8,128)(2,1)S(1)} collective-permute-done((bf16[48,3584]{1,0:T(8,128)(2,1)S(1)}, bf16[48,3584]{1,0:T(8,128)(2,1)S(1)}, u32[]{:S(2)}, u32[]{:S(2)}) %collective-permute-start.20) | collective-permute-done | bytes 344096 | tf_op jit(solution)/shard_map/ppermute | solution.py:37
  79.8 3.7 %collective-permute-done.22.refs_8_ = bf16[48,3584]{1,0:T(8,128)(2,1)S(1)} collective-permute-done((bf16[48,3584]{1,0:T(8,128)(2,1)S(1)}, bf16[48,3584]{1,0:T(8,128)(2,1)S(1)}, u32[]{:S(2)}, u32[]{:S(2)}) %collective-permute-start.22) | collective-permute-done | bytes 344096 | tf_op jit(solution)/shard_map/ppermute | solution.py:37
  85.0 15.6 %shard_map.79 = f32[32,128]{1,0:T(8,128)} custom-call(s32[7]{0:T(128)} %stack.44.starts, s32[1,640]{1,0:T(1,128)} %reshape.91.targets, bf16[96,3584]{1,0:T(8,128)(2,1)} %copy-done.2, bf16[64,3584]{1,0:T(8,128)(2,1)} %collective-permute-done.13.refs_1_, bf16[80,3584]{1,0:T(8,128)(2,1)} %collective-permute-done.14.refs_2_, bf16[64,3584]{1,0:T(8,128)(2,1)} %copy-done.7, ...), custom_call_target="tpu_custom_call" | custom-call | flops 6165626880 | bytes 15024128 | tf_op jit(solution)/shard_map/pallas_call | solution.py:173
  100.7 16.8 %all_to_all.18 = f32[32,1,128]{2,1,0:T(1,128)S(1)} all-to-all(f32[32,1,128]{2,1,0:T(1,128)} %bitcast.154), channel_id=1, replica_groups=mesh['z'=8,'x'=4,'yh'=2,'yl'=2,'c'=2] {'z','x'}, dimensions={0} | all-to-all | bytes 32768 | tf_op jit(solution)/shard_map/all_to_all | solution.py:375
  117.7 1.2 collective-permute-start.23
  122.1 5.2 %all-to-all-start.1 = ((f32[256,1,128]{2,1,0:T(1,128)}), f32[256,1,128]{2,1,0:T(1,128)S(1)}, u32[]{:S(2)}, u32[]{:S(2)}) async-start(f32[256,1,128]{2,1,0:T(1,128)} %broadcast_in_dim.2), calls=%async_computation.1 | async-start | bytes 262144 | tf_op jit(solution)/shard_map/all_to_all | solution.py:386
  127.9 12.5 %all-to-all-done.1 = f32[256,1,128]{2,1,0:T(1,128)S(1)} async-done(((f32[256,1,128]{2,1,0:T(1,128)}), f32[256,1,128]{2,1,0:T(1,128)S(1)}, u32[]{:S(2)}, u32[]{:S(2)}) %all-to-all-start.1) | async-done | bytes 131104 | tf_op jit(solution)/shard_map/all_to_all | solution.py:386
  141.1 3.0 %shard_map.80 = (f32[1,128]{1,0:T(1,128)}, f32[1,22]{1,0:T(1,128)}) custom-call(s32[1]{0:T(128)} %bitcast.place, f32[32,8,128]{2,1,0:T(8,128)} %bitcast.151, f32[1,128]{1,0:T(1,128)} %pad_bitcast_fusion.weights), custom_call_target="tpu_custom_call" | custom-call | tf_op jit(solution)/shard_map/pallas_call | solution.py:388
  (111 shorter events, 12.7 us)
Async XLA Ops:
  0.6 13.7 %copy-start.5 = (s32[4096]{0:T(1024)S(1)}, s32[4096]{0:T(1024)}, u32[]{:S(2)}) copy-start(s32[4096]{0:T(1024)} %param.8) | copy-start | bytes 49156
  0.6 16.6 %collective-permute-start.2 = (bf16[3584,384]{1,0:T(8,128)(2,1)}, bf16[3584,384]{1,0:T(8,128)(2,1)}, u32[]{:S(2)}, u32[]{:S(2)}) collective-permute-start(bf16[3584,384]{1,0:T(8,128)(2,1)} %refs_9_.1), channel_id=1, source_target_pairs={{0,1},{1,0},{2,3},{3,2},{4,5},{5,4},{6,7},{7,6},{8,9},{9,8},{10,11... | collective-permute-start | bytes 8257544 | tf_op jit(solution)/shard_map/ppermute | solution.py:23
  4.0 32.5 %collective-permute-start.11 = (bf16[3584,384]{1,0:T(8,128)(2,1)}, bf16[3584,384]{1,0:T(8,128)(2,1)}, u32[]{:S(2)}, u32[]{:S(2)}) collective-permute-start(bf16[3584,384]{1,0:T(8,128)(2,1)} %refs_9_.1), channel_id=1, source_target_pairs={{0,2},{1,7},{2,4},{3,1},{4,6},{5,3},{6,0},{7,5},{8,10},{9,15},{10,... | collective-permute-start | bytes 8257544 | tf_op jit(solution)/shard_map/ppermute | solution.py:328
  6.1 8.8 %collective-permute-start.1 = (bf16[32,3584]{1,0:T(8,128)(2,1)S(1)}, bf16[32,3584]{1,0:T(8,128)(2,1)S(1)}, u32[]{:S(2)}, u32[]{:S(2)}) collective-permute-start(bf16[32,3584]{1,0:T(8,128)(2,1)S(1)} %pad_maximum_fusion.5), channel_id=1, source_target_pairs={{0,32},{1,225},{32,64},{33,1},{64,96},{65,33},{96,128},{97,65},{12... | collective-permute-start | bytes 688136 | tf_op jit(solution)/shard_map/ppermute | solution.py:37
  11.8 5.5 %collective-permute-start = (bf16[32,3584]{1,0:T(8,128)(2,1)S(1)}, bf16[32,3584]{1,0:T(8,128)(2,1)S(1)}, u32[]{:S(2)}, u32[]{:S(2)}) collective-permute-start(bf16[32,3584]{1,0:T(8,128)(2,1)S(1)} %pad_maximum_fusion.4), channel_id=1, source_target_pairs={{0,8},{1,25},{8,16},{9,1},{16,24},{17,9},{24,0},{25,17},{2,10},{3,... | collective-permute-start | bytes 688136 | tf_op jit(solution)/shard_map/ppermute | solution.py:37
  17.3 6.3 %collective-permute-start.4 = (bf16[32,3584]{1,0:T(8,128)(2,1)S(1)}, bf16[32,3584]{1,0:T(8,128)(2,1)S(1)}, u32[]{:S(2)}, u32[]{:S(2)}) collective-permute-start(bf16[32,3584]{1,0:T(8,128)(2,1)S(1)} %collective-permute-done.1), channel_id=1, source_target_pairs={{0,32},{1,225},{32,64},{33,1},{64,96},{65,33},{96,128},{97,65},{12... | collective-permute-start | bytes 688136 | tf_op jit(solution)/shard_map/ppermute | solution.py:37
  18.4 5.2 %collective-permute-start.3 = (bf16[16,3584]{1,0:T(8,128)(2,1)S(1)}, bf16[16,3584]{1,0:T(8,128)(2,1)S(1)}, u32[]{:S(2)}, u32[]{:S(2)}) collective-permute-start(bf16[16,3584]{1,0:T(8,128)(2,1)S(1)} %slice.250), channel_id=1, source_target_pairs={{0,8},{1,25},{8,16},{9,1},{16,24},{17,9},{24,0},{25,17},{2,10},{3,... | collective-permute-start | bytes 344072 | tf_op jit(solution)/shard_map/ppermute | solution.py:37
  23.7 5.4 %collective-permute-start.9 = (bf16[64,3584]{1,0:T(8,128)(2,1)S(1)}, bf16[64,3584]{1,0:T(8,128)(2,1)}, u32[]{:S(2)}, u32[]{:S(2)}) collective-permute-start(bf16[64,3584]{1,0:T(8,128)(2,1)S(1)} %pad_maximum_fusion.2.refs_0_), channel_id=1, source_target_pairs={{0,1},{1,0},{2,3},{3,2},{4,5},{5,4},{6,7},{7,6},{8,9},{9,8},{10,11... | collective-permute-start | bytes 1376264 | tf_op jit(solution)/shard_map/ppermute | solution.py:23
  23.8 23.9 %copy-start = (bf16[80,3584]{1,0:T(8,128)(2,1)}, bf16[80,3584]{1,0:T(8,128)(2,1)S(1)}, u32[]{:S(2)}) copy-start(bf16[80,3584]{1,0:T(8,128)(2,1)S(1)} %pad_maximum_fusion.1.refs_1_) | copy-start | bytes 1720324
  23.8 5.7 %collective-permute-start.7 = (bf16[80,3584]{1,0:T(8,128)(2,1)S(1)}, bf16[80,3584]{1,0:T(8,128)(2,1)}, u32[]{:S(2)}, u32[]{:S(2)}) collective-permute-start(bf16[80,3584]{1,0:T(8,128)(2,1)S(1)} %pad_maximum_fusion.1.refs_1_), channel_id=1, source_target_pairs={{0,1},{1,0},{2,3},{3,2},{4,5},{5,4},{6,7},{7,6},{8,9},{9,8},{10,11... | collective-permute-start | bytes 1720328 | tf_op jit(solution)/shard_map/ppermute | solution.py:23
  24.5 12.0 %collective-permute-start.6 = (bf16[96,3584]{1,0:T(8,128)(2,1)S(1)}, bf16[96,3584]{1,0:T(8,128)(2,1)S(1)}, u32[]{:S(2)}, u32[]{:S(2)}) collective-permute-start(bf16[96,3584]{1,0:T(8,128)(2,1)S(1)} %pad_maximum_fusion), channel_id=1, source_target_pairs={{0,32},{1,225},{32,64},{33,1},{64,96},{65,33},{96,128},{97,65},{12... | collective-permute-start | bytes 2064392 | tf_op jit(solution)/shard_map/ppermute | solution.py:37
  25.6 10.8 %collective-permute-start.5 = (bf16[80,3584]{1,0:T(8,128)(2,1)S(1)}, bf16[80,3584]{1,0:T(8,128)(2,1)S(1)}, u32[]{:S(2)}, u32[]{:S(2)}) collective-permute-start(bf16[80,3584]{1,0:T(8,128)(2,1)S(1)} %pad_maximum_fusion.1.refs_1_), channel_id=1, source_target_pairs={{0,8},{1,25},{8,16},{9,1},{16,24},{17,9},{24,0},{25,17},{2,10},{3,... | collective-permute-start | bytes 1720328 | tf_op jit(solution)/shard_map/ppermute | solution.py:37
  29.0 10.6 %collective-permute-start.10 = (bf16[64,3584]{1,0:T(8,128)(2,1)}, bf16[64,3584]{1,0:T(8,128)(2,1)}, u32[]{:S(2)}, u32[]{:S(2)}) collective-permute-start(bf16[64,3584]{1,0:T(8,128)(2,1)} %collective-permute-done.9), channel_id=1, source_target_pairs={{0,32},{1,225},{32,64},{33,1},{64,96},{65,33},{96,128},{97,65},{12... | collective-permute-start | bytes 1376264 | tf_op jit(solution)/shard_map/ppermute | solution.py:37
  29.5 12.4 %collective-permute-start.8 = (bf16[80,3584]{1,0:T(8,128)(2,1)}, bf16[80,3584]{1,0:T(8,128)(2,1)}, u32[]{:S(2)}, u32[]{:S(2)}) collective-permute-start(bf16[80,3584]{1,0:T(8,128)(2,1)} %collective-permute-done.7), channel_id=1, source_target_pairs={{0,8},{1,25},{8,16},{9,1},{16,24},{17,9},{24,0},{25,17},{2,10},{3,... | collective-permute-start | bytes 1720328 | tf_op jit(solution)/shard_map/ppermute | solution.py:37
  36.5 11.2 %copy-start.4 = (bf16[96,3584]{1,0:T(8,128)(2,1)}, bf16[96,3584]{1,0:T(8,128)(2,1)S(1)}, u32[]{:S(2)}) copy-start(bf16[96,3584]{1,0:T(8,128)(2,1)S(1)} %collective-permute-done.6.refs_2_) | copy-start | bytes 2064388
  41.9 22.4 %collective-permute-start.17 = (bf16[3584,384]{1,0:T(8,128)(2,1)}, bf16[3584,384]{1,0:T(8,128)(2,1)}, u32[]{:S(2)}, u32[]{:S(2)}) collective-permute-start(bf16[3584,384]{1,0:T(8,128)(2,1)} %collective-permute-done.11.refs_6_.refs_11_), channel_id=1, source_target_pairs={{0,1},{1,0},{2,3},{3,2},{4,5},{5,4},{6,7},{7,6},{8,9},{9,8},{10,11... | collective-permute-start | bytes 8257544 | tf_op jit(solution)/shard_map/ppermute | solution.py:23
  43.3 15.8 %collective-permute-start.12 = (bf16[96,3584]{1,0:T(8,128)(2,1)S(1)}, bf16[96,3584]{1,0:T(8,128)(2,1)S(1)}, u32[]{:S(2)}, u32[]{:S(2)}) collective-permute-start(bf16[96,3584]{1,0:T(8,128)(2,1)S(1)} %collective-permute-done.6.refs_2_), channel_id=1, source_target_pairs={{0,32},{1,225},{32,64},{33,1},{64,96},{65,33},{96,128},{97,65},{12... | collective-permute-start | bytes 2064392 | tf_op jit(solution)/shard_map/ppermute | solution.py:37
  45.3 13.9 %collective-permute-start.14 = (bf16[80,3584]{1,0:T(8,128)(2,1)S(1)}, bf16[80,3584]{1,0:T(8,128)(2,1)}, u32[]{:S(2)}, u32[]{:S(2)}) collective-permute-start(bf16[80,3584]{1,0:T(8,128)(2,1)S(1)} %collective-permute-done.5.refs_4_), channel_id=1, source_target_pairs={{0,8},{1,25},{8,16},{9,1},{16,24},{17,9},{24,0},{25,17},{2,10},{3,... | collective-permute-start | bytes 1720328 | tf_op jit(solution)/shard_map/ppermute | solution.py:37
  47.0 12.1 %collective-permute-start.13 = (bf16[64,3584]{1,0:T(8,128)(2,1)}, bf16[64,3584]{1,0:T(8,128)(2,1)}, u32[]{:S(2)}, u32[]{:S(2)}) collective-permute-start(bf16[64,3584]{1,0:T(8,128)(2,1)} %collective-permute-done.10.refs_3_), channel_id=1, source_target_pairs={{0,32},{1,225},{32,64},{33,1},{64,96},{65,33},{96,128},{97,65},{12... | collective-permute-start | bytes 1376264 | tf_op jit(solution)/shard_map/ppermute | solution.py:37
  59.2 13.3 %copy-start.2 = (bf16[96,3584]{1,0:T(8,128)(2,1)}, bf16[96,3584]{1,0:T(8,128)(2,1)S(1)}, u32[]{:S(2)}) copy-start(bf16[96,3584]{1,0:T(8,128)(2,1)S(1)} %collective-permute-done.12.refs_0_) | copy-start | bytes 2064388
  59.2 13.3 %collective-permute-start.15 = (bf16[64,3584]{1,0:T(8,128)(2,1)S(1)}, bf16[64,3584]{1,0:T(8,128)(2,1)S(1)}, u32[]{:S(2)}, u32[]{:S(2)}) collective-permute-start(bf16[64,3584]{1,0:T(8,128)(2,1)S(1)} %slice.321), channel_id=1, source_target_pairs={{0,32},{1,225},{32,64},{33,1},{64,96},{65,33},{96,128},{97,65},{12... | collective-permute-start | bytes 1376264 | tf_op jit(solution)/shard_map/ppermute | solution.py:37
  61.5 11.0 %collective-permute-start.16 = (bf16[48,3584]{1,0:T(8,128)(2,1)S(1)}, bf16[48,3584]{1,0:T(8,128)(2,1)S(1)}, u32[]{:S(2)}, u32[]{:S(2)}) collective-permute-start(bf16[48,3584]{1,0:T(8,128)(2,1)S(1)} %pad_maximum_fusion.3), channel_id=1, source_target_pairs={{0,8},{1,25},{8,16},{9,1},{16,24},{17,9},{24,0},{25,17},{2,10},{3,... | collective-permute-start | bytes 1032200 | tf_op jit(solution)/shard_map/ppermute | solution.py:37
  63.8 8.7 %collective-permute-start.19 = (bf16[48,3584]{1,0:T(8,128)(2,1)S(1)}, bf16[48,3584]{1,0:T(8,128)(2,1)S(1)}, u32[]{:S(2)}, u32[]{:S(2)}) collective-permute-start(bf16[48,3584]{1,0:T(8,128)(2,1)S(1)} %pad_maximum_fusion.3), channel_id=1, source_target_pairs={{0,1},{1,0},{2,3},{3,2},{4,5},{5,4},{6,7},{7,6},{8,9},{9,8},{10,11... | collective-permute-start | bytes 1032200 | tf_op jit(solution)/shard_map/ppermute | solution.py:23
  63.8 13.4 %collective-permute-start.18 = (bf16[64,3584]{1,0:T(8,128)(2,1)}, bf16[64,3584]{1,0:T(8,128)(2,1)S(1)}, u32[]{:S(2)}, u32[]{:S(2)}) collective-permute-start(bf16[64,3584]{1,0:T(8,128)(2,1)} %collective-permute-done.13.refs_1_), channel_id=1, source_target_pairs={{0,32},{1,225},{32,64},{33,1},{64,96},{65,33},{96,128},{97,65},{12... | collective-permute-start | bytes 1376264 | tf_op jit(solution)/shard_map/ppermute | solution.py:37
  72.5 11.0 %collective-permute-start.21 = (bf16[64,3584]{1,0:T(8,128)(2,1)S(1)}, bf16[64,3584]{1,0:T(8,128)(2,1)S(1)}, u32[]{:S(2)}, u32[]{:S(2)}) collective-permute-start(bf16[64,3584]{1,0:T(8,128)(2,1)S(1)} %collective-permute-done.15.refs_3_), channel_id=1, source_target_pairs={{0,32},{1,225},{32,64},{33,1},{64,96},{65,33},{96,128},{97,65},{12... | collective-permute-start | bytes 1376264 | tf_op jit(solution)/shard_map/ppermute | solution.py:37
  72.6 7.2 %collective-permute-start.20 = (bf16[48,3584]{1,0:T(8,128)(2,1)S(1)}, bf16[48,3584]{1,0:T(8,128)(2,1)S(1)}, u32[]{:S(2)}, u32[]{:S(2)}) collective-permute-start(bf16[48,3584]{1,0:T(8,128)(2,1)S(1)} %collective-permute-done.19), channel_id=1, source_target_pairs={{0,8},{1,25},{8,16},{9,1},{16,24},{17,9},{24,0},{25,17},{2,10},{3,... | collective-permute-start | bytes 1032200 | tf_op jit(solution)/shard_map/ppermute | solution.py:37
  75.6 7.9 %collective-permute-start.22 = (bf16[48,3584]{1,0:T(8,128)(2,1)S(1)}, bf16[48,3584]{1,0:T(8,128)(2,1)S(1)}, u32[]{:S(2)}, u32[]{:S(2)}) collective-permute-start(bf16[48,3584]{1,0:T(8,128)(2,1)S(1)} %collective-permute-done.16.refs_5_), channel_id=1, source_target_pairs={{0,8},{1,25},{8,16},{9,1},{16,24},{17,9},{24,0},{25,17},{2,10},{3,... | collective-permute-start | bytes 1032200 | tf_op jit(solution)/shard_map/ppermute | solution.py:37
  77.2 41.7 %copy-start.13 = (s32[8]{0:T(128)S(1)}, s32[8]{0:T(128)}, u32[]{:S(2)}) copy-start(s32[8]{0:T(128)} %param.9) | copy-start | bytes 100
  77.2 41.7 %copy-start.14 = (s32[8]{0:T(128)S(1)}, s32[8]{0:T(128)}, u32[]{:S(2)}) copy-start(s32[8]{0:T(128)} %param.10) | copy-start | bytes 100
  77.2 50.1 %copy-start.15 = (f32[22]{0:T(128)S(1)}, f32[22]{0:T(128)}, u32[]{:S(2)}) copy-start(f32[22]{0:T(128)} %param.11) | copy-start | bytes 268
  117.7 2.0 %collective-permute-start.23 = (f32[128]{0:T(128)S(1)}, f32[128]{0:T(128)S(1)}, u32[]{:S(2)}, u32[]{:S(2)}) collective-permute-start(f32[128]{0:T(128)S(1)} %pad_maximum_fusion.6), channel_id=1, source_target_pairs={{0,1},{1,0},{2,3},{3,2},{4,5},{5,4},{6,7},{7,6},{8,9},{9,8},{10,11... | collective-permute-start | bytes 1544 | tf_op jit(solution)/shard_map/ppermute | solution.py:23
  122.1 18.4 %all-to-all-start.1 = ((f32[256,1,128]{2,1,0:T(1,128)}), f32[256,1,128]{2,1,0:T(1,128)S(1)}, u32[]{:S(2)}, u32[]{:S(2)}) async-start(f32[256,1,128]{2,1,0:T(1,128)} %broadcast_in_dim.2), calls=%async_computation.1 | async-start | bytes 262144 | tf_op jit(solution)/shard_map/all_to_all | solution.py:386
  (9 other events, 52.7 us)

commit v4 on v3

--- a/solution.py
+++ b/solution.py
@@ -356,10 +356,10 @@
     xb3, xb3_mate = onward(mine_b2, "x"), onward(mate_b2, "x")
     col_in_mate = shift(col_in, "c", 1)
     far_cols = [[col_in], [col_in_mate]]
-    done_1 = tile_stats(pieces, wanted[0], far_cols, scalars(*in_starts), prev=stats_1)
+    za3, xb3, far_starts = together(za3, xb3, scalars(*in_starts))
+    za4, xb4 = onward(za3, "z"), onward(xb3, "x")
+    done_1 = tile_stats(pieces, wanted[0], far_cols, far_starts, prev=stats_1)
     stats_2 = done_1[1]
-    za3, xb3, stats_2 = together(za3, xb3, stats_2)
-    za4, xb4 = onward(za3, "z"), onward(xb3, "x")
     cols = near_cols + far_cols
     pieces = pieces_of(
         [za2, za2_mate, xb2, za3, za3_mate, xb3, xb3_mate, za4, xb4], mine_4

time: 144 us -> 143 us (level)
  waiting for transfers between devices: 37.2 us -> 34.4 us
  starting transfers between devices: 43.3 us -> 45.7 us
  blocking collectives: 16.8 us -> 15.3 us
    ppermute x17, waiting for transfers between devices: 19.1 us -> 16.4 us  [onward(): return lax.ppermute(a, (axis, 'c'), moves)]
    ppermute x6, starting transfers between devices: 6.62 us -> 8.68 us  [shift(): return lax.ppermute(a, axis, [(i, (i + by) % n) for i in range(n)])]
    all_to_all x1, blocking collectives: 16.8 us -> 15.3 us  [body(): mine = lax.all_to_all(every, DP, 0, 0, tiled=True)]
  transfers between devices with their start and end apart: 25 -> 25, of which waited for: 10 -> 9; matrix products, arithmetic and copies ran while one was open for 4% -> 4% of each run, Pallas kernels for 11% -> 11%
where the time goes in v4:
time: 143 us; the launch traced here: 142 us
  starting transfers between devices  45.7 us (32%)
  Pallas kernels  34.8 us (24%)
  waiting for transfers between devices  34.4 us (24%)
  blocking collectives  15.3 us (11%)
  local copies, waits for them, and re-layouts  8.33 us (6%)
  other arithmetic  2.71 us (2%)
    pallas_call x3, Pallas kernels, tile_stats(): pl.pallas_call(functools.partial(stats_kernel, tuple(listed), tuple((len(...  31.9 us
    ppermute x17, starting transfers between devices, onward(): return lax.ppermute(a, (axis, 'c'), moves)  30.2 us
    ppermute x17, waiting for transfers between devices, onward(): return lax.ppermute(a, (axis, 'c'), moves)  16.4 us
    all_to_all x1, blocking collectives, body(): mine = lax.all_to_all(every, DP, 0, 0, tiled=True)  15.3 us
    all_to_all x1, waiting for transfers between devices, body(): notes = lax.all_to_all(sent, ALL, 0, 0, tiled=True)  12.4 us
    ppermute x6, starting transfers between devices, shift(): return lax.ppermute(a, axis, [(i, (i + by) % n) for i in range(n)])  8.68 us
    all_to_all x1, starting transfers between devices, body(): notes = lax.all_to_all(sent, ALL, 0, 0, tiled=True)  5.84 us
    ppermute x1, waiting for transfers between devices, body(): col_in = lax.ppermute(head_weight, VOCAB_AXES, moves)  4.95 us
  transfers between devices with their start and end apart: 25, of which 9 were waited for; matrix products, arithmetic and copies ran while one was open for 4% of the time, Pallas kernels for 11%

profile of v4, /device:TPU:1, one launch (start us, length us, event | category | flops | bytes accessed | tf_op | source)
XLA Modules:
  0.0 142.4 jit_solution(5976324943331688179)
XLA Ops:
  0.6 3.3 %collective-permute-start.2 = (bf16[3584,384]{1,0:T(8,128)(2,1)}, bf16[3584,384]{1,0:T(8,128)(2,1)}, u32[]{:S(2)}, u32[]{:S(2)}) collective-permute-start(bf16[3584,384]{1,0:T(8,128)(2,1)} %refs_9_.1), channel_id=1, source_target_pairs={{0,1},{1,0},{2,3},{3,2},{4,5},{5,4},{6,7},{7,6},{8,9},{9,8},{10,11... | collective-permute-start | bytes 8257544 | tf_op jit(solution)/shard_map/ppermute | solution.py:23
  4.0 1.0 collective-permute-start.11
  5.0 1.1 constant_dynamic-slice_fusion.3
  6.1 5.7 %collective-permute-start.1 = (bf16[32,3584]{1,0:T(8,128)(2,1)S(1)}, bf16[32,3584]{1,0:T(8,128)(2,1)S(1)}, u32[]{:S(2)}, u32[]{:S(2)}) collective-permute-start(bf16[32,3584]{1,0:T(8,128)(2,1)S(1)} %pad_maximum_fusion.5), channel_id=1, source_target_pairs={{0,32},{1,225},{32,64},{33,1},{64,96},{65,33},{96,128},{97,65},{12... | collective-permute-start | bytes 688136 | tf_op jit(solution)/shard_map/ppermute | solution.py:37
  11.8 2.6 %collective-permute-start = (bf16[32,3584]{1,0:T(8,128)(2,1)S(1)}, bf16[32,3584]{1,0:T(8,128)(2,1)S(1)}, u32[]{:S(2)}, u32[]{:S(2)}) collective-permute-start(bf16[32,3584]{1,0:T(8,128)(2,1)S(1)} %pad_maximum_fusion.4), channel_id=1, source_target_pairs={{0,8},{1,25},{8,16},{9,1},{16,24},{17,9},{24,0},{25,17},{2,10},{3,... | collective-permute-start | bytes 688136 | tf_op jit(solution)/shard_map/ppermute | solution.py:37
  14.9 2.4 %collective-permute-done = bf16[32,3584]{1,0:T(8,128)(2,1)S(1)} collective-permute-done((bf16[32,3584]{1,0:T(8,128)(2,1)S(1)}, bf16[32,3584]{1,0:T(8,128)(2,1)S(1)}, u32[]{:S(2)}, u32[]{:S(2)}) %collective-permute-start) | collective-permute-done | bytes 229408 | tf_op jit(solution)/shard_map/ppermute | solution.py:37
  17.3 0.9 collective-permute-start.4
  18.4 3.4 %collective-permute-start.3 = (bf16[16,3584]{1,0:T(8,128)(2,1)S(1)}, bf16[16,3584]{1,0:T(8,128)(2,1)S(1)}, u32[]{:S(2)}, u32[]{:S(2)}) collective-permute-start(bf16[16,3584]{1,0:T(8,128)(2,1)S(1)} %slice.250), channel_id=1, source_target_pairs={{0,8},{1,25},{8,16},{9,1},{16,24},{17,9},{24,0},{25,17},{2,10},{3,... | collective-permute-start | bytes 344072 | tf_op jit(solution)/shard_map/ppermute | solution.py:37
  21.9 1.7 %collective-permute-done.3 = bf16[16,3584]{1,0:T(8,128)(2,1)S(1)} collective-permute-done((bf16[16,3584]{1,0:T(8,128)(2,1)S(1)}, bf16[16,3584]{1,0:T(8,128)(2,1)S(1)}, u32[]{:S(2)}, u32[]{:S(2)}) %collective-permute-start.3) | collective-permute-done | bytes 114720 | tf_op jit(solution)/shard_map/ppermute | solution.py:37
  24.5 1.2 collective-permute-start.6
  25.6 3.4 %collective-permute-start.5 = (bf16[80,3584]{1,0:T(8,128)(2,1)S(1)}, bf16[80,3584]{1,0:T(8,128)(2,1)S(1)}, u32[]{:S(2)}, u32[]{:S(2)}) collective-permute-start(bf16[80,3584]{1,0:T(8,128)(2,1)S(1)} %pad_maximum_fusion.1.refs_1_), channel_id=1, source_target_pairs={{0,8},{1,25},{8,16},{9,1},{16,24},{17,9},{24,0},{25,17},{2,10},{3,... | collective-permute-start | bytes 1720328 | tf_op jit(solution)/shard_map/ppermute | solution.py:37
  31.5 5.0 %collective-permute-done.11.refs_6_.refs_11_ = bf16[3584,384]{1,0:T(8,128)(2,1)} collective-permute-done((bf16[3584,384]{1,0:T(8,128)(2,1)}, bf16[3584,384]{1,0:T(8,128)(2,1)}, u32[]{:S(2)}, u32[]{:S(2)}) %collective-permute-start.11) | collective-permute-done | bytes 2752544 | tf_op jit(solution)/shard_map/ppermute | solution.py:328
  36.5 3.1 %collective-permute-done.10.refs_3_ = bf16[64,3584]{1,0:T(8,128)(2,1)} collective-permute-done((bf16[64,3584]{1,0:T(8,128)(2,1)}, bf16[64,3584]{1,0:T(8,128)(2,1)}, u32[]{:S(2)}, u32[]{:S(2)}) %collective-permute-start.10) | collective-permute-done | bytes 458784 | tf_op jit(solution)/shard_map/ppermute | solution.py:37
  39.6 2.3 %collective-permute-done.8.refs_5_ = bf16[80,3584]{1,0:T(8,128)(2,1)} collective-permute-done((bf16[80,3584]{1,0:T(8,128)(2,1)}, bf16[80,3584]{1,0:T(8,128)(2,1)}, u32[]{:S(2)}, u32[]{:S(2)}) %collective-permute-start.8) | collective-permute-done | bytes 573472 | tf_op jit(solution)/shard_map/ppermute | solution.py:37
  41.9 1.4 collective-permute-start.22
  43.3 1.9 %collective-permute-start.12 = (bf16[96,3584]{1,0:T(8,128)(2,1)S(1)}, bf16[96,3584]{1,0:T(8,128)(2,1)S(1)}, u32[]{:S(2)}, u32[]{:S(2)}) collective-permute-start(bf16[96,3584]{1,0:T(8,128)(2,1)S(1)} %collective-permute-done.6.refs_2_), channel_id=1, source_target_pairs={{0,32},{1,225},{32,64},{33,1},{64,96},{65,33},{96,128},{97,65},{12... | collective-permute-start | bytes 2064392 | tf_op jit(solution)/shard_map/ppermute | solution.py:37
  45.3 1.7 %collective-permute-start.14 = (bf16[80,3584]{1,0:T(8,128)(2,1)S(1)}, bf16[80,3584]{1,0:T(8,128)(2,1)S(1)}, u32[]{:S(2)}, u32[]{:S(2)}) collective-permute-start(bf16[80,3584]{1,0:T(8,128)(2,1)S(1)} %collective-permute-done.5.refs_4_), channel_id=1, source_target_pairs={{0,8},{1,25},{8,16},{9,1},{16,24},{17,9},{24,0},{25,17},{2,10},{3,... | collective-permute-start | bytes 1720328 | tf_op jit(solution)/shard_map/ppermute | solution.py:37
  47.7 8.1 %shard_map.77.refs_8_ = f32[2,512]{1,0:T(2,128)} custom-call(s32[2]{0:T(128)} %pad_add_fusion.3.starts, s32[1,512]{1,0:T(1,128)} %bitcast.158, bf16[64,3584]{1,0:T(8,128)(2,1)} %copy-done.3, bf16[80,3584]{1,0:T(8,128)(2,1)} %copy-done, bf16[96,3584]{1,0:T(8,128)(2,1)} %copy-done.4, bf16[64,3584]{1,0:T(8,128)(2,1)} %collective-permute-done.10.refs_3_, ...), custom_call_target="tpu_custom_call" | custom-call | flops 2554331136 | bytes 8830976 | tf_op jit(solution)/shard_map/pallas_call | solution.py:173
  55.9 3.3 %collective-permute-done.13.refs_1_ = bf16[64,3584]{1,0:T(8,128)(2,1)} collective-permute-done((bf16[64,3584]{1,0:T(8,128)(2,1)}, bf16[64,3584]{1,0:T(8,128)(2,1)}, u32[]{:S(2)}, u32[]{:S(2)}) %collective-permute-start.13) | collective-permute-done | bytes 458784 | tf_op jit(solution)/shard_map/ppermute | solution.py:37
  59.2 2.2 %collective-permute-start.15 = (bf16[64,3584]{1,0:T(8,128)(2,1)S(1)}, bf16[64,3584]{1,0:T(8,128)(2,1)S(1)}, u32[]{:S(2)}, u32[]{:S(2)}) collective-permute-start(bf16[64,3584]{1,0:T(8,128)(2,1)S(1)} %slice.321), channel_id=1, source_target_pairs={{0,32},{1,225},{32,64},{33,1},{64,96},{65,33},{96,128},{97,65},{12... | collective-permute-start | bytes 1376264 | tf_op jit(solution)/shard_map/ppermute | solution.py:37
  61.5 1.8 %collective-permute-start.16 = (bf16[48,3584]{1,0:T(8,128)(2,1)S(1)}, bf16[48,3584]{1,0:T(8,128)(2,1)S(1)}, u32[]{:S(2)}, u32[]{:S(2)}) collective-permute-start(bf16[48,3584]{1,0:T(8,128)(2,1)S(1)} %pad_maximum_fusion.3), channel_id=1, source_target_pairs={{0,8},{1,25},{8,16},{9,1},{16,24},{17,9},{24,0},{25,17},{2,10},{3,... | collective-permute-start | bytes 1032200 | tf_op jit(solution)/shard_map/ppermute | solution.py:37
  64.4 3.5 %collective-permute-done.16.refs_5_ = bf16[48,3584]{1,0:T(8,128)(2,1)S(1)} collective-permute-done((bf16[48,3584]{1,0:T(8,128)(2,1)S(1)}, bf16[48,3584]{1,0:T(8,128)(2,1)S(1)}, u32[]{:S(2)}, u32[]{:S(2)}) %collective-permute-start.16) | collective-permute-done | bytes 344096 | tf_op jit(solution)/shard_map/ppermute | solution.py:37
  68.0 2.3 %collective-permute-start.20 = (bf16[64,3584]{1,0:T(8,128)(2,1)S(1)}, bf16[64,3584]{1,0:T(8,128)(2,1)S(1)}, u32[]{:S(2)}, u32[]{:S(2)}) collective-permute-start(bf16[64,3584]{1,0:T(8,128)(2,1)S(1)} %collective-permute-done.15.refs_3_), channel_id=1, source_target_pairs={{0,32},{1,225},{32,64},{33,1},{64,96},{65,33},{96,128},{97,65},{12... | collective-permute-start | bytes 1376264 | tf_op jit(solution)/shard_map/ppermute | solution.py:37
  70.3 1.4 %collective-permute-start.19 = (bf16[48,3584]{1,0:T(8,128)(2,1)}, bf16[48,3584]{1,0:T(8,128)(2,1)S(1)}, u32[]{:S(2)}, u32[]{:S(2)}) collective-permute-start(bf16[48,3584]{1,0:T(8,128)(2,1)} %collective-permute-done.18), channel_id=1, source_target_pairs={{0,8},{1,25},{8,16},{9,1},{16,24},{17,9},{24,0},{25,17},{2,10},{3,... | collective-permute-start | bytes 1032200 | tf_op jit(solution)/shard_map/ppermute | solution.py:37
  72.4 8.1 %shard_map.78.refs_13_ = f32[2,512]{1,0:T(2,128)} custom-call(s32[2]{0:T(128)} %pad_add_fusion.4.starts, s32[1,512]{1,0:T(1,128)} %bitcast.159, bf16[64,3584]{1,0:T(8,128)(2,1)} %copy-done.3, bf16[80,3584]{1,0:T(8,128)(2,1)} %copy-done, bf16[96,3584]{1,0:T(8,128)(2,1)} %copy-done.4, bf16[64,3584]{1,0:T(8,128)(2,1)} %collective-permute-done.10.refs_3_, ...), custom_call_target="tpu_custom_call" | custom-call | flops 2554331136 | bytes 8830976 | tf_op jit(solution)/shard_map/pallas_call | solution.py:173
  81.6 0.8 copy-done.10
  82.4 15.6 %shard_map.79 = f32[32,128]{1,0:T(8,128)} custom-call(s32[7]{0:T(128)} %stack.44.starts, s32[1,640]{1,0:T(1,128)} %reshape.91.targets, bf16[96,3584]{1,0:T(8,128)(2,1)} %copy-done.2, bf16[64,3584]{1,0:T(8,128)(2,1)} %collective-permute-done.13.refs_1_, bf16[80,3584]{1,0:T(8,128)(2,1)} %copy-done.7, bf16[64,3584]{1,0:T(8,128)(2,1)} %copy-done.8, ...), custom_call_target="tpu_custom_call" | custom-call | flops 6165626880 | bytes 15024128 | tf_op jit(solution)/shard_map/pallas_call | solution.py:173
  98.0 15.3 %all_to_all.18 = f32[32,1,128]{2,1,0:T(1,128)S(1)} all-to-all(f32[32,1,128]{2,1,0:T(1,128)} %bitcast.154), channel_id=1, replica_groups=mesh['z'=8,'x'=4,'yh'=2,'yl'=2,'c'=2] {'z','x'}, dimensions={0} | all-to-all | bytes 32768 | tf_op jit(solution)/shard_map/all_to_all | solution.py:375
  113.5 3.3 %collective-permute-start.23 = (f32[128]{0:T(128)S(1)}, f32[128]{0:T(128)S(1)}, u32[]{:S(2)}, u32[]{:S(2)}) collective-permute-start(f32[128]{0:T(128)S(1)} %pad_maximum_fusion.6), channel_id=1, source_target_pairs={{0,1},{1,0},{2,3},{3,2},{4,5},{5,4},{6,7},{7,6},{8,9},{9,8},{10,11... | collective-permute-start | bytes 1544 | tf_op jit(solution)/shard_map/ppermute | solution.py:23
  119.9 5.8 %all-to-all-start.1 = ((f32[256,1,128]{2,1,0:T(1,128)}), f32[256,1,128]{2,1,0:T(1,128)S(1)}, u32[]{:S(2)}, u32[]{:S(2)}) async-start(f32[256,1,128]{2,1,0:T(1,128)} %broadcast_in_dim.2), calls=%async_computation.1 | async-start | bytes 262144 | tf_op jit(solution)/shard_map/all_to_all | solution.py:386
  126.4 12.4 %all-to-all-done.1 = f32[256,1,128]{2,1,0:T(1,128)S(1)} async-done(((f32[256,1,128]{2,1,0:T(1,128)}), f32[256,1,128]{2,1,0:T(1,128)S(1)}, u32[]{:S(2)}, u32[]{:S(2)}) %all-to-all-start.1) | async-done | bytes 131104 | tf_op jit(solution)/shard_map/all_to_all | solution.py:386
  139.4 3.0 %shard_map.80 = (f32[1,128]{1,0:T(1,128)}, f32[1,22]{1,0:T(1,128)}) custom-call(s32[1]{0:T(128)} %bitcast.place, f32[32,8,128]{2,1,0:T(8,128)} %bitcast.151, f32[1,128]{1,0:T(1,128)} %pad_bitcast_fusion.weights), custom_call_target="tpu_custom_call" | custom-call | tf_op jit(solution)/shard_map/pallas_call | solution.py:388
  (111 shorter events, 12.1 us)
Async XLA Ops:
  0.6 13.7 %copy-start.5 = (s32[4096]{0:T(1024)S(1)}, s32[4096]{0:T(1024)}, u32[]{:S(2)}) copy-start(s32[4096]{0:T(1024)} %param.8) | copy-start | bytes 49156
  0.6 16.6 %collective-permute-start.2 = (bf16[3584,384]{1,0:T(8,128)(2,1)}, bf16[3584,384]{1,0:T(8,128)(2,1)}, u32[]{:S(2)}, u32[]{:S(2)}) collective-permute-start(bf16[3584,384]{1,0:T(8,128)(2,1)} %refs_9_.1), channel_id=1, source_target_pairs={{0,1},{1,0},{2,3},{3,2},{4,5},{5,4},{6,7},{7,6},{8,9},{9,8},{10,11... | collective-permute-start | bytes 8257544 | tf_op jit(solution)/shard_map/ppermute | solution.py:23
  4.0 32.5 %collective-permute-start.11 = (bf16[3584,384]{1,0:T(8,128)(2,1)}, bf16[3584,384]{1,0:T(8,128)(2,1)}, u32[]{:S(2)}, u32[]{:S(2)}) collective-permute-start(bf16[3584,384]{1,0:T(8,128)(2,1)} %refs_9_.1), channel_id=1, source_target_pairs={{0,2},{1,7},{2,4},{3,1},{4,6},{5,3},{6,0},{7,5},{8,10},{9,15},{10,... | collective-permute-start | bytes 8257544 | tf_op jit(solution)/shard_map/ppermute | solution.py:328
  6.1 8.8 %collective-permute-start.1 = (bf16[32,3584]{1,0:T(8,128)(2,1)S(1)}, bf16[32,3584]{1,0:T(8,128)(2,1)S(1)}, u32[]{:S(2)}, u32[]{:S(2)}) collective-permute-start(bf16[32,3584]{1,0:T(8,128)(2,1)S(1)} %pad_maximum_fusion.5), channel_id=1, source_target_pairs={{0,32},{1,225},{32,64},{33,1},{64,96},{65,33},{96,128},{97,65},{12... | collective-permute-start | bytes 688136 | tf_op jit(solution)/shard_map/ppermute | solution.py:37
  11.8 5.5 %collective-permute-start = (bf16[32,3584]{1,0:T(8,128)(2,1)S(1)}, bf16[32,3584]{1,0:T(8,128)(2,1)S(1)}, u32[]{:S(2)}, u32[]{:S(2)}) collective-permute-start(bf16[32,3584]{1,0:T(8,128)(2,1)S(1)} %pad_maximum_fusion.4), channel_id=1, source_target_pairs={{0,8},{1,25},{8,16},{9,1},{16,24},{17,9},{24,0},{25,17},{2,10},{3,... | collective-permute-start | bytes 688136 | tf_op jit(solution)/shard_map/ppermute | solution.py:37
  17.3 6.3 %collective-permute-start.4 = (bf16[32,3584]{1,0:T(8,128)(2,1)S(1)}, bf16[32,3584]{1,0:T(8,128)(2,1)S(1)}, u32[]{:S(2)}, u32[]{:S(2)}) collective-permute-start(bf16[32,3584]{1,0:T(8,128)(2,1)S(1)} %collective-permute-done.1), channel_id=1, source_target_pairs={{0,32},{1,225},{32,64},{33,1},{64,96},{65,33},{96,128},{97,65},{12... | collective-permute-start | bytes 688136 | tf_op jit(solution)/shard_map/ppermute | solution.py:37
  18.4 5.2 %collective-permute-start.3 = (bf16[16,3584]{1,0:T(8,128)(2,1)S(1)}, bf16[16,3584]{1,0:T(8,128)(2,1)S(1)}, u32[]{:S(2)}, u32[]{:S(2)}) collective-permute-start(bf16[16,3584]{1,0:T(8,128)(2,1)S(1)} %slice.250), channel_id=1, source_target_pairs={{0,8},{1,25},{8,16},{9,1},{16,24},{17,9},{24,0},{25,17},{2,10},{3,... | collective-permute-start | bytes 344072 | tf_op jit(solution)/shard_map/ppermute | solution.py:37
  23.7 5.4 %collective-permute-start.9 = (bf16[64,3584]{1,0:T(8,128)(2,1)S(1)}, bf16[64,3584]{1,0:T(8,128)(2,1)}, u32[]{:S(2)}, u32[]{:S(2)}) collective-permute-start(bf16[64,3584]{1,0:T(8,128)(2,1)S(1)} %pad_maximum_fusion.2.refs_0_), channel_id=1, source_target_pairs={{0,1},{1,0},{2,3},{3,2},{4,5},{5,4},{6,7},{7,6},{8,9},{9,8},{10,11... | collective-permute-start | bytes 1376264 | tf_op jit(solution)/shard_map/ppermute | solution.py:23
  23.8 23.9 %copy-start = (bf16[80,3584]{1,0:T(8,128)(2,1)}, bf16[80,3584]{1,0:T(8,128)(2,1)S(1)}, u32[]{:S(2)}) copy-start(bf16[80,3584]{1,0:T(8,128)(2,1)S(1)} %pad_maximum_fusion.1.refs_1_) | copy-start | bytes 1720324
  23.8 5.7 %collective-permute-start.7 = (bf16[80,3584]{1,0:T(8,128)(2,1)S(1)}, bf16[80,3584]{1,0:T(8,128)(2,1)}, u32[]{:S(2)}, u32[]{:S(2)}) collective-permute-start(bf16[80,3584]{1,0:T(8,128)(2,1)S(1)} %pad_maximum_fusion.1.refs_1_), channel_id=1, source_target_pairs={{0,1},{1,0},{2,3},{3,2},{4,5},{5,4},{6,7},{7,6},{8,9},{9,8},{10,11... | collective-permute-start | bytes 1720328 | tf_op jit(solution)/shard_map/ppermute | solution.py:23
  24.5 12.0 %collective-permute-start.6 = (bf16[96,3584]{1,0:T(8,128)(2,1)S(1)}, bf16[96,3584]{1,0:T(8,128)(2,1)S(1)}, u32[]{:S(2)}, u32[]{:S(2)}) collective-permute-start(bf16[96,3584]{1,0:T(8,128)(2,1)S(1)} %pad_maximum_fusion), channel_id=1, source_target_pairs={{0,32},{1,225},{32,64},{33,1},{64,96},{65,33},{96,128},{97,65},{12... | collective-permute-start | bytes 2064392 | tf_op jit(solution)/shard_map/ppermute | solution.py:37
  25.6 10.8 %collective-permute-start.5 = (bf16[80,3584]{1,0:T(8,128)(2,1)S(1)}, bf16[80,3584]{1,0:T(8,128)(2,1)S(1)}, u32[]{:S(2)}, u32[]{:S(2)}) collective-permute-start(bf16[80,3584]{1,0:T(8,128)(2,1)S(1)} %pad_maximum_fusion.1.refs_1_), channel_id=1, source_target_pairs={{0,8},{1,25},{8,16},{9,1},{16,24},{17,9},{24,0},{25,17},{2,10},{3,... | collective-permute-start | bytes 1720328 | tf_op jit(solution)/shard_map/ppermute | solution.py:37
  29.0 10.6 %collective-permute-start.10 = (bf16[64,3584]{1,0:T(8,128)(2,1)}, bf16[64,3584]{1,0:T(8,128)(2,1)}, u32[]{:S(2)}, u32[]{:S(2)}) collective-permute-start(bf16[64,3584]{1,0:T(8,128)(2,1)} %collective-permute-done.9), channel_id=1, source_target_pairs={{0,32},{1,225},{32,64},{33,1},{64,96},{65,33},{96,128},{97,65},{12... | collective-permute-start | bytes 1376264 | tf_op jit(solution)/shard_map/ppermute | solution.py:37
  29.5 12.4 %collective-permute-start.8 = (bf16[80,3584]{1,0:T(8,128)(2,1)}, bf16[80,3584]{1,0:T(8,128)(2,1)}, u32[]{:S(2)}, u32[]{:S(2)}) collective-permute-start(bf16[80,3584]{1,0:T(8,128)(2,1)} %collective-permute-done.7), channel_id=1, source_target_pairs={{0,8},{1,25},{8,16},{9,1},{16,24},{17,9},{24,0},{25,17},{2,10},{3,... | collective-permute-start | bytes 1720328 | tf_op jit(solution)/shard_map/ppermute | solution.py:37
  41.9 30.5 %collective-permute-start.22 = (bf16[3584,384]{1,0:T(8,128)(2,1)}, bf16[3584,384]{1,0:T(8,128)(2,1)}, u32[]{:S(2)}, u32[]{:S(2)}) collective-permute-start(bf16[3584,384]{1,0:T(8,128)(2,1)} %collective-permute-done.11.refs_6_.refs_11_), channel_id=1, source_target_pairs={{0,1},{1,0},{2,3},{3,2},{4,5},{5,4},{6,7},{7,6},{8,9},{9,8},{10,11... | collective-permute-start | bytes 8257544 | tf_op jit(solution)/shard_map/ppermute | solution.py:23
  43.3 15.8 %collective-permute-start.12 = (bf16[96,3584]{1,0:T(8,128)(2,1)S(1)}, bf16[96,3584]{1,0:T(8,128)(2,1)S(1)}, u32[]{:S(2)}, u32[]{:S(2)}) collective-permute-start(bf16[96,3584]{1,0:T(8,128)(2,1)S(1)} %collective-permute-done.6.refs_2_), channel_id=1, source_target_pairs={{0,32},{1,225},{32,64},{33,1},{64,96},{65,33},{96,128},{97,65},{12... | collective-permute-start | bytes 2064392 | tf_op jit(solution)/shard_map/ppermute | solution.py:37
  45.3 13.9 %collective-permute-start.14 = (bf16[80,3584]{1,0:T(8,128)(2,1)S(1)}, bf16[80,3584]{1,0:T(8,128)(2,1)S(1)}, u32[]{:S(2)}, u32[]{:S(2)}) collective-permute-start(bf16[80,3584]{1,0:T(8,128)(2,1)S(1)} %collective-permute-done.5.refs_4_), channel_id=1, source_target_pairs={{0,8},{1,25},{8,16},{9,1},{16,24},{17,9},{24,0},{25,17},{2,10},{3,... | collective-permute-start | bytes 1720328 | tf_op jit(solution)/shard_map/ppermute | solution.py:37
  47.0 12.1 %collective-permute-start.13 = (bf16[64,3584]{1,0:T(8,128)(2,1)}, bf16[64,3584]{1,0:T(8,128)(2,1)}, u32[]{:S(2)}, u32[]{:S(2)}) collective-permute-start(bf16[64,3584]{1,0:T(8,128)(2,1)} %collective-permute-done.10.refs_3_), channel_id=1, source_target_pairs={{0,32},{1,225},{32,64},{33,1},{64,96},{65,33},{96,128},{97,65},{12... | collective-permute-start | bytes 1376264 | tf_op jit(solution)/shard_map/ppermute | solution.py:37
  59.1 21.4 %copy-start.7 = (bf16[80,3584]{1,0:T(8,128)(2,1)}, bf16[80,3584]{1,0:T(8,128)(2,1)S(1)}, u32[]{:S(2)}) copy-start(bf16[80,3584]{1,0:T(8,128)(2,1)S(1)} %collective-permute-done.14.refs_2_) | copy-start | bytes 1720324
  59.2 21.4 %copy-start.2 = (bf16[96,3584]{1,0:T(8,128)(2,1)}, bf16[96,3584]{1,0:T(8,128)(2,1)S(1)}, u32[]{:S(2)}) copy-start(bf16[96,3584]{1,0:T(8,128)(2,1)S(1)} %collective-permute-done.12.refs_0_) | copy-start | bytes 2064388
  59.2 8.7 %collective-permute-start.15 = (bf16[64,3584]{1,0:T(8,128)(2,1)S(1)}, bf16[64,3584]{1,0:T(8,128)(2,1)S(1)}, u32[]{:S(2)}, u32[]{:S(2)}) collective-permute-start(bf16[64,3584]{1,0:T(8,128)(2,1)S(1)} %slice.321), channel_id=1, source_target_pairs={{0,32},{1,225},{32,64},{33,1},{64,96},{65,33},{96,128},{97,65},{12... | collective-permute-start | bytes 1376264 | tf_op jit(solution)/shard_map/ppermute | solution.py:37
  61.5 6.5 %collective-permute-start.16 = (bf16[48,3584]{1,0:T(8,128)(2,1)S(1)}, bf16[48,3584]{1,0:T(8,128)(2,1)S(1)}, u32[]{:S(2)}, u32[]{:S(2)}) collective-permute-start(bf16[48,3584]{1,0:T(8,128)(2,1)S(1)} %pad_maximum_fusion.3), channel_id=1, source_target_pairs={{0,8},{1,25},{8,16},{9,1},{16,24},{17,9},{24,0},{25,17},{2,10},{3,... | collective-permute-start | bytes 1032200 | tf_op jit(solution)/shard_map/ppermute | solution.py:37
  63.3 7.0 %collective-permute-start.18 = (bf16[48,3584]{1,0:T(8,128)(2,1)S(1)}, bf16[48,3584]{1,0:T(8,128)(2,1)}, u32[]{:S(2)}, u32[]{:S(2)}) collective-permute-start(bf16[48,3584]{1,0:T(8,128)(2,1)S(1)} %pad_maximum_fusion.3), channel_id=1, source_target_pairs={{0,1},{1,0},{2,3},{3,2},{4,5},{5,4},{6,7},{7,6},{8,9},{9,8},{10,11... | collective-permute-start | bytes 1032200 | tf_op jit(solution)/shard_map/ppermute | solution.py:23
  63.9 16.8 %collective-permute-start.17 = (bf16[64,3584]{1,0:T(8,128)(2,1)}, bf16[64,3584]{1,0:T(8,128)(2,1)S(1)}, u32[]{:S(2)}, u32[]{:S(2)}) collective-permute-start(bf16[64,3584]{1,0:T(8,128)(2,1)} %collective-permute-done.13.refs_1_), channel_id=1, source_target_pairs={{0,32},{1,225},{32,64},{33,1},{64,96},{65,33},{96,128},{97,65},{12... | collective-permute-start | bytes 1376264 | tf_op jit(solution)/shard_map/ppermute | solution.py:37
  68.0 12.7 %collective-permute-start.20 = (bf16[64,3584]{1,0:T(8,128)(2,1)S(1)}, bf16[64,3584]{1,0:T(8,128)(2,1)S(1)}, u32[]{:S(2)}, u32[]{:S(2)}) collective-permute-start(bf16[64,3584]{1,0:T(8,128)(2,1)S(1)} %collective-permute-done.15.refs_3_), channel_id=1, source_target_pairs={{0,32},{1,225},{32,64},{33,1},{64,96},{65,33},{96,128},{97,65},{12... | collective-permute-start | bytes 1376264 | tf_op jit(solution)/shard_map/ppermute | solution.py:37
  70.3 10.4 %collective-permute-start.19 = (bf16[48,3584]{1,0:T(8,128)(2,1)}, bf16[48,3584]{1,0:T(8,128)(2,1)S(1)}, u32[]{:S(2)}, u32[]{:S(2)}) collective-permute-start(bf16[48,3584]{1,0:T(8,128)(2,1)} %collective-permute-done.18), channel_id=1, source_target_pairs={{0,8},{1,25},{8,16},{9,1},{16,24},{17,9},{24,0},{25,17},{2,10},{3,... | collective-permute-start | bytes 1032200 | tf_op jit(solution)/shard_map/ppermute | solution.py:37
  71.7 9.0 %collective-permute-start.21 = (bf16[48,3584]{1,0:T(8,128)(2,1)S(1)}, bf16[48,3584]{1,0:T(8,128)(2,1)}, u32[]{:S(2)}, u32[]{:S(2)}) collective-permute-start(bf16[48,3584]{1,0:T(8,128)(2,1)S(1)} %collective-permute-done.16.refs_5_), channel_id=1, source_target_pairs={{0,8},{1,25},{8,16},{9,1},{16,24},{17,9},{24,0},{25,17},{2,10},{3,... | collective-permute-start | bytes 1032200 | tf_op jit(solution)/shard_map/ppermute | solution.py:37
  80.6 36.2 %copy-start.13 = (s32[8]{0:T(128)S(1)}, s32[8]{0:T(128)}, u32[]{:S(2)}) copy-start(s32[8]{0:T(128)} %param.9) | copy-start | bytes 100
  80.6 36.2 %copy-start.14 = (s32[8]{0:T(128)S(1)}, s32[8]{0:T(128)}, u32[]{:S(2)}) copy-start(s32[8]{0:T(128)} %param.10) | copy-start | bytes 100
  80.6 45.2 %copy-start.15 = (f32[22]{0:T(128)S(1)}, f32[22]{0:T(128)}, u32[]{:S(2)}) copy-start(f32[22]{0:T(128)} %param.11) | copy-start | bytes 268
  113.5 4.1 %collective-permute-start.23 = (f32[128]{0:T(128)S(1)}, f32[128]{0:T(128)S(1)}, u32[]{:S(2)}, u32[]{:S(2)}) collective-permute-start(f32[128]{0:T(128)S(1)} %pad_maximum_fusion.6), channel_id=1, source_target_pairs={{0,1},{1,0},{2,3},{3,2},{4,5},{5,4},{6,7},{7,6},{8,9},{9,8},{10,11... | collective-permute-start | bytes 1544 | tf_op jit(solution)/shard_map/ppermute | solution.py:23
  119.9 18.8 %all-to-all-start.1 = ((f32[256,1,128]{2,1,0:T(1,128)}), f32[256,1,128]{2,1,0:T(1,128)S(1)}, u32[]{:S(2)}, u32[]{:S(2)}) async-start(f32[256,1,128]{2,1,0:T(1,128)} %broadcast_in_dim.2), calls=%async_computation.1 | async-start | bytes 262144 | tf_op jit(solution)/shard_map/all_to_all | solution.py:386
  (9 other events, 58.1 us)
